TPU v7x, 32 devices: a whole 2x2x4 slice. The times are simulated.
32 devices in a mesh: seq: 16 (over z, x, core), chan: 2 (over y).
Axes of the slice: x: 2, y: 2, z: 4, core: 2. Of those that a mesh axis runs over, the one named last changes fastest.
Arguments:
- features: bfloat16 [4096, 3, 8192], P('seq', None, 'chan'), may hold values from -6 to 6
- residual_in: bfloat16 [4096, 8192], P('seq', 'chan'), may hold values from -6 to 6
- short_filter: float32 [3, 3, 8192], P(None, None, 'chan'), may hold values from -3.5 to 3.5
- decay_rates: float32 [8192, 16], P('chan'), as said below
- residues: float32 [8192, 16], P('chan'), may hold values from -0.12 to 0.12
- skip_gain: float32 [8192], P('chan'), may hold values from -4 to 4
- out_weight: bfloat16 [8192, 8192], P('chan', 'seq'), may hold values from -0.09375 to 0.09375
- final_gain: float32 [8192], P('chan'), may hold values from 0.5 to 1.5
- embedding: bfloat16 [512, 8192], P(None, 'chan')
- next_ids: int32 [4096], P('seq'), may hold values from 65 to 84, as said below
Outputs:
- block_out: bfloat16 [4096, 8192], P('seq', 'chan')
- log_like: float32 [4096], P('seq')
Inputs may be any that keep to these rules, and one draw needn't show every extreme that they name: `next_ids`: each entry is one of 65, 67, 71, 84. `decay_rates`: all between 1.2e-5 and 0.05.
All inputs are finite; a program needn't handle non-finite values.
Results may differ from a plain program's by a relative error of at most 0.015.
Values may be sent and summed in bfloat16 or wider, within the bound.
No kernel may reach another device: no remote copies, remote signals or barrier semaphores. Data moves between devices by JAX's collectives and lax.ppermute only.
A program may use at most 256 MiB of HBM per device.

v0:
```python
import jax
import jax.numpy as jnp
from jax import lax
from jax.sharding import PartitionSpec as P


def shifted(value, axis, steps):
    count = lax.axis_size(axis)
    first, last = (max(0, -steps), min(count, count - steps))
    return lax.ppermute(value, axis, [(source, source + steps) for source in range(first, last)])


def short_conv(padded, taps_weight, count):
    short_len = taps_weight.shape[0]
    output = taps_weight[0] * padded[short_len - 1 : short_len - 1 + count]
    for offset in range(1, short_len):
        output = (
            output
            + taps_weight[offset] * padded[short_len - 1 - offset : short_len - 1 - offset + count]
        )
    return output


def modal_conv(signal, rates_part, residue_part, start_state):
    channels, length = signal.shape
    block_len = min(128, length)
    blocks = length // block_len
    shaped = signal.reshape(channels, blocks, block_len)
    offsets = jnp.arange(block_len, dtype=jnp.float32)
    middle = 0.5 * (block_len - 1)
    falling = residue_part[:, :, None] * jnp.exp(
        -rates_part[:, :, None] * (offsets - middle)[None, None, :]
    )
    rising = jnp.exp(rates_part[:, :, None] * (offsets - middle)[None, None, :])
    full_lag = jnp.einsum("cma,cmb->cab", falling, rising, precision=lax.Precision.HIGHEST)
    positions = jnp.arange(block_len, dtype=jnp.int32)
    causal = positions[:, None] >= positions[None, :]
    toeplitz = jnp.where(causal[None], full_lag, 0.0)
    inside = jnp.einsum("cab,cnb->cna", toeplitz, shaped, precision=lax.Precision.HIGHEST)
    end_decay = jnp.exp(-rates_part[:, :, None] * (block_len - 1 - offsets)[None, None, :])
    states = jnp.einsum("cmb,cnb->cmn", end_decay, shaped, precision=lax.Precision.HIGHEST)
    target = jnp.arange(blocks + 1, dtype=jnp.int32)
    source = jnp.arange(blocks, dtype=jnp.int32)
    gap = (target[:, None] - 1 - source[None, :]).astype(jnp.float32)
    before = target[:, None] > source[None, :]
    span = rates_part * block_len
    weights = jnp.where(
        before[None, None],
        jnp.exp(-span[:, :, None, None] * jnp.maximum(gap, 0.0)[None, None]),
        0.0,
    )
    from_start = (
        jnp.exp(-span[:, :, None] * target.astype(jnp.float32)[None, None, :])
        * start_state[:, :, None]
    )
    entering = (
        jnp.einsum("cmnk,cmk->cmn", weights, states, precision=lax.Precision.HIGHEST) + from_start
    )
    previous = entering[:, :, :blocks]
    last_state = entering[:, :, blocks]
    mode_lift = residue_part[:, :, None] * jnp.exp(
        -rates_part[:, :, None] * (offsets + 1.0)[None, None, :]
    )
    carried = jnp.einsum("cma,cmn->cna", mode_lift, previous, precision=lax.Precision.HIGHEST)
    return ((inside + carried).reshape(channels, length), last_state)


def modal_grouped(signal, rates_part, residue_part, start_state):
    channels = signal.shape[0]
    group_size = min(128, channels)
    groups = channels // group_size

    def one_group(pieces):
        return modal_conv(pieces[0], pieces[1], pieces[2], pieces[3])

    outputs, states = lax.map(
        one_group,
        (
            signal.reshape(groups, group_size, -1),
            rates_part.reshape(groups, group_size, -1),
            residue_part.reshape(groups, group_size, -1),
            start_state.reshape(groups, group_size, -1),
        ),
    )
    return (outputs.reshape(channels, -1), states.reshape(channels, -1))


def local(
    features,
    residual_in,
    short_filter,
    decay_rates,
    residues,
    skip_gain,
    out_weight,
    final_gain,
    embedding,
    next_ids,
):
    tok_rows = features.shape[0]
    short_len = short_filter.shape[0]
    rim_rows = shifted(features[tok_rows - (short_len - 1) :], "seq", 1)
    padded = jnp.concatenate([rim_rows, features], axis=0).astype(jnp.float32)
    streams = short_conv(padded, short_filter, tok_rows)
    queries = streams[:, 0, :]
    mixed_kv = (streams[:, 1, :] * streams[:, 2, :]).astype(jnp.bfloat16)
    by_channel = lax.all_to_all(mixed_kv.T, "seq", split_axis=0, concat_axis=1, tiled=True)
    chan_count = by_channel.shape[0]
    chan_start = lax.axis_index("seq") * chan_count
    rates_part = lax.dynamic_slice_in_dim(decay_rates, chan_start, chan_count, 0)
    residue_part = lax.dynamic_slice_in_dim(residues, chan_start, chan_count, 0)
    convolved, unused_state = modal_grouped(
        by_channel.astype(jnp.float32),
        rates_part,
        residue_part,
        jnp.zeros((chan_count, decay_rates.shape[1]), jnp.float32),
    )
    returned = lax.all_to_all(
        convolved.astype(jnp.bfloat16), "seq", split_axis=1, concat_axis=0, tiled=True
    )
    filtered = returned.T
    gated = (
        queries * (filtered.astype(jnp.float32) + skip_gain * mixed_kv.astype(jnp.float32))
    ).astype(jnp.bfloat16)
    partial_out = jnp.dot(
        gated,
        lax.all_gather(out_weight, "seq", axis=1, tiled=True),
        preferred_element_type=jnp.float32,
    )
    summed = lax.psum_scatter(partial_out, "chan", scatter_dimension=1, tiled=True)
    block_out = (residual_in.astype(jnp.float32) + summed).astype(jnp.bfloat16)
    block_f = block_out.astype(jnp.float32)
    width_all = block_f.shape[1] * lax.axis_size("chan")
    scaled = (block_f * final_gain).astype(jnp.bfloat16)
    partial_logits = lax.dot_general(
        scaled, embedding, (((1,), (1,)), ((), ())), preferred_element_type=jnp.float32
    )
    sum_squares, raw_logits = (
        lax.psum(jnp.sum(block_f * block_f, axis=1).astype(jnp.bfloat16), "chan").astype(
            jnp.float32
        ),
        lax.psum(partial_logits.astype(jnp.bfloat16), "chan").astype(jnp.float32),
    )
    inv_rms = lax.rsqrt(sum_squares / width_all + 1e-06)
    logits = raw_logits * inv_rms[:, None]
    vocab_ids = jnp.arange(logits.shape[1], dtype=jnp.int32)
    one_hot = next_ids[:, None] == vocab_ids[None, :]
    chosen = jnp.sum(jnp.where(one_hot, logits, 0.0), axis=1)
    log_like = chosen - jax.nn.logsumexp(logits, axis=1)
    return (block_out, log_like)


def solution(mesh):
    return jax.shard_map(
        local,
        mesh=mesh,
        in_specs=(
            P("seq", None, "chan"),
            P("seq", "chan"),
            P(None, None, "chan"),
            P("chan", None),
            P("chan", None),
            P("chan"),
            P("chan", "seq"),
            P("chan"),
            P(None, "chan"),
            P("seq"),
        ),
        out_specs=(P("seq", "chan"), P("seq")),
        check_vma=False,
    )
```

profile of v0, /device:TPU:0, one launch (start us, length us, event | category | flops | bytes accessed | tf_op | source)
XLA Modules:
  0.0 600.2 jit_solution(1614094154330800188)
XLA Ops:
  8.9 2.4 collective-permute-start
  12.1 4.7 maximum_convert_fusion
  16.9 7.9 %fusion.37 = f32[256,3,4096]{2,0,1:T(8,128)} fusion(f32[258,3,4096]{2,0,1:T(8,128)S(1)} %maximum_convert_fusion, f32[3,4096]{1,0:T(4,128)S(1)} %get-tuple-element.86, f32[3,4096]{1,0:T(4,128)S(1)} %get-tuple-element.87, f32[3,4096]{1,0:T(4,128)S(1)} %get-tuple-element.85), kind=kLoop, calls=%fused_computation.51 | loop fusion | flops 15728640 | bytes 50479104 | tf_op jit(solution)/shard_map/add | solution.py:18
  24.7 4.0 fusion.63
  28.7 2.5 copy.27
  31.2 8.4 %all-to-all-start = ((bf16[16,256,256]{2,1,0:T(8,128)(2,1)}), bf16[16,256,256]{2,1,0:T(8,128)(2,1)S(1)}, u32[]{:S(2)}, u32[]{:S(2)}) async-start(bf16[16,256,256]{2,1,0:T(8,128)(2,1)} %bitcast.83), calls=%async_computation | async-start | bytes 4194304 | tf_op jit(solution)/shard_map/all_to_all | solution.py:107
  41.3 71.9 %all-to-all-done = bf16[16,256,256]{2,1,0:T(8,128)(2,1)S(1)} async-done(((bf16[16,256,256]{2,1,0:T(8,128)(2,1)}), bf16[16,256,256]{2,1,0:T(8,128)(2,1)S(1)}, u32[]{:S(2)}, u32[]{:S(2)}) %all-to-all-start) | async-done | bytes 2097184 | tf_op jit(solution)/shard_map/all_to_all | solution.py:107
  113.6 4.3 copy.28
  118.0 5.0 reshape.148
  123.0 218.1 %while.12 = (s32[]{:T(128)}, bf16[2,128,4096]{2,1,0:T(8,128)(2,1)}, f32[2,128,4096]{2,1,0:T(8,128)}, f32[2,128,16]{2,1,0:T(8,128)}, f32[2,128,16]{2,1,0:T(8,128)S(1)}, /*index=5*/s32[]{:T(128)}) while((s32[]{:T(128)}, bf16[2,128,4096]{2,1,0:T(8,128)(2,1)}, f32[2,128,4096]{2,1,0:T(8,128)}, f32[2,128,16]{2,1,0:T(8,128)}, ...), condition=%wide.region_1.2_spmd, body=%wide.region_0.1_spmd.sunk | while | flops 1444506112 | bytes 74717624 | solution.py:76
  125.4 3.4 fusion.90
  129.0 5.7 exponential_select_fusion.2
  134.7 27.0 %copy.42 = f32[128,16,33,32]{2,3,1,0:T(8,128)} copy(f32[128,16,33,32]{0,3,2,1:T(8,128)} %exponential_select_fusion.2) | data formatting | bytes 17301504 | tf_op jit(solution)/shard_map/while/body/eval_jaxpr/jit(_where)/select_n | solution.py:47
  161.7 33.1 %fusion.91 = f32[128,16,1,33]{3,2,1,0:T(1,128)S(1)} fusion(f32[128,16,33,32]{2,3,1,0:T(8,128)} %copy.42, f32[128,16,32,1]{2,3,1,0:T(1,128)S(1)} %bitcast.80), kind=kOutput, calls=%fused_computation.88.clone.1 | convolution fusion | flops 25952256 | bytes 9183232 | tf_op jit(solution)/shard_map/while/body/eval_jaxpr/cmnk,cmk->cmn/dot_general | solution.py:57
  194.9 4.4 fusion.92
  199.3 14.3 %fusion.93 = f32[128,128,128]{2,1,0:T(8,128)S(1)} fusion(f32[128,16]{1,0:T(8,128)S(1)} %get-tuple-element.123, f32[128]{0:T(128)S(1)} %iota_add_fusion.8, f32[128,16]{1,0:T(8,128)S(1)} %get-tuple-element.124, f32[128,16]{1,0:T(8,128)S(1)} %dynamic-slice_bitcast_fusion.7), kind=kOutput, calls=%fused_computation.18.clone.1 | convolution fusion | flops 403439616 | bytes 8413696 | tf_op jit(solution)/shard_map/while/body/eval_jaxpr/cma,cmb->cab/dot_general | solution.py:35
  213.6 13.3 %fusion.94 = bf16[128,32,128]{2,1,0:T(8,128)(2,1)S(1)} fusion(f32[128,32,128]{2,1,0:T(8,128)S(1)} %fusion.92, f32[128,32,128]{2,1,0:T(8,128)S(1)} %bitcast.79, f32[128,128,128]{2,1,0:T(8,128)S(1)} %fusion.93, pred[128,128]{1,0:T(8,128)(4,1)S(1)} %iota_compare_fusion.6), kind=kOutput, calls=%fused_computation.6.clone.1 | convolution fusion | flops 808452096 | bytes 13647872 | tf_op jit(solution)/shard_map/while/body/eval_jaxpr/cab,cnb->cna/dot_general | solution.py:39
  231.1 3.4 fusion.90
  234.7 5.5 exponential_select_fusion.2
  240.2 27.0 %copy.42 = f32[128,16,33,32]{2,3,1,0:T(8,128)} copy(f32[128,16,33,32]{0,3,2,1:T(8,128)} %exponential_select_fusion.2) | data formatting | bytes 17301504 | tf_op jit(solution)/shard_map/while/body/eval_jaxpr/jit(_where)/select_n | solution.py:47
  267.2 33.6 %fusion.91 = f32[128,16,1,33]{3,2,1,0:T(1,128)S(1)} fusion(f32[128,16,33,32]{2,3,1,0:T(8,128)} %copy.42, f32[128,16,32,1]{2,3,1,0:T(1,128)S(1)} %bitcast.80), kind=kOutput, calls=%fused_computation.88.clone.1 | convolution fusion | flops 25952256 | bytes 9183232 | tf_op jit(solution)/shard_map/while/body/eval_jaxpr/cmnk,cmk->cmn/dot_general | solution.py:57
  300.9 4.4 fusion.92
  305.3 14.5 %fusion.93 = f32[128,128,128]{2,1,0:T(8,128)S(1)} fusion(f32[128,16]{1,0:T(8,128)S(1)} %get-tuple-element.123, f32[128]{0:T(128)S(1)} %iota_add_fusion.8, f32[128,16]{1,0:T(8,128)S(1)} %get-tuple-element.124, f32[128,16]{1,0:T(8,128)S(1)} %dynamic-slice_bitcast_fusion.7), kind=kOutput, calls=%fused_computation.18.clone.1 | convolution fusion | flops 403439616 | bytes 8413696 | tf_op jit(solution)/shard_map/while/body/eval_jaxpr/cma,cmb->cab/dot_general | solution.py:35
  319.8 13.2 %fusion.94 = bf16[128,32,128]{2,1,0:T(8,128)(2,1)S(1)} fusion(f32[128,32,128]{2,1,0:T(8,128)S(1)} %fusion.92, f32[128,32,128]{2,1,0:T(8,128)S(1)} %bitcast.79, f32[128,128,128]{2,1,0:T(8,128)S(1)} %fusion.93, pred[128,128]{1,0:T(8,128)(4,1)S(1)} %iota_compare_fusion.6), kind=kOutput, calls=%fused_computation.6.clone.1 | convolution fusion | flops 808452096 | bytes 13647872 | tf_op jit(solution)/shard_map/while/body/eval_jaxpr/cab,cnb->cna/dot_general | solution.py:39
  344.0 70.5 %all_to_all.23 = bf16[256,16,256]{2,0,1:T(8,128)(2,1)S(1)} all-to-all(bf16[256,16,256]{2,0,1:T(8,128)(2,1)S(1)} %copy.31), channel_id=1, replica_groups=mesh['seq'=16,'chan'=2] {'seq'}, dimensions={1} | all-to-all | bytes 4194304 | tf_op jit(solution)/shard_map/all_to_all | solution.py:118
  414.5 2.4 convert_element_type.114
  417.0 5.6 copy.32
  422.6 33.7 %fusion.44 = f32[256,8192]{1,0:T(8,128)} fusion(bf16[4096,8192]{1,0:T(8,128)(2,1)} %all-gather.2.cloned.1.call-done, f32[256,3,4096]{2,0,1:T(8,128)} %fusion.37, f32[4096,256]{0,1:T(8,128)} %copy.32, f32[4096]{0:T(1024)S(1)} %copy-done.6), kind=kOutput, calls=%fused_computation.68 | convolution fusion | flops 17187209216 | bytes 92291072 | tf_op jit(solution)/shard_map/dot_general | solution.py:125
  456.3 104.2 %reduce-scatter.2.cloned.1.call-done = f32[256,4096]{1,0:T(8,128)} async-done(((f32[256,8192]{1,0:T(8,128)}), f32[256,4096]{1,0:T(8,128)}) %reduce-scatter.2.cloned.1.call-update) | async-done | bytes 4194320 | tf_op jit(solution)/shard_map/reduce_scatter | solution.py:130
  560.5 3.2 fusion.40
  567.0 4.9 psum.15
  572.0 18.4 %all-reduce.2.cloned.1.call-done = bf16[256,512]{1,0:T(8,128)(2,1)} async-done(((bf16[256,512]{1,0:T(8,128)(2,1)}), bf16[256,512]{1,0:T(8,128)(2,1)}) %all-reduce.2.cloned.1.call-update) | async-done | bytes 262160 | tf_op jit(solution)/shard_map/psum | solution.py:142
  (73 shorter events, 22.0 us)
Async XLA Ops:
  7.2 4.1 copy-start.3
  7.2 415.4 %all-gather.2.cloned.1.call-start = ((), (), s32[]{:S(2)}) async-start(), calls=%async_computation.3 | async-start | bytes 71303168 | tf_op jit(solution)/shard_map/all_gather | solution.py:127
  8.9 3.2 collective-permute-start
  31.2 82.0 %all-to-all-start = ((bf16[16,256,256]{2,1,0:T(8,128)(2,1)}), bf16[16,256,256]{2,1,0:T(8,128)(2,1)S(1)}, u32[]{:S(2)}, u32[]{:S(2)}) async-start(bf16[16,256,256]{2,1,0:T(8,128)(2,1)} %bitcast.83), calls=%async_computation | async-start | bytes 4194304 | tf_op jit(solution)/shard_map/all_to_all | solution.py:107
  39.6 520.9 %reduce-scatter.2.cloned.1.call-start = ((), (), s32[]{:S(2)}) async-start(), calls=%async_computation.4 | async-start | bytes 12582912 | tf_op jit(solution)/shard_map/reduce_scatter | solution.py:130
  161.7 33.1 %copy-start.2 = (f32[2,128,16]{2,1,0:T(8,128)S(1)}, f32[2,128,16]{2,1,0:T(8,128)}, u32[]{:S(2)}) copy-start(f32[2,128,16]{2,1,0:T(8,128)} %get-tuple-element.140) | copy-start | bytes 49156 | tf_op jit(solution)/shard_map/while
  267.2 33.6 %copy-start.2 = (f32[2,128,16]{2,1,0:T(8,128)S(1)}, f32[2,128,16]{2,1,0:T(8,128)}, u32[]{:S(2)}) copy-start(f32[2,128,16]{2,1,0:T(8,128)} %get-tuple-element.140) | copy-start | bytes 49156 | tf_op jit(solution)/shard_map/while
  417.0 5.6 copy-start.6
  456.2 104.2 %copy-start = (bf16[256,4096]{1,0:T(8,128)(2,1)S(1)}, bf16[256,4096]{1,0:T(8,128)(2,1)}, u32[]{:S(2)}) copy-start(bf16[256,4096]{1,0:T(8,128)(2,1)} %param.13) | copy-start | bytes 6291460
  456.3 108.7 %copy-start.7 = (f32[4096]{0:T(1024)S(1)}, f32[4096]{0:T(1024)}, u32[]{:S(2)}) copy-start(f32[4096]{0:T(1024)} %param.19) | copy-start | bytes 49156
  456.3 134.1 %all-reduce.2.cloned.1.call-start = ((), (), s32[]{:S(2)}) async-start(), calls=%async_computation.5 | async-start | bytes 524288 | tf_op jit(solution)/shard_map/psum | solution.py:142
  560.5 4.5 copy-start.5
  563.7 1.3 copy-start.1
  565.0 26.5 %copy-start.4 = (s32[256]{0:T(256)S(1)}, s32[256]{0:T(256)}, u32[]{:S(2)}) copy-start(s32[256]{0:T(256)} %param.21) | copy-start | bytes 3076
Sparse Core Ops, SparseCore 0:
  9.6 389.3 all-gather.1
  456.4 104.0 reduce-scatter.1
  567.1 23.1 all-reduce.1
where the time goes:
time: 607 us; the launch traced here: 600 us
  waiting for transfers between devices  196 us (32%)
  matrix products  173 us (29%)
  local copies, waits for them, and re-layouts  86 us (14%)
  blocking collectives  75.5 us (12%)
  other arithmetic  37.3 us (6%)
  between operations  14.2 us (2%)
  starting transfers between devices  10.9 us (2%)
  loops' own time  7.18 us (1%)
    reduce_scatter x1, waiting for transfers between devices, local(): lax.psum_scatter(partial_out, 'chan', scatter_dimension=1, tiled=True)  104 us
    all_to_all x1, waiting for transfers between devices, local(): lax.all_to_all(mixed_kv.T, 'seq', split_axis=0, concat_axis=1, tiled=True)  71.9 us
    all_to_all x1, blocking collectives, local(): lax.all_to_all(convolved.astype(jnp.bfloat16), 'seq', split_axis=1, conca...  70.5 us
    dot_general x2, matrix products, modal_conv(): jnp.einsum('cmnk,cmk->cmn', weights, states, precision=lax.Precision.HIGH...  66.7 us
    select_n x2, local copies, waits for them, and re-layouts, modal_conv(): jnp.where(before[None, None], jnp.exp(-span[:, :, None, None] * jnp.maxim...  54 us
    dot_general x1, matrix products, local(): jnp.dot(gated, lax.all_gather(out_weight, 'seq', axis=1, tiled=True), pre...  33.7 us
    dot_general x2, matrix products, modal_conv(): jnp.einsum('cma,cmb->cab', falling, rising, precision=lax.Precision.HIGHEST)  28.7 us
    dot_general x2, matrix products, modal_conv(): jnp.einsum('cab,cnb->cna', toeplitz, shaped, precision=lax.Precision.HIGH...  26.5 us
  transfers between devices with their start and end apart: 5, of which 4 were waited for; matrix products, arithmetic and copies ran while one was open for 42% of the time, Pallas kernels for 0%

commit v1 on v0

v1 whole, which is shorter than its diff:
```python
import functools
import itertools

import jax
import jax.numpy as jnp
from jax import lax
from jax.experimental import pallas as pl
from jax.experimental.pallas import tpu as pltpu
from jax.sharding import PartitionSpec as P

F32 = jnp.float32
BF16 = jnp.bfloat16
LANES = 128
SUBLANES = 8
GROUP = LANES * SUBLANES


def xor_permute(value, axis, mask):
    count = lax.axis_size(axis)
    return lax.ppermute(value, axis, [(source, source ^ mask) for source in range(count)])


def shifted(value, axis, steps):
    count = lax.axis_size(axis)
    first, last = (max(0, -steps), min(count, count - steps))
    return lax.ppermute(value, axis, [(source, source + steps) for source in range(first, last)])


def fill_stream(scratch, halo, block):
    scratch[:SUBLANES, :] = halo
    scratch[SUBLANES:, :] = block.astype(F32)


def short_stream(scratch, taps_ref, stream, lanes, rows):
    taps = taps_ref.shape[0] // 3
    total = taps_ref[stream : stream + 1, lanes] * scratch[SUBLANES : SUBLANES + rows, lanes]
    for offset in range(1, taps):
        row = offset * 3 + stream
        start = SUBLANES - offset
        total = total + taps_ref[row : row + 1, lanes] * scratch[start : start + rows, lanes]
    return total


def lane_blocks():
    return [(part, slice(part * LANES, (part + 1) * LANES)) for part in range(SUBLANES)]


def states_kernel(
    keys_ref, values_ref, halo_ref, taps_ref, rates_ref, mixed_ref, end_ref, keys_f, values_f, rows_f
):
    rows = mixed_ref.shape[0]
    modes = rates_ref.shape[0]
    fill_stream(keys_f, halo_ref[1], keys_ref[0])
    fill_stream(values_f, halo_ref[2], values_ref[0])
    for part, lanes in lane_blocks():
        mixed = (
            short_stream(keys_f, taps_ref, 1, lanes, rows)
            * short_stream(values_f, taps_ref, 2, lanes, rows)
        ).astype(BF16)
        mixed_ref[:, lanes] = mixed
        rows_f[:, part * SUBLANES : (part + 1) * SUBLANES, :] = mixed.astype(F32).reshape(
            rows // SUBLANES, SUBLANES, LANES
        )
    decay = [jnp.exp(-rates_ref[mode]) for mode in range(modes)]

    def eight(block, states):
        for step in range(SUBLANES):
            entry = rows_f[block, pl.ds(step, SUBLANES, stride=SUBLANES), :]
            states = tuple(d * s + entry for d, s in zip(decay, states))
        return states

    zeros = tuple(jnp.zeros((SUBLANES, LANES), F32) for _ in range(modes))
    states = lax.fori_loop(0, rows // SUBLANES, eight, zeros)
    for mode in range(modes):
        end_ref[mode] = states[mode]


def gated_kernel(
    queries_ref,
    halo_ref,
    taps_ref,
    mixed_ref,
    skip_ref,
    rates_ref,
    residues_ref,
    enter_ref,
    gated_ref,
    queries_f,
    rows_f,
    long_f,
):
    rows = mixed_ref.shape[0]
    modes = rates_ref.shape[0]
    fill_stream(queries_f, halo_ref[0], queries_ref[0])
    for part, lanes in lane_blocks():
        rows_f[:, part * SUBLANES : (part + 1) * SUBLANES, :] = (
            mixed_ref[:, lanes].astype(F32).reshape(rows // SUBLANES, SUBLANES, LANES)
        )
    decay = [jnp.exp(-rates_ref[mode]) for mode in range(modes)]
    weight = [residues_ref[mode] for mode in range(modes)]

    def eight(block, states):
        for step in range(SUBLANES):
            entry = rows_f[block, pl.ds(step, SUBLANES, stride=SUBLANES), :]
            states = tuple(d * s + entry for d, s in zip(decay, states))
            terms = [w * s for w, s in zip(weight, states)]
            while len(terms) > 1:
                terms = [sum(terms[at : at + 2][1:], terms[at]) for at in range(0, len(terms), 2)]
            long_f[block, pl.ds(step, SUBLANES, stride=SUBLANES), :] = terms[0]
        return states

    lax.fori_loop(0, rows // SUBLANES, eight, tuple(enter_ref[mode] for mode in range(modes)))
    for part, lanes in lane_blocks():
        filtered = long_f[:, part * SUBLANES : (part + 1) * SUBLANES, :].reshape(rows, LANES)
        filtered = filtered.astype(BF16).astype(F32)
        direct = skip_ref[:, lanes] * mixed_ref[:, lanes].astype(F32)
        queries = short_stream(queries_f, taps_ref, 0, lanes, rows)
        gated_ref[:, lanes] = (queries * (filtered + direct)).astype(BF16)


def vmem_params(mib):
    return pltpu.CompilerParams(
        dimension_semantics=("arbitrary",), vmem_limit_bytes=mib * 1024 * 1024
    )


def mixed_and_states(streams, halo, taps, rates):
    rows, width = streams.shape[1:]
    modes = rates.shape[0]
    stream = lambda which: pl.BlockSpec((1, rows, GROUP), lambda g: (which, 0, g))
    modal = pl.BlockSpec((modes, SUBLANES, LANES), lambda g: (0, g, 0))
    return pl.pallas_call(
        states_kernel,
        grid=(width // GROUP,),
        in_specs=[
            stream(1),
            stream(2),
            pl.BlockSpec((3, SUBLANES, GROUP), lambda g: (0, 0, g)),
            pl.BlockSpec((taps.shape[0], GROUP), lambda g: (0, g)),
            modal,
        ],
        out_specs=[pl.BlockSpec((rows, GROUP), lambda g: (0, g)), modal],
        out_shape=[
            jax.ShapeDtypeStruct((rows, width), BF16),
            jax.ShapeDtypeStruct(rates.shape, F32),
        ],
        scratch_shapes=[
            pltpu.VMEM((rows + SUBLANES, GROUP), F32),
            pltpu.VMEM((rows + SUBLANES, GROUP), F32),
            pltpu.VMEM((rows // SUBLANES, SUBLANES * SUBLANES, LANES), F32),
        ],
        compiler_params=vmem_params(32),
        cost_estimate=pl.CostEstimate(flops=rows * width, bytes_accessed=rows, transcendentals=0),
        name="mixed_and_states",
    )(streams, streams, halo, taps, rates)


def gated_rows(streams, halo, taps, mixed, skip, rates, residues, entering, base, steps):
    rows, width = mixed.shape
    modes = rates.shape[0]
    modal = pl.BlockSpec((modes, SUBLANES, LANES), lambda g: (0, base + g, 0))
    return pl.pallas_call(
        gated_kernel,
        grid=(steps,),
        in_specs=[
            pl.BlockSpec((1, rows, GROUP), lambda g: (0, 0, base + g)),
            pl.BlockSpec((3, SUBLANES, GROUP), lambda g: (0, 0, base + g)),
            pl.BlockSpec((taps.shape[0], GROUP), lambda g: (0, base + g)),
            pl.BlockSpec((rows, GROUP), lambda g: (0, base + g)),
            pl.BlockSpec((1, GROUP), lambda g: (0, base + g)),
            modal,
            modal,
            modal,
        ],
        out_specs=pl.BlockSpec((rows, GROUP), lambda g: (0, g)),
        out_shape=jax.ShapeDtypeStruct((rows, steps * GROUP), BF16),
        scratch_shapes=[
            pltpu.VMEM((rows + SUBLANES, GROUP), F32),
            pltpu.VMEM((rows // SUBLANES, SUBLANES * SUBLANES, LANES), F32),
            pltpu.VMEM((rows // SUBLANES, SUBLANES * SUBLANES, LANES), F32),
        ],
        compiler_params=vmem_params(32),
        cost_estimate=pl.CostEstimate(flops=rows * width, bytes_accessed=rows, transcendentals=0),
        name="gated_rows",
    )(streams, halo, taps, mixed, skip, rates, residues, entering)


def entering_states(end, rates, rows, merges, before_last=()):
    place = lax.axis_index("seq")
    total, entering = end, jnp.zeros_like(end)
    held = []
    for bits in merges:
        span, count = 1 << bits[0], 1 << len(bits)
        last = bits == merges[-1]
        if last and before_last:
            total, *held = tied(total, *before_last)
        extra = span >> 1 if last and count == 2 else 0
        others = [
            (mask, xor_permute(total, "seq", (mask * span) | extra)) for mask in range(1, count)
        ]
        own = (place // span) % count
        inside = (place % span) * rows
        merged = jnp.zeros_like(total)
        for mask, value in [(0, total), *others]:
            run = own ^ mask
            gap = jnp.maximum(own - 1 - run, 0) * (span * rows) + inside
            ahead = jnp.exp(-rates * gap.astype(F32)) * value
            entering = entering + jnp.where(run < own, ahead, 0.0)
            gap = (count - 1 - run) * (span * rows)
            merged = merged + jnp.exp(-rates * gap.astype(F32)) * value
        total = merged
    return entering, held


def output_kernel(
    order_ref, added_ref, residual_ref, gain_ref, table_ref, block_ref, packed_ref, logits, squares
):
    at = pl.program_id(0)

    @pl.when(at == 0)
    def _():
        logits[...] = jnp.zeros_like(logits)
        squares[...] = jnp.zeros_like(squares)

    block = (residual_ref[...].astype(F32) + added_ref[0].astype(F32)).astype(BF16)
    block_ref[...] = block
    block_f = block.astype(F32)
    scaled = (block_f * gain_ref[...]).astype(BF16)
    logits[...] += lax.dot_general(
        table_ref[...], scaled, (((1,), (1,)), ((), ())), preferred_element_type=F32
    )
    squared = block_f * block_f
    width = squared.shape[1]
    for start in range(0, width, LANES):
        squares[...] += squared[:, start : start + LANES]

    @pl.when(at == pl.num_programs(0) - 1)
    def _():
        vocab = logits.shape[0]
        summed = jnp.sum(squares[...].T, axis=0, keepdims=True)
        high = summed.astype(BF16).astype(F32)
        row = lax.broadcasted_iota(jnp.int32, (16, summed.shape[1]), 0)
        extra = jnp.where(row == 0, high, jnp.where(row == 1, summed - high, 0.0))
        packed_ref[:vocab, :] = logits[...].astype(BF16)
        packed_ref[vocab:, :] = extra.astype(BF16)


def output_rows(order, added, residual_in, gain, table):
    parts, rows, width = added.shape
    vocab = table.shape[0]
    return pl.pallas_call(
        output_kernel,
        grid_spec=pltpu.PrefetchScalarGridSpec(
            num_scalar_prefetch=1,
            grid=(parts,),
            in_specs=[
                pl.BlockSpec((1, rows, width), lambda p, order: (order[p], 0, 0)),
                pl.BlockSpec((rows, width), lambda p, order: (0, p)),
                pl.BlockSpec((1, width), lambda p, order: (0, p)),
                pl.BlockSpec((vocab, width), lambda p, order: (0, p)),
            ],
            out_specs=[
                pl.BlockSpec((rows, width), lambda p, order: (0, p)),
                pl.BlockSpec((vocab + 16, rows), lambda p, order: (0, 0)),
            ],
            scratch_shapes=[
                pltpu.VMEM((vocab, rows), F32),
                pltpu.VMEM((rows, LANES), F32),
            ],
        ),
        out_shape=[
            jax.ShapeDtypeStruct(residual_in.shape, BF16),
            jax.ShapeDtypeStruct((vocab + 16, rows), BF16),
        ],
        compiler_params=vmem_params(32),
        cost_estimate=pl.CostEstimate(
            flops=2 * rows * parts * width * vocab,
            bytes_accessed=2 * parts * width * (3 * rows + vocab),
            transcendentals=0,
        ),
        name="output_rows",
    )(order, added, residual_in, gain, table)


def like_kernel(width, first_ref, second_ref, ids_ref, like_ref):
    rows = ids_ref.shape[1]
    vocab = first_ref.shape[0] - 16
    total = first_ref[...].astype(F32) + second_ref[...].astype(F32)
    squares = total[vocab : vocab + 1, :] + total[vocab + 1 : vocab + 2, :]
    inv_rms = lax.rsqrt(squares / width + 1e-06)
    logits = total[:vocab, :] * inv_rms
    largest = jnp.max(logits, axis=0, keepdims=True)
    summed = jnp.sum(jnp.exp(logits - largest), axis=0, keepdims=True)
    vocab_ids = lax.broadcasted_iota(jnp.int32, (vocab, rows), 0)
    chosen = jnp.sum(jnp.where(vocab_ids == ids_ref[...], logits, 0.0), axis=0, keepdims=True)
    like_ref[...] = chosen - (largest + jnp.log(summed))


def log_likelihood(first, second, next_ids, width):
    rows = next_ids.shape[0]
    like = pl.pallas_call(
        functools.partial(like_kernel, width),
        out_shape=jax.ShapeDtypeStruct((1, rows), F32),
        compiler_params=pltpu.CompilerParams(vmem_limit_bytes=16 * 1024 * 1024),
        name="log_likelihood",
    )(first, second, next_ids[None, :])
    return like[0]


def summed_over_chan(value):
    count = lax.axis_size("chan")
    total, span = value, 1
    while span < count // 2:
        total = (total.astype(F32) + xor_permute(total, "chan", span).astype(F32)).astype(BF16)
        span *= 2
    return total, xor_permute(total, "chan", span)


def placed_pairs(count, chans, per_chan, same, seq_mask, chan_mask):
    pairs = []
    for place, chan in itertools.product(range(count), range(chans)):
        if (place // per_chan == chan) == same:
            target = (place ^ seq_mask) * chans + (chan ^ chan_mask)
            pairs.append((place * chans + chan, target))
    return pairs


def tied(*values):
    return lax.optimization_barrier(values)


def far_pieces(out_weight, cuts):
    return [
        lax.slice_in_dim(out_weight, first, last, axis=1)
        for first, last in itertools.pairwise(cuts)
    ]


def joined(*rows):
    return tied(jnp.concatenate([jnp.concatenate(parts, axis=1) for parts in rows], axis=0))[0]


def product(rows, *weights):
    outs = [jnp.dot(rows, weight, preferred_element_type=F32).astype(BF16) for weight in weights]
    return outs[0] if len(outs) == 1 else jnp.concatenate(outs, axis=1)


def projected_fast(gated, out_weight, core_weight, far):
    count, chans = lax.axis_size("seq"), lax.axis_size("chan")
    per_chan = count // chans
    rows, block = gated[0].shape[0], out_weight.shape[1]
    core, side, low = 1, 2, 4

    below = [xor_permute(part, "seq", low) for part in gated]
    beside = [xor_permute(gated[0], "seq", side)]
    later, far[1] = tied(gated[1], far[1])
    beside.append(xor_permute(later, "seq", side))
    below[0], beside[1] = tied(below[0], beside[1])
    across = [xor_permute(below[0], "seq", side)]
    beside[0], far[2], far[0] = tied(beside[0], far[2], far[0])
    first = joined(gated, beside)
    near_first = product(first, out_weight, core_weight)
    below[1], across[0], waiting = tied(below[1], across[0], far[3])
    far[3] = xor_permute(waiting, "seq", per_chan)
    across.append(xor_permute(below[1], "seq", side))
    second = joined(below, across)

    def reduced(partial, masks, same, after=None):
        pairs = placed_pairs(count, chans, per_chan, not same, 0, 1)
        other = lax.ppermute(partial, ("seq", "chan"), pairs)
        if after is not None:
            other, _ = tied(other, after)
        total = (partial.astype(F32) + other.astype(F32)).astype(BF16)
        back = []
        for at, mask in enumerate(masks):
            mine = total[at * rows : (at + 1) * rows]
            if mask:
                pairs = placed_pairs(count, chans, per_chan, same, mask, 0)
                mine = lax.ppermute(mine, ("seq", "chan"), pairs)
            back.append(mine)
        return back

    far_core = [xor_permute(piece, "seq", core) for piece in far[:-1]]
    near_back = reduced(near_first, (0, side), True)
    early = jnp.concatenate(far[:-1] + far_core, axis=1)
    early_first = product(first, early)
    near_second = product(second, out_weight, core_weight)
    early_second = product(second, early)
    last, *_ = tied(far[-1], early_second, near_second)
    last_core = xor_permute(last, "seq", core)
    last = jnp.concatenate([last, last_core], axis=1)
    last_all = jnp.concatenate([product(first, last), product(second, last)], axis=0)
    near_back += reduced(near_second, (low, low | side), True, last_all)
    early_back = reduced(early_first, (0, side), False)
    early_back += reduced(early_second, (low, low | side), False, last_all)
    last_back = reduced(last_all, (0, side, low, low | side), False)
    here = lax.axis_index("seq") // per_chan == lax.axis_index("chan")
    cut = block - last_core.shape[1]
    blocks = {}
    for at, mask in enumerate((0, side, low, low | side)):
        for half in range(2):
            near_block = near_back[at][:, half * block : (half + 1) * block]
            late_block = jnp.concatenate(
                [
                    early_back[at][:, half * cut : (half + 1) * cut],
                    last_back[at][:, half * (block - cut) : (half + 1) * (block - cut)],
                ],
                axis=1,
            )
            blocks[mask | (half * core)] = jnp.where(here, near_block, late_block)
    added = jnp.stack([blocks[mask] for mask in range(per_chan)])
    order = jnp.arange(per_chan, dtype=jnp.int32) ^ (lax.axis_index("seq") % per_chan)
    return added, order


def projected_plain(gated, out_weight):
    count, chans = lax.axis_size("seq"), lax.axis_size("chan")
    per_chan = count // chans
    partial = jnp.dot(
        gated,
        lax.all_gather(out_weight, "seq", axis=1, tiled=True),
        preferred_element_type=F32,
    )
    summed = lax.psum_scatter(partial, "chan", scatter_dimension=1, tiled=True)
    rows = gated.shape[0]
    added = summed.reshape(rows, per_chan, -1).transpose(1, 0, 2)
    return added, jnp.arange(per_chan, dtype=jnp.int32)


def local(
    features,
    residual_in,
    short_filter,
    decay_rates,
    residues,
    skip_gain,
    out_weight,
    final_gain,
    embedding,
    next_ids,
):
    rows, _, width = features.shape
    short_len = short_filter.shape[0]
    modes = decay_rates.shape[1]
    streams = jnp.transpose(features, (1, 0, 2))
    rim = shifted(features[rows - (short_len - 1) :], "seq", 1)
    halo = jnp.pad(
        jnp.transpose(rim, (1, 0, 2)).astype(F32), ((0, 0), (SUBLANES - (short_len - 1), 0), (0, 0))
    )
    taps = short_filter.reshape(short_len * 3, width)
    rates = decay_rates.T.reshape(modes, width // LANES, LANES)
    weights = residues.T.reshape(modes, width // LANES, LANES)
    count, chans = lax.axis_size("seq"), lax.axis_size("chan")
    fast = chans == 2 and count == 16
    top = count // chans
    if fast:
        block = out_weight.shape[1]
        far = far_pieces(out_weight, range(0, block + 1, block // 4))
        far = [xor_permute(piece, "seq", top) for piece in far[:3]] + far[3:]
        core_weight = xor_permute(out_weight, "seq", 1)

    mixed, end = mixed_and_states(streams, halo, taps, rates)
    bits = range(count.bit_length() - 1)
    merges = [(0,), (1, 2), (3,)] if fast else [(bit,) for bit in bits]
    entering, held = entering_states(end, rates, rows, merges, far[:1] if fast else ())
    if fast:
        far = held + far[1:]
    if fast:
        entering, core_weight = tied(entering, core_weight)
    groups = width // GROUP
    edges = (0, groups // 2, groups) if fast else (0, groups)
    gated = []
    for base, stop in itertools.pairwise(edges):
        gated.append(
            gated_rows(
                streams,
                halo,
                taps,
                mixed,
                skip_gain[None, :],
                rates,
                weights,
                entering,
                base,
                stop - base,
            )
        )
        entering, _ = tied(entering, gated[-1])
    if fast:
        added, order = projected_fast(gated, out_weight, core_weight, far)
    else:
        added, order = projected_plain(gated[0], out_weight)
    block_out, packed = output_rows(order, added, residual_in, final_gain[None, :], embedding)
    first, second = summed_over_chan(packed)
    return block_out, log_likelihood(first, second, next_ids, float(width * chans))


def solution(mesh):
    return jax.shard_map(
        local,
        mesh=mesh,
        in_specs=(
            P("seq", None, "chan"),
            P("seq", "chan"),
            P(None, None, "chan"),
            P("chan", None),
            P("chan", None),
            P("chan"),
            P("chan", "seq"),
            P("chan"),
            P(None, "chan"),
            P("seq"),
        ),
        out_specs=(P("seq", "chan"), P("seq")),
        check_vma=False,
    )
```

time: 607 us -> 361 us (0.59)
  matrix products: 173 us -> 23.5 us
  starting transfers between devices: 10.9 us -> 127 us
  blocking collectives: 75.5 us -> 0 us
  local copies, waits for them, and re-layouts: 86 us -> 18.9 us
  waiting for transfers between devices: 196 us -> 131 us
  Pallas kernels: 0 us -> 32.5 us
  between operations: 14.2 us -> 1.49 us
  other arithmetic: 37.3 us -> 26.2 us
  loops' own time: 7.18 us -> 0 us
    dot_general x12 -> x8, matrix products: 173 us -> 23.5 us  [product(): jnp.dot(rows, weight, preferred_element_type=F32).astype(BF16)]
    ppermute x0 -> x35, waiting for transfers between devices: none -> 131 us  [the longest x21 104 us: xor_permute(): lax.ppermute(value, axis, [(source, source ^ mask) for source in range(co...]
    ppermute x0 -> x35, starting transfers between devices: none -> 125 us  [the longest x21 87 us: xor_permute(): lax.ppermute(value, axis, [(source, source ^ mask) for source in range(co...]
    reduce_scatter x1 -> x0, waiting for transfers between devices: 104 us -> none  [local(): lax.psum_scatter(partial_out, 'chan', scatter_dimension=1, tiled=True)]
    all_to_all x1 -> x0, waiting for transfers between devices: 71.9 us -> none  [local(): lax.all_to_all(mixed_kv.T, 'seq', split_axis=0, concat_axis=1, tiled=True)]
    all_to_all x1 -> x0, blocking collectives: 70.5 us -> none  [local(): lax.all_to_all(convolved.astype(jnp.bfloat16), 'seq', split_axis=1, conca...]
    select_n x2 -> x0, local copies, waits for them, and re-layouts: 54 us -> none  [modal_conv(): jnp.where(before[None, None], jnp.exp(-span[:, :, None, None] * jnp.maxim...]
    pallas_call x0 -> x5, Pallas kernels: none -> 32.5 us  [the longest x2 14.9 us: gated_rows(): pl.pallas_call(gated_kernel, grid=(steps,), in_specs=[pl.BlockSpec((1, ro...]
  transfers between devices with their start and end apart: 5 -> 36, of which waited for: 4 -> 14; matrix products, arithmetic and copies ran while one was open for 42% -> 17% of each run, Pallas kernels for 0% -> 7%
where the time goes in v1:
time: 361 us; the launch traced here: 360 us
  waiting for transfers between devices  131 us (36%)
  starting transfers between devices  127 us (35%)
  Pallas kernels  32.5 us (9%)
  other arithmetic  26.2 us (7%)
  matrix products  23.5 us (7%)
  local copies, waits for them, and re-layouts  18.9 us (5%)
    ppermute x21, waiting for transfers between devices, xor_permute(): lax.ppermute(value, axis, [(source, source ^ mask) for source in range(co...  104 us
    ppermute x21, starting transfers between devices, xor_permute(): lax.ppermute(value, axis, [(source, source ^ mask) for source in range(co...  87 us
    dot_general x8, matrix products, product(): jnp.dot(rows, weight, preferred_element_type=F32).astype(BF16)  23.5 us
    ppermute x5, starting transfers between devices, reduced(): other = lax.ppermute(partial, ('seq', 'chan'), pairs)  20.8 us
    concatenate x2, other arithmetic, joined(): jnp.concatenate([jnp.concatenate(parts, axis=1) for parts in rows], axis=0)  17.9 us
    ppermute x9, starting transfers between devices, reduced(): mine = lax.ppermute(mine, ('seq', 'chan'), pairs)  16.7 us
    ppermute x9, waiting for transfers between devices, reduced(): mine = lax.ppermute(mine, ('seq', 'chan'), pairs)  16 us
    pallas_call x2, Pallas kernels, gated_rows(): pl.pallas_call(gated_kernel, grid=(steps,), in_specs=[pl.BlockSpec((1, ro...  14.9 us
  transfers between devices with their start and end apart: 36, of which 14 were waited for; matrix products, arithmetic and copies ran while one was open for 17% of the time, Pallas kernels for 7%

profile of v1, /device:TPU:0, one launch (start us, length us, event | category | flops | bytes accessed | tf_op | source)
XLA Modules:
  0.0 359.8 jit_solution(11516878671007879153)
XLA Ops:
  4.3 4.3 %fusion.16 = (bf16[4096,128]{1,0:T(8,128)(2,1)}, bf16[4096,128]{1,0:T(8,128)(2,1)}, bf16[4096,128]{1,0:T(8,128)(2,1)}, bf16[4096,128]{1,0:T(8,128)(2,1)}) fusion(bf16[4096,512]{1,0:T(8,128)(2,1)} %param.16), kind=kLoop, calls=%fused_computation.55 | loop fusion | bytes 8388608 | tf_op jit(solution)/shard_map/slice | solution.py:334
  8.6 4.0 %collective-permute-start.5 = (bf16[4096,128]{1,0:T(8,128)(2,1)}, bf16[4096,128]{1,0:T(8,128)(2,1)}, u32[]{:S(2)}, u32[]{:S(2)}) collective-permute-start(bf16[4096,128]{1,0:T(8,128)(2,1)} %get-tuple-element.49), channel_id=1, source_target_pairs={{0,16},{2,18},{4,20},{6,22},{8,24},{10,26},{12,28},{14,30},{16,0},... | collective-permute-start | bytes 3145736 | tf_op jit(solution)/shard_map/ppermute | solution.py:20
  15.6 10.8 %mixed_and_states.1 = (bf16[256,4096]{1,0:T(8,128)(2,1)S(1)}, f32[16,32,128]{2,1,0:T(8,128)S(1)}) custom-call(bf16[3,256,4096]{2,1,0:T(8,128)(2,1)S(1)} %bitcast.63, bf16[3,256,4096]{2,1,0:T(8,128)(2,1)S(1)} %bitcast.64, f32[3,8,4096]{2,1,0:T(8,128)S(1)} %pad_convert_fusion.halo_ref, f32[9,4096]{1,0:T(8,128)S(1)} %reshape.13.taps_ref, ...), custom_call_target="tpu_custom_call" | custom-call | flops 1048576 | bytes 256 | tf_op jit(solution)/shard_map/mixed_and_states/pallas_call | solution.py:132
  32.8 18.1 %collective-permute-done.4 = f32[16,32,128]{2,1,0:T(8,128)S(1)} collective-permute-done((f32[16,32,128]{2,1,0:T(8,128)}, f32[16,32,128]{2,1,0:T(8,128)S(1)}, u32[]{:S(2)}, u32[]{:S(2)}) %collective-permute-start.4) | collective-permute-done | bytes 262176 | tf_op jit(solution)/shard_map/ppermute | solution.py:20
  50.8 5.3 %collective-permute-done.3 = f32[16,32,128]{2,1,0:T(8,128)} collective-permute-done((f32[16,32,128]{2,1,0:T(8,128)}, f32[16,32,128]{2,1,0:T(8,128)}, u32[]{:S(2)}, u32[]{:S(2)}) %collective-permute-start.3) | collective-permute-done | bytes 262176 | tf_op jit(solution)/shard_map/ppermute | solution.py:20
  58.1 23.4 %collective-permute-done.5 = bf16[4096,128]{1,0:T(8,128)(2,1)} collective-permute-done((bf16[4096,128]{1,0:T(8,128)(2,1)}, bf16[4096,128]{1,0:T(8,128)(2,1)}, u32[]{:S(2)}, u32[]{:S(2)}) %collective-permute-start.5) | collective-permute-done | bytes 1048608 | tf_op jit(solution)/shard_map/ppermute | solution.py:20
  81.5 4.2 %collective-permute-start.6 = (f32[16,32,128]{2,1,0:T(8,128)}, f32[16,32,128]{2,1,0:T(8,128)}, u32[]{:S(2)}, u32[]{:S(2)}) collective-permute-start(f32[16,32,128]{2,1,0:T(8,128)} %multiply_add_fusion), channel_id=1, source_target_pairs={{0,24},{2,26},{4,28},{6,30},{8,16},{10,18},{12,20},{14,22},{16,8},... | collective-permute-start | bytes 786440 | tf_op jit(solution)/shard_map/ppermute | solution.py:20
  86.8 6.4 %collective-permute-done.6 = f32[16,32,128]{2,1,0:T(8,128)} collective-permute-done((f32[16,32,128]{2,1,0:T(8,128)}, f32[16,32,128]{2,1,0:T(8,128)}, u32[]{:S(2)}, u32[]{:S(2)}) %collective-permute-start.6) | collective-permute-done | bytes 262176 | tf_op jit(solution)/shard_map/ppermute | solution.py:20
  97.5 7.5 %gated_rows.2 = bf16[256,2048]{1,0:T(8,128)(2,1)} custom-call(bf16[3,256,4096]{2,1,0:T(8,128)(2,1)S(1)} %bitcast.65, f32[3,8,4096]{2,1,0:T(8,128)S(1)} %pad_convert_fusion.halo_ref, f32[9,4096]{1,0:T(8,128)S(1)} %reshape.13.taps_ref, bf16[256,4096]{1,0:T(8,128)(2,1)S(1)} %get-tuple-element.24.mixed_ref, f32[1,4096]{1,0:T(1,128)S(1)} %bitcast.72, ...), custom_call_target="tpu_custom_call" | custom-call | flops 1048576 | bytes 256 | tf_op jit(solution)/shard_map/gated_rows/pallas_call | solution.py:162
  106.6 45.9 %collective-permute-start.10 = (bf16[256,2048]{1,0:T(8,128)(2,1)}, bf16[256,2048]{1,0:T(8,128)(2,1)}, u32[]{:S(2)}, u32[]{:S(2)}) collective-permute-start(bf16[256,2048]{1,0:T(8,128)(2,1)} %gated_rows.2), channel_id=1, source_target_pairs={{0,8},{2,10},{4,12},{6,14},{8,0},{10,2},{12,4},{14,6},{16,24},{18,... | collective-permute-start | bytes 3145736 | tf_op jit(solution)/shard_map/ppermute | solution.py:20
  152.5 7.5 %gated_rows.3 = bf16[256,2048]{1,0:T(8,128)(2,1)} custom-call(bf16[3,256,4096]{2,1,0:T(8,128)(2,1)S(1)} %bitcast.66, f32[3,8,4096]{2,1,0:T(8,128)S(1)} %pad_convert_fusion.halo_ref, f32[9,4096]{1,0:T(8,128)S(1)} %reshape.13.taps_ref, bf16[256,4096]{1,0:T(8,128)(2,1)S(1)} %get-tuple-element.24.mixed_ref, f32[1,4096]{1,0:T(1,128)S(1)} %bitcast.73, ...), custom_call_target="tpu_custom_call" | custom-call | flops 1048576 | bytes 256 | tf_op jit(solution)/shard_map/gated_rows/pallas_call | solution.py:162
  163.2 19.9 %collective-permute-done.10 = bf16[256,2048]{1,0:T(8,128)(2,1)} collective-permute-done((bf16[256,2048]{1,0:T(8,128)(2,1)}, bf16[256,2048]{1,0:T(8,128)(2,1)}, u32[]{:S(2)}, u32[]{:S(2)}) %collective-permute-start.10) | collective-permute-done | bytes 1048608 | tf_op jit(solution)/shard_map/ppermute | solution.py:20
  189.1 4.7 %convolution_convert_fusion.4 = bf16[512,512]{1,0:T(8,128)(2,1)S(1)} fusion(bf16[512,4096]{1,0:T(8,128)(2,1)S(1)} %maximum_maximum_fusion, bf16[4096,512]{1,0:T(8,128)(2,1)} %collective-permute-done.7), kind=kOutput, calls=%fused_computation.10 | convolution fusion | flops 2147745792 | bytes 8912896 | tf_op jit(solution)/shard_map/dot_general | solution.py:344
  197.7 7.7 %collective-permute-done.18 = bf16[256,2048]{1,0:T(8,128)(2,1)S(1)} collective-permute-done((bf16[256,2048]{1,0:T(8,128)(2,1)}, bf16[256,2048]{1,0:T(8,128)(2,1)S(1)}, u32[]{:S(2)}, u32[]{:S(2)}) %collective-permute-start.18) | collective-permute-done | bytes 1048608 | tf_op jit(solution)/shard_map/ppermute | solution.py:20
  206.9 11.0 %collective-permute-done.19 = bf16[256,2048]{1,0:T(8,128)(2,1)S(1)} collective-permute-done((bf16[256,2048]{1,0:T(8,128)(2,1)}, bf16[256,2048]{1,0:T(8,128)(2,1)S(1)}, u32[]{:S(2)}, u32[]{:S(2)}) %collective-permute-start.19) | collective-permute-done | bytes 1048608 | tf_op jit(solution)/shard_map/ppermute | solution.py:20
  219.6 15.3 %collective-permute-start.20 = (bf16[4096,128]{1,0:T(8,128)(2,1)S(1)}, bf16[4096,128]{1,0:T(8,128)(2,1)S(1)}, u32[]{:S(2)}, u32[]{:S(2)}) collective-permute-start(bf16[4096,128]{1,0:T(8,128)(2,1)S(1)} %copy-done.9), channel_id=1, source_target_pairs={{0,16},{2,18},{4,20},{6,22},{8,24},{10,26},{12,28},{14,30},{16,0},... | collective-permute-start | bytes 3145736 | tf_op jit(solution)/shard_map/ppermute | solution.py:20
  235.7 3.5 convolution_convert_fusion.1
  239.2 3.5 collective-permute-start.17
  243.1 3.6 %collective-permute-start.24 = (bf16[256,1024]{1,0:T(8,128)(2,1)S(1)}, bf16[256,1024]{1,0:T(8,128)(2,1)}, u32[]{:S(2)}, u32[]{:S(2)}) collective-permute-start(bf16[256,1024]{1,0:T(8,128)(2,1)S(1)} %slice.167), channel_id=1, source_target_pairs={{0,4},{2,6},{4,0},{6,2},{8,12},{10,14},{12,8},{14,10},{17,21},{19,... | collective-permute-start | bytes 1572872 | tf_op jit(solution)/shard_map/ppermute | solution.py:379
  246.7 15.6 %maximum_maximum_fusion.1 = bf16[512,4096]{1,0:T(8,128)(2,1)S(1)} fusion(bf16[256,2048]{1,0:T(8,128)(2,1)S(1)} %collective-permute-done.21, bf16[256,2048]{1,0:T(8,128)(2,1)S(1)} %collective-permute-done.19, bf16[256,2048]{1,0:T(8,128)(2,1)S(1)} %collective-permute-done.18, bf16[256,2048]{1,0:T(8,128)(2,1)} %collective-permute-done.10), kind=kLoop, calls=%fused_computation.1 | loop fusion | flops 16777216 | bytes 8388608 | tf_op jit(solution)/shard_map/concatenate | solution.py:340
  262.3 4.7 %convolution_convert_fusion.2 = bf16[512,512]{1,0:T(8,128)(2,1)S(1)} fusion(bf16[512,4096]{1,0:T(8,128)(2,1)S(1)} %maximum_maximum_fusion.1, bf16[4096,512]{1,0:T(8,128)(2,1)} %collective-permute-done.7), kind=kOutput, calls=%fused_computation.8 | convolution fusion | flops 2147745792 | bytes 8912896 | tf_op jit(solution)/shard_map/dot_general | solution.py:344
  269.5 3.5 convolution_convert_fusion
  273.0 5.8 %collective-permute-done.20 = bf16[4096,128]{1,0:T(8,128)(2,1)S(1)} collective-permute-done((bf16[4096,128]{1,0:T(8,128)(2,1)S(1)}, bf16[4096,128]{1,0:T(8,128)(2,1)S(1)}, u32[]{:S(2)}, u32[]{:S(2)}) %collective-permute-start.20) | collective-permute-done | bytes 1048608 | tf_op jit(solution)/shard_map/ppermute | solution.py:20
  281.1 6.4 %collective-permute-start.29 = (bf16[512,768]{1,0:T(8,128)(2,1)S(1)}, bf16[512,768]{1,0:T(8,128)(2,1)S(1)}, u32[]{:S(2)}, u32[]{:S(2)}) collective-permute-start(bf16[512,768]{1,0:T(8,128)(2,1)S(1)} %convolution_convert_fusion), channel_id=1, source_target_pairs={{0,1},{2,3},{4,5},{6,7},{8,9},{10,11},{12,13},{14,15},{17,16},{19,... | collective-permute-start | bytes 2359304 | tf_op jit(solution)/shard_map/ppermute | solution.py:370
  290.6 8.2 %collective-permute-start.23 = (bf16[1024,256]{1,0:T(8,128)(2,1)S(1)}, bf16[1024,256]{1,0:T(8,128)(2,1)S(1)}, u32[]{:S(2)}, u32[]{:S(2)}) collective-permute-start(bf16[1024,256]{1,0:T(8,128)(2,1)S(1)} %pad_maximum_fusion.2), channel_id=1, source_target_pairs={{0,1},{2,3},{4,5},{6,7},{8,9},{10,11},{12,13},{14,15},{17,16},{19,... | collective-permute-start | bytes 1572872 | tf_op jit(solution)/shard_map/ppermute | solution.py:370
  298.8 10.2 %collective-permute-done.27 = bf16[512,1024]{1,0:T(8,128)(2,1)S(1)} collective-permute-done((bf16[512,1024]{1,0:T(8,128)(2,1)S(1)}, bf16[512,1024]{1,0:T(8,128)(2,1)S(1)}, u32[]{:S(2)}, u32[]{:S(2)}) %collective-permute-start.27) | collective-permute-done | bytes 1048608 | tf_op jit(solution)/shard_map/ppermute | solution.py:370
  311.1 6.5 %collective-permute-start.28 = (bf16[256,1024]{1,0:T(8,128)(2,1)S(1)}, bf16[256,1024]{1,0:T(8,128)(2,1)S(1)}, u32[]{:S(2)}, u32[]{:S(2)}) collective-permute-start(bf16[256,1024]{1,0:T(8,128)(2,1)S(1)} %get-tuple-element.51), channel_id=1, source_target_pairs={{0,8},{2,10},{4,12},{6,14},{8,0},{10,2},{12,4},{14,6},{17,25},{19,... | collective-permute-start | bytes 1572872 | tf_op jit(solution)/shard_map/ppermute | solution.py:379
  324.8 5.5 %collective-permute-done.28 = bf16[256,1024]{1,0:T(8,128)(2,1)S(1)} collective-permute-done((bf16[256,1024]{1,0:T(8,128)(2,1)S(1)}, bf16[256,1024]{1,0:T(8,128)(2,1)S(1)}, u32[]{:S(2)}, u32[]{:S(2)}) %collective-permute-start.28) | collective-permute-done | bytes 524320 | tf_op jit(solution)/shard_map/ppermute | solution.py:379
  330.5 10.4 %collective-permute-done.32 = bf16[256,1024]{1,0:T(8,128)(2,1)S(1)} collective-permute-done((bf16[256,1024]{1,0:T(8,128)(2,1)S(1)}, bf16[256,1024]{1,0:T(8,128)(2,1)S(1)}, u32[]{:S(2)}, u32[]{:S(2)}) %collective-permute-start.32) | collective-permute-done | bytes 524320 | tf_op jit(solution)/shard_map/ppermute | solution.py:379
  341.1 5.9 %output_rows.1 = (bf16[256,4096]{1,0:T(8,128)(2,1)}, bf16[528,256]{1,0:T(8,128)(2,1)S(1)}) custom-call(s32[8]{0:T(128)S(1)} %iota_xor_fusion.order_ref, bf16[8,256,512]{2,1,0:T(8,128)(2,1)S(1)} %fusion.1.added_ref, bf16[256,4096]{1,0:T(8,128)(2,1)S(1)} %copy-done.3, f32[1,4096]{1,0:T(1,128)S(1)} %bitcast.74, bf16[512,4096]{1,0:T(8,128)(2,1)S(1)} %copy-done.2), custom_call_target="tpu_custom_call" | custom-call | flops 1073741824 | bytes 10485760 | tf_op jit(solution)/shard_map/output_rows/pallas_call | solution.py:251
  347.0 7.5 %collective-permute-start.35 = (bf16[528,256]{1,0:T(8,128)(2,1)S(1)}, bf16[528,256]{1,0:T(8,128)(2,1)S(1)}, u32[]{:S(2)}, u32[]{:S(2)}) collective-permute-start(bf16[528,256]{1,0:T(8,128)(2,1)S(1)} %get-tuple-element.45.first_ref), channel_id=1, source_target_pairs={{0,1},{1,0},{2,3},{3,2},{4,5},{5,4},{6,7},{7,6},{8,9},{9,8},{10,11... | collective-permute-start | bytes 811016 | tf_op jit(solution)/shard_map/ppermute | solution.py:20
  354.6 4.4 %collective-permute-done.35.second_ref = bf16[528,256]{1,0:T(8,128)(2,1)S(1)} collective-permute-done((bf16[528,256]{1,0:T(8,128)(2,1)S(1)}, bf16[528,256]{1,0:T(8,128)(2,1)S(1)}, u32[]{:S(2)}, u32[]{:S(2)}) %collective-permute-start.35) | collective-permute-done | bytes 270368 | tf_op jit(solution)/shard_map/ppermute | solution.py:20
  (138 shorter events, 57.3 us)
Async XLA Ops:
  0.6 94.0 %collective-permute-start.7 = (bf16[4096,512]{1,0:T(8,128)(2,1)}, bf16[4096,512]{1,0:T(8,128)(2,1)}, u32[]{:S(2)}, u32[]{:S(2)}) collective-permute-start(bf16[4096,512]{1,0:T(8,128)(2,1)} %param.16), channel_id=1, source_target_pairs={{0,2},{2,0},{4,6},{6,4},{8,10},{10,8},{12,14},{14,12},{16,18},{18,... | collective-permute-start | bytes 12582920 | tf_op jit(solution)/shard_map/ppermute | solution.py:20
  2.2 10.6 %collective-permute-start = (bf16[2,3,4096]{2,0,1:T(2,128)(2,1)S(1)}, bf16[2,3,4096]{2,0,1:T(2,128)(2,1)S(1)}, u32[]{:S(2)}, u32[]{:S(2)}) collective-permute-start(bf16[2,3,4096]{2,0,1:T(2,128)(2,1)S(1)} %slice.123), channel_id=1, source_target_pairs={{0,2},{2,4},{4,6},{6,8},{8,10},{10,12},{12,14},{14,16},{16,18},{18... | collective-permute-start | bytes 147464 | tf_op jit(solution)/shard_map/ppermute | solution.py:26
  8.6 72.9 %collective-permute-start.5 = (bf16[4096,128]{1,0:T(8,128)(2,1)}, bf16[4096,128]{1,0:T(8,128)(2,1)}, u32[]{:S(2)}, u32[]{:S(2)}) collective-permute-start(bf16[4096,128]{1,0:T(8,128)(2,1)} %get-tuple-element.49), channel_id=1, source_target_pairs={{0,16},{2,18},{4,20},{6,22},{8,24},{10,26},{12,28},{14,30},{16,0},... | collective-permute-start | bytes 3145736 | tf_op jit(solution)/shard_map/ppermute | solution.py:20
  29.3 21.6 %collective-permute-start.4 = (f32[16,32,128]{2,1,0:T(8,128)}, f32[16,32,128]{2,1,0:T(8,128)S(1)}, u32[]{:S(2)}, u32[]{:S(2)}) collective-permute-start(f32[16,32,128]{2,1,0:T(8,128)} %multiply_add_fusion.1), channel_id=1, source_target_pairs={{0,12},{2,14},{4,8},{6,10},{8,4},{10,6},{12,0},{14,2},{16,28},{18,... | collective-permute-start | bytes 786440 | tf_op jit(solution)/shard_map/ppermute | solution.py:20
  31.3 24.8 %collective-permute-start.3 = (f32[16,32,128]{2,1,0:T(8,128)}, f32[16,32,128]{2,1,0:T(8,128)}, u32[]{:S(2)}, u32[]{:S(2)}) collective-permute-start(f32[16,32,128]{2,1,0:T(8,128)} %multiply_add_fusion.1), channel_id=1, source_target_pairs={{0,8},{2,10},{4,12},{6,14},{8,0},{10,2},{12,4},{14,6},{16,24},{18,... | collective-permute-start | bytes 786440 | tf_op jit(solution)/shard_map/ppermute | solution.py:20
  32.3 23.8 %collective-permute-start.2 = (f32[16,32,128]{2,1,0:T(8,128)}, f32[16,32,128]{2,1,0:T(8,128)}, u32[]{:S(2)}, u32[]{:S(2)}) collective-permute-start(f32[16,32,128]{2,1,0:T(8,128)} %multiply_add_fusion.1), channel_id=1, source_target_pairs={{0,4},{2,6},{4,0},{6,2},{8,12},{10,14},{12,8},{14,10},{16,20},{18,... | collective-permute-start | bytes 786440 | tf_op jit(solution)/shard_map/ppermute | solution.py:20
  50.8 109.1 %collective-permute-start.11 = (bf16[4096,128]{1,0:T(8,128)(2,1)}, bf16[4096,128]{1,0:T(8,128)(2,1)}, u32[]{:S(2)}, u32[]{:S(2)}) collective-permute-start(bf16[4096,128]{1,0:T(8,128)(2,1)} %get-tuple-element.47), channel_id=1, source_target_pairs={{0,16},{2,18},{4,20},{6,22},{8,24},{10,26},{12,28},{14,30},{16,0},... | collective-permute-start | bytes 3145736 | tf_op jit(solution)/shard_map/ppermute | solution.py:20
  81.5 11.7 %collective-permute-start.6 = (f32[16,32,128]{2,1,0:T(8,128)}, f32[16,32,128]{2,1,0:T(8,128)}, u32[]{:S(2)}, u32[]{:S(2)}) collective-permute-start(f32[16,32,128]{2,1,0:T(8,128)} %multiply_add_fusion), channel_id=1, source_target_pairs={{0,24},{2,26},{4,28},{6,30},{8,16},{10,18},{12,20},{14,22},{16,8},... | collective-permute-start | bytes 786440 | tf_op jit(solution)/shard_map/ppermute | solution.py:20
  85.7 74.6 %collective-permute-start.9 = (bf16[4096,128]{1,0:T(8,128)(2,1)}, bf16[4096,128]{1,0:T(8,128)(2,1)}, u32[]{:S(2)}, u32[]{:S(2)}) collective-permute-start(bf16[4096,128]{1,0:T(8,128)(2,1)} %get-tuple-element.48), channel_id=1, source_target_pairs={{0,16},{2,18},{4,20},{6,22},{8,24},{10,26},{12,28},{14,30},{16,0},... | collective-permute-start | bytes 3145736 | tf_op jit(solution)/shard_map/ppermute | solution.py:20
  105.0 55.5 %collective-permute-start.8 = (bf16[256,2048]{1,0:T(8,128)(2,1)}, bf16[256,2048]{1,0:T(8,128)(2,1)}, u32[]{:S(2)}, u32[]{:S(2)}) collective-permute-start(bf16[256,2048]{1,0:T(8,128)(2,1)} %gated_rows.2), channel_id=1, source_target_pairs={{0,4},{2,6},{4,0},{6,2},{8,12},{10,14},{12,8},{14,10},{16,20},{18,... | collective-permute-start | bytes 3145736 | tf_op jit(solution)/shard_map/ppermute | solution.py:20
  106.6 76.5 %collective-permute-start.10 = (bf16[256,2048]{1,0:T(8,128)(2,1)}, bf16[256,2048]{1,0:T(8,128)(2,1)}, u32[]{:S(2)}, u32[]{:S(2)}) collective-permute-start(bf16[256,2048]{1,0:T(8,128)(2,1)} %gated_rows.2), channel_id=1, source_target_pairs={{0,8},{2,10},{4,12},{6,14},{8,0},{10,2},{12,4},{14,6},{16,24},{18,... | collective-permute-start | bytes 3145736 | tf_op jit(solution)/shard_map/ppermute | solution.py:20
  160.0 24.5 %collective-permute-start.12 = (bf16[256,2048]{1,0:T(8,128)(2,1)}, bf16[256,2048]{1,0:T(8,128)(2,1)S(1)}, u32[]{:S(2)}, u32[]{:S(2)}) collective-permute-start(bf16[256,2048]{1,0:T(8,128)(2,1)} %gated_rows.3), channel_id=1, source_target_pairs={{0,4},{2,6},{4,0},{6,2},{8,12},{10,14},{12,8},{14,10},{16,20},{18,... | collective-permute-start | bytes 3145736 | tf_op jit(solution)/shard_map/ppermute | solution.py:20
  160.3 45.1 %collective-permute-start.18 = (bf16[256,2048]{1,0:T(8,128)(2,1)}, bf16[256,2048]{1,0:T(8,128)(2,1)S(1)}, u32[]{:S(2)}, u32[]{:S(2)}) collective-permute-start(bf16[256,2048]{1,0:T(8,128)(2,1)} %gated_rows.3), channel_id=1, source_target_pairs={{0,8},{2,10},{4,12},{6,14},{8,0},{10,2},{12,4},{14,6},{16,24},{18,... | collective-permute-start | bytes 3145736 | tf_op jit(solution)/shard_map/ppermute | solution.py:20
  160.3 74.8 %collective-permute-start.15 = (bf16[4096,128]{1,0:T(8,128)(2,1)}, bf16[4096,128]{1,0:T(8,128)(2,1)S(1)}, u32[]{:S(2)}, u32[]{:S(2)}) collective-permute-start(bf16[4096,128]{1,0:T(8,128)(2,1)} %collective-permute-done.11), channel_id=1, source_target_pairs={{0,2},{2,0},{4,6},{6,4},{8,10},{10,8},{12,14},{14,12},{16,18},{18,... | collective-permute-start | bytes 3145736 | tf_op jit(solution)/shard_map/ppermute | solution.py:20
  160.5 59.1 %collective-permute-start.14 = (bf16[4096,128]{1,0:T(8,128)(2,1)}, bf16[4096,128]{1,0:T(8,128)(2,1)S(1)}, u32[]{:S(2)}, u32[]{:S(2)}) collective-permute-start(bf16[4096,128]{1,0:T(8,128)(2,1)} %collective-permute-done.5), channel_id=1, source_target_pairs={{0,2},{2,0},{4,6},{6,4},{8,10},{10,8},{12,14},{14,12},{16,18},{18,... | collective-permute-start | bytes 3145736 | tf_op jit(solution)/shard_map/ppermute | solution.py:20
  193.8 24.1 %collective-permute-start.19 = (bf16[256,2048]{1,0:T(8,128)(2,1)}, bf16[256,2048]{1,0:T(8,128)(2,1)S(1)}, u32[]{:S(2)}, u32[]{:S(2)}) collective-permute-start(bf16[256,2048]{1,0:T(8,128)(2,1)} %collective-permute-done.10), channel_id=1, source_target_pairs={{0,4},{2,6},{4,0},{6,2},{8,12},{10,14},{12,8},{14,10},{16,20},{18,... | collective-permute-start | bytes 3145736 | tf_op jit(solution)/shard_map/ppermute | solution.py:20
  194.6 40.8 %collective-permute-start.16 = (bf16[4096,128]{1,0:T(8,128)(2,1)}, bf16[4096,128]{1,0:T(8,128)(2,1)S(1)}, u32[]{:S(2)}, u32[]{:S(2)}) collective-permute-start(bf16[4096,128]{1,0:T(8,128)(2,1)} %collective-permute-done.9), channel_id=1, source_target_pairs={{0,2},{2,0},{4,6},{6,4},{8,10},{10,8},{12,14},{14,12},{16,18},{18,... | collective-permute-start | bytes 3145736 | tf_op jit(solution)/shard_map/ppermute | solution.py:20
  205.4 37.3 %collective-permute-start.13 = (bf16[512,1024]{1,0:T(8,128)(2,1)S(1)}, bf16[512,1024]{1,0:T(8,128)(2,1)S(1)}, u32[]{:S(2)}, u32[]{:S(2)}) collective-permute-start(bf16[512,1024]{1,0:T(8,128)(2,1)S(1)} %pad_maximum_fusion), channel_id=1, source_target_pairs={{1,0},{3,2},{5,4},{7,6},{9,8},{11,10},{13,12},{15,14},{16,17},{18,... | collective-permute-start | bytes 3145736 | tf_op jit(solution)/shard_map/ppermute | solution.py:370
  217.8 28.9 %collective-permute-start.21 = (bf16[256,2048]{1,0:T(8,128)(2,1)S(1)}, bf16[256,2048]{1,0:T(8,128)(2,1)S(1)}, u32[]{:S(2)}, u32[]{:S(2)}) collective-permute-start(bf16[256,2048]{1,0:T(8,128)(2,1)S(1)} %collective-permute-done.18), channel_id=1, source_target_pairs={{0,4},{2,6},{4,0},{6,2},{8,12},{10,14},{12,8},{14,10},{16,20},{18,... | collective-permute-start | bytes 3145736 | tf_op jit(solution)/shard_map/ppermute | solution.py:20
  219.6 59.2 %collective-permute-start.20 = (bf16[4096,128]{1,0:T(8,128)(2,1)S(1)}, bf16[4096,128]{1,0:T(8,128)(2,1)S(1)}, u32[]{:S(2)}, u32[]{:S(2)}) collective-permute-start(bf16[4096,128]{1,0:T(8,128)(2,1)S(1)} %copy-done.9), channel_id=1, source_target_pairs={{0,16},{2,18},{4,20},{6,22},{8,24},{10,26},{12,28},{14,30},{16,0},... | collective-permute-start | bytes 3145736 | tf_op jit(solution)/shard_map/ppermute | solution.py:20
  239.2 39.7 %collective-permute-start.17 = (bf16[512,768]{1,0:T(8,128)(2,1)S(1)}, bf16[512,768]{1,0:T(8,128)(2,1)S(1)}, u32[]{:S(2)}, u32[]{:S(2)}) collective-permute-start(bf16[512,768]{1,0:T(8,128)(2,1)S(1)} %convolution_convert_fusion.1), channel_id=1, source_target_pairs={{0,1},{2,3},{4,5},{6,7},{8,9},{10,11},{12,13},{14,15},{17,16},{19,... | collective-permute-start | bytes 2359304 | tf_op jit(solution)/shard_map/ppermute | solution.py:370
  243.1 79.6 %collective-permute-start.24 = (bf16[256,1024]{1,0:T(8,128)(2,1)S(1)}, bf16[256,1024]{1,0:T(8,128)(2,1)}, u32[]{:S(2)}, u32[]{:S(2)}) collective-permute-start(bf16[256,1024]{1,0:T(8,128)(2,1)S(1)} %slice.167), channel_id=1, source_target_pairs={{0,4},{2,6},{4,0},{6,2},{8,12},{10,14},{12,8},{14,10},{17,21},{19,... | collective-permute-start | bytes 1572872 | tf_op jit(solution)/shard_map/ppermute | solution.py:379
  278.8 9.0 %collective-permute-start.22 = (bf16[4096,128]{1,0:T(8,128)(2,1)S(1)}, bf16[4096,128]{1,0:T(8,128)(2,1)S(1)}, u32[]{:S(2)}, u32[]{:S(2)}) collective-permute-start(bf16[4096,128]{1,0:T(8,128)(2,1)S(1)} %collective-permute-done.20), channel_id=1, source_target_pairs={{0,2},{2,0},{4,6},{6,4},{8,10},{10,8},{12,14},{14,12},{16,18},{18,... | collective-permute-start | bytes 3145736 | tf_op jit(solution)/shard_map/ppermute | solution.py:20
  279.1 8.7 %collective-permute-start.25 = (bf16[256,768]{1,0:T(8,128)(2,1)S(1)}, bf16[256,768]{1,0:T(8,128)(2,1)S(1)}, u32[]{:S(2)}, u32[]{:S(2)}) collective-permute-start(bf16[256,768]{1,0:T(8,128)(2,1)S(1)} %slice.169), channel_id=1, source_target_pairs={{1,5},{3,7},{5,1},{7,3},{9,13},{11,15},{13,9},{15,11},{16,20},{18,... | collective-permute-start | bytes 1179656 | tf_op jit(solution)/shard_map/ppermute | solution.py:379
  279.8 29.2 %collective-permute-start.27 = (bf16[512,1024]{1,0:T(8,128)(2,1)S(1)}, bf16[512,1024]{1,0:T(8,128)(2,1)S(1)}, u32[]{:S(2)}, u32[]{:S(2)}) collective-permute-start(bf16[512,1024]{1,0:T(8,128)(2,1)S(1)} %pad_maximum_fusion.1), channel_id=1, source_target_pairs={{1,0},{3,2},{5,4},{7,6},{9,8},{11,10},{13,12},{15,14},{16,17},{18,... | collective-permute-start | bytes 3145736 | tf_op jit(solution)/shard_map/ppermute | solution.py:370
  281.1 27.9 %collective-permute-start.29 = (bf16[512,768]{1,0:T(8,128)(2,1)S(1)}, bf16[512,768]{1,0:T(8,128)(2,1)S(1)}, u32[]{:S(2)}, u32[]{:S(2)}) collective-permute-start(bf16[512,768]{1,0:T(8,128)(2,1)S(1)} %convolution_convert_fusion), channel_id=1, source_target_pairs={{0,1},{2,3},{4,5},{6,7},{8,9},{10,11},{12,13},{14,15},{17,16},{19,... | collective-permute-start | bytes 2359304 | tf_op jit(solution)/shard_map/ppermute | solution.py:370
  290.6 29.3 %collective-permute-start.23 = (bf16[1024,256]{1,0:T(8,128)(2,1)S(1)}, bf16[1024,256]{1,0:T(8,128)(2,1)S(1)}, u32[]{:S(2)}, u32[]{:S(2)}) collective-permute-start(bf16[1024,256]{1,0:T(8,128)(2,1)S(1)} %pad_maximum_fusion.2), channel_id=1, source_target_pairs={{0,1},{2,3},{4,5},{6,7},{8,9},{10,11},{12,13},{14,15},{17,16},{19,... | collective-permute-start | bytes 1572872 | tf_op jit(solution)/shard_map/ppermute | solution.py:370
  309.3 8.3 %collective-permute-start.30 = (bf16[256,768]{1,0:T(8,128)(2,1)S(1)}, bf16[256,768]{1,0:T(8,128)(2,1)S(1)}, u32[]{:S(2)}, u32[]{:S(2)}) collective-permute-start(bf16[256,768]{1,0:T(8,128)(2,1)S(1)} %get-tuple-element.53), channel_id=1, source_target_pairs={{1,9},{3,11},{5,13},{7,15},{9,1},{11,3},{13,5},{15,7},{16,24},{18,... | collective-permute-start | bytes 1179656 | tf_op jit(solution)/shard_map/ppermute | solution.py:379
  310.4 9.5 %collective-permute-start.33 = (bf16[256,768]{1,0:T(8,128)(2,1)S(1)}, bf16[256,768]{1,0:T(8,128)(2,1)S(1)}, u32[]{:S(2)}, u32[]{:S(2)}) collective-permute-start(bf16[256,768]{1,0:T(8,128)(2,1)S(1)} %get-tuple-element.52), channel_id=1, source_target_pairs={{1,13},{3,15},{5,9},{7,11},{9,5},{11,7},{13,1},{15,3},{16,28},{18,... | collective-permute-start | bytes 1179656 | tf_op jit(solution)/shard_map/ppermute | solution.py:379
  311.1 19.2 %collective-permute-start.28 = (bf16[256,1024]{1,0:T(8,128)(2,1)S(1)}, bf16[256,1024]{1,0:T(8,128)(2,1)S(1)}, u32[]{:S(2)}, u32[]{:S(2)}) collective-permute-start(bf16[256,1024]{1,0:T(8,128)(2,1)S(1)} %get-tuple-element.51), channel_id=1, source_target_pairs={{0,8},{2,10},{4,12},{6,14},{8,0},{10,2},{12,4},{14,6},{17,25},{19,... | collective-permute-start | bytes 1572872 | tf_op jit(solution)/shard_map/ppermute | solution.py:379
  317.6 23.3 %collective-permute-start.32 = (bf16[256,1024]{1,0:T(8,128)(2,1)S(1)}, bf16[256,1024]{1,0:T(8,128)(2,1)S(1)}, u32[]{:S(2)}, u32[]{:S(2)}) collective-permute-start(bf16[256,1024]{1,0:T(8,128)(2,1)S(1)} %get-tuple-element.50), channel_id=1, source_target_pairs={{0,12},{2,14},{4,8},{6,10},{8,4},{10,6},{12,0},{14,2},{17,29},{19,... | collective-permute-start | bytes 1572872 | tf_op jit(solution)/shard_map/ppermute | solution.py:379
  347.0 12.0 %collective-permute-start.35 = (bf16[528,256]{1,0:T(8,128)(2,1)S(1)}, bf16[528,256]{1,0:T(8,128)(2,1)S(1)}, u32[]{:S(2)}, u32[]{:S(2)}) collective-permute-start(bf16[528,256]{1,0:T(8,128)(2,1)S(1)} %get-tuple-element.45.first_ref), channel_id=1, source_target_pairs={{0,1},{1,0},{2,3},{3,2},{4,5},{5,4},{6,7},{7,6},{8,9},{9,8},{10,11... | collective-permute-start | bytes 811016 | tf_op jit(solution)/shard_map/ppermute | solution.py:20
  (21 other events, 296.9 us)

commit v2 on v1

--- a/solution.py
+++ b/solution.py
@@ -194,9 +194,8 @@
         last = bits == merges[-1]
         if last and before_last:
             total, *held = tied(total, *before_last)
-        extra = span >> 1 if last and count == 2 else 0
         others = [
-            (mask, xor_permute(total, "seq", (mask * span) | extra)) for mask in range(1, count)
+            (mask, xor_permute(total, "seq", mask * span)) for mask in range(1, count)
         ]
         own = (place // span) % count
         inside = (place % span) * rows
@@ -316,98 +315,113 @@
     return total, xor_permute(total, "chan", span)
 
 
-def placed_pairs(count, chans, per_chan, same, seq_mask, chan_mask):
-    pairs = []
-    for place, chan in itertools.product(range(count), range(chans)):
-        if (place // per_chan == chan) == same:
-            target = (place ^ seq_mask) * chans + (chan ^ chan_mask)
-            pairs.append((place * chans + chan, target))
-    return pairs
-
-
 def tied(*values):
     return lax.optimization_barrier(values)
 
 
-def far_pieces(out_weight, cuts):
-    return [
-        lax.slice_in_dim(out_weight, first, last, axis=1)
-        for first, last in itertools.pairwise(cuts)
-    ]
-
-
-def joined(*rows):
-    return tied(jnp.concatenate([jnp.concatenate(parts, axis=1) for parts in rows], axis=0))[0]
-
-
-def product(rows, *weights):
-    outs = [jnp.dot(rows, weight, preferred_element_type=F32).astype(BF16) for weight in weights]
-    return outs[0] if len(outs) == 1 else jnp.concatenate(outs, axis=1)
-
-
-def projected_fast(gated, out_weight, core_weight, far):
+def column_pieces(weight, cuts):
+    return [lax.slice_in_dim(weight, first, last, axis=1) for first, last in itertools.pairwise(cuts)]
+
+
+def join_kernel(steps, *refs):
+    pieces, out_ref = refs[:-1], refs[-1]
+    half = len(pieces) // 2
+    rows = pieces[0].shape[0]
+    at = pl.program_id(0)
+    for held, wanted in ((pieces[:half], at < steps), (pieces[half:], at >= steps)):
+
+        @pl.when(wanted)
+        def _(held=held):
+            for index, piece in enumerate(held):
+                out_ref[index * rows : (index + 1) * rows, :] = piece[...]
+
+
+def joined(*rows_of):
+    leading, others = ([parts[half] for parts in rows_of] for half in range(2))
+    rows = leading[0].shape[0]
+    steps, more = leading[0].shape[1] // GROUP, others[0].shape[1] // GROUP
+    return pl.pallas_call(
+        functools.partial(join_kernel, steps),
+        grid=(steps + more,),
+        in_specs=[pl.BlockSpec((rows, GROUP), lambda g: (0, jnp.minimum(g, steps - 1)))] * len(leading)
+        + [pl.BlockSpec((rows, GROUP), lambda g: (0, jnp.maximum(g - steps, 0)))] * len(others),
+        out_specs=pl.BlockSpec((rows * len(leading), GROUP), lambda g: (0, g)),
+        out_shape=jax.ShapeDtypeStruct((rows * len(leading), (steps + more) * GROUP), BF16),
+        compiler_params=vmem_params(32),
+        cost_estimate=pl.CostEstimate(flops=rows * GROUP, bytes_accessed=rows, transcendentals=0),
+        name="joined",
+    )(*leading, *others)
+
+
+def product(rows, weight):
+    return jnp.dot(rows, weight, preferred_element_type=F32).astype(BF16)
+
+
+def projected_fast(gated, out_weight, core_weight, far, cuts):
     count, chans = lax.axis_size("seq"), lax.axis_size("chan")
     per_chan = count // chans
-    rows, block = gated[0].shape[0], out_weight.shape[1]
+    rows = gated[0].shape[0]
     core, side, low = 1, 2, 4
+    here = lax.axis_index("seq") // per_chan == lax.axis_index("chan")
 
     below = [xor_permute(part, "seq", low) for part in gated]
-    beside = [xor_permute(gated[0], "seq", side)]
-    later, far[1] = tied(gated[1], far[1])
-    beside.append(xor_permute(later, "seq", side))
-    below[0], beside[1] = tied(below[0], beside[1])
+    beside = [xor_permute(part, "seq", side) for part in gated]
+    below[0], beside[0] = tied(below[0], beside[0])
     across = [xor_permute(below[0], "seq", side)]
-    beside[0], far[2], far[0] = tied(beside[0], far[2], far[0])
+    below[1], beside[1], far[0], far[1], across[0] = tied(
+        below[1], beside[1], far[0], far[1], across[0]
+    )
+    across.append(xor_permute(below[1], "seq", side))
     first = joined(gated, beside)
-    near_first = product(first, out_weight, core_weight)
-    below[1], across[0], waiting = tied(below[1], across[0], far[3])
-    far[3] = xor_permute(waiting, "seq", per_chan)
-    across.append(xor_permute(below[1], "seq", side))
-    second = joined(below, across)
-
-    def reduced(partial, masks, same, after=None):
-        pairs = placed_pairs(count, chans, per_chan, not same, 0, 1)
-        other = lax.ppermute(partial, ("seq", "chan"), pairs)
-        if after is not None:
-            other, _ = tied(other, after)
-        total = (partial.astype(F32) + other.astype(F32)).astype(BF16)
-        back = []
+    near_first = [product(first, out_weight), product(first, core_weight)]
+
+    def far_products(rows_all, which):
+        return [product(rows_all, far[which]), product(rows_all, far_core[which])]
+
+    def shared(near, parts, span):
+        first_at, last_at = span
+        close = jnp.concatenate([part[:, first_at:last_at] for part in near], axis=1)
+        distant = jnp.concatenate(
+            [jnp.concatenate([part[half] for part in parts], axis=1) for half in range(2)], axis=1
+        )
+        return jnp.where(here, distant, close), jnp.where(here, close, distant)
+
+    def summed(sent, kept):
+        other = xor_permute(sent, "chan", 1)
+        return (kept.astype(F32) + other.astype(F32)).astype(BF16)
+
+    def returned(total, masks):
+        back = {}
         for at, mask in enumerate(masks):
             mine = total[at * rows : (at + 1) * rows]
-            if mask:
-                pairs = placed_pairs(count, chans, per_chan, same, mask, 0)
-                mine = lax.ppermute(mine, ("seq", "chan"), pairs)
-            back.append(mine)
+            back[mask] = xor_permute(mine, "seq", mask) if mask else mine
         return back
 
-    far_core = [xor_permute(piece, "seq", core) for piece in far[:-1]]
-    near_back = reduced(near_first, (0, side), True)
-    early = jnp.concatenate(far[:-1] + far_core, axis=1)
-    early_first = product(first, early)
-    near_second = product(second, out_weight, core_weight)
-    early_second = product(second, early)
-    last, *_ = tied(far[-1], early_second, near_second)
-    last_core = xor_permute(last, "seq", core)
-    last = jnp.concatenate([last, last_core], axis=1)
-    last_all = jnp.concatenate([product(first, last), product(second, last)], axis=0)
-    near_back += reduced(near_second, (low, low | side), True, last_all)
-    early_back = reduced(early_first, (0, side), False)
-    early_back += reduced(early_second, (low, low | side), False, last_all)
-    last_back = reduced(last_all, (0, side, low, low | side), False)
-    here = lax.axis_index("seq") // per_chan == lax.axis_index("chan")
-    cut = block - last_core.shape[1]
+    far_core = [xor_permute(piece, "seq", core) for piece in far[:2]]
+    early = (0, cuts[2])
+    parts = [far_products(first, 0), far_products(first, 1)]
+    sent, kept = shared(near_first, parts, early)
+    sent, *across = tied(sent, *across)
+    back = returned(summed(sent, kept), (0, side))
+    second = joined(below, across)
+    near_second = [product(second, out_weight), product(second, core_weight)]
+    parts = [far_products(second, 0), far_products(second, 1)]
+    total = summed(*shared(near_second, parts, early))
+    last, _ = tied(far[2], parts)
+    far_core.append(xor_permute(last, "seq", core))
+    last_span = (cuts[2], cuts[3])
+    last_total = [
+        summed(*shared(near, [far_products(rows_all, 2)], last_span))
+        for near, rows_all in ((near_first, first), (near_second, second))
+    ]
+    back |= returned(total, (low, low | side))
+    last_back = returned(last_total[0], (0, side)) | returned(last_total[1], (low, low | side))
     blocks = {}
-    for at, mask in enumerate((0, side, low, low | side)):
+    for mask in (0, side, low, low | side):
         for half in range(2):
-            near_block = near_back[at][:, half * block : (half + 1) * block]
-            late_block = jnp.concatenate(
-                [
-                    early_back[at][:, half * cut : (half + 1) * cut],
-                    last_back[at][:, half * (block - cut) : (half + 1) * (block - cut)],
-                ],
-                axis=1,
+            blocks[mask | (half * core)] = jnp.concatenate(
+                [jnp.split(value[mask], 2, axis=1)[half] for value in (back, last_back)], axis=1
             )
-            blocks[mask | (half * core)] = jnp.where(here, near_block, late_block)
     added = jnp.stack([blocks[mask] for mask in range(per_chan)])
     order = jnp.arange(per_chan, dtype=jnp.int32) ^ (lax.axis_index("seq") % per_chan)
     return added, order
@@ -455,8 +469,9 @@
     top = count // chans
     if fast:
         block = out_weight.shape[1]
-        far = far_pieces(out_weight, range(0, block + 1, block // 4))
-        far = [xor_permute(piece, "seq", top) for piece in far[:3]] + far[3:]
+        cuts = (0, block // 4, block * 3 // 4, block)
+        far = column_pieces(out_weight, cuts)
+        far[0] = xor_permute(far[0], "seq", top)
         core_weight = xor_permute(out_weight, "seq", 1)
 
     mixed, end = mixed_and_states(streams, halo, taps, rates)
@@ -464,7 +479,8 @@
     merges = [(0,), (1, 2), (3,)] if fast else [(bit,) for bit in bits]
     entering, held = entering_states(end, rates, rows, merges, far[:1] if fast else ())
     if fast:
-        far = held + far[1:]
+        entering, *waiting = tied(entering, *far[1:])
+        far = held + [xor_permute(piece, "seq", top) for piece in waiting]
     if fast:
         entering, core_weight = tied(entering, core_weight)
     groups = width // GROUP
@@ -487,7 +503,7 @@
         )
         entering, _ = tied(entering, gated[-1])
     if fast:
-        added, order = projected_fast(gated, out_weight, core_weight, far)
+        added, order = projected_fast(gated, out_weight, core_weight, far, cuts)
     else:
         added, order = projected_plain(gated[0], out_weight)
     block_out, packed = output_rows(order, added, residual_in, final_gain[None, :], embedding)

time: 361 us -> 333 us (0.922)
  starting transfers between devices: 127 us -> 34.9 us
  waiting for transfers between devices: 131 us -> 201 us
  other arithmetic: 26.2 us -> 5.83 us
  matrix products: 23.5 us -> 34.8 us
  Pallas kernels: 32.5 us -> 36.7 us
    ppermute x21 -> x29, waiting for transfers between devices: 104 us -> 201 us  [xor_permute(): lax.ppermute(value, axis, [(source, source ^ mask) for source in range(co...]
    ppermute x21 -> x29, starting transfers between devices: 87 us -> 32.9 us  [xor_permute(): lax.ppermute(value, axis, [(source, source ^ mask) for source in range(co...]
    ppermute x14 -> x0, starting transfers between devices: 37.5 us -> none  [the longest x5 20.8 us: reduced(): other = lax.ppermute(partial, ('seq', 'chan'), pairs)]
    ppermute x14 -> x0, waiting for transfers between devices: 26.2 us -> none  [the longest x9 16 us: reduced(): mine = lax.ppermute(mine, ('seq', 'chan'), pairs)]
    concatenate x5 -> x0, other arithmetic: 18.2 us -> none  [the longest x2 17.9 us: joined(): jnp.concatenate([jnp.concatenate(parts, axis=1) for parts in rows], axis=0)]
    dot_general x8 -> x16, matrix products: 23.5 us -> 34.8 us  [product(): return jnp.dot(rows, weight, preferred_element_type=F32).astype(BF16)]
    pallas_call x0 -> x2, Pallas kernels: none -> 4.91 us  [joined(): pl.pallas_call(functools.partial(join_kernel, steps), grid=(steps + more,...]
    unnamed x42 -> x30, local copies, waits for them, and re-layouts: 12.6 us -> 10.2 us
  transfers between devices with their start and end apart: 36 -> 30, of which waited for: 14 -> 14; matrix products, arithmetic and copies ran while one was open for 17% -> 15% of each run, Pallas kernels for 7% -> 7%
where the time goes in v2:
time: 333 us; the launch traced here: 332 us
  waiting for transfers between devices  201 us (60%)
  Pallas kernels  36.7 us (11%)
  starting transfers between devices  34.9 us (10%)
  matrix products  34.8 us (10%)
  local copies, waits for them, and re-layouts  17.8 us (5%)
  other arithmetic  5.83 us (2%)
    ppermute x29, waiting for transfers between devices, xor_permute(): lax.ppermute(value, axis, [(source, source ^ mask) for source in range(co...  201 us
    dot_general x16, matrix products, product(): return jnp.dot(rows, weight, preferred_element_type=F32).astype(BF16)  34.8 us
    ppermute x29, starting transfers between devices, xor_permute(): lax.ppermute(value, axis, [(source, source ^ mask) for source in range(co...  32.9 us
    pallas_call x2, Pallas kernels, gated_rows(): pl.pallas_call(gated_kernel, grid=(steps,), in_specs=[pl.BlockSpec((1, ro...  14.2 us
    pallas_call x1, Pallas kernels, mixed_and_states(): pl.pallas_call(states_kernel, grid=(width // GROUP,), in_specs=[stream(1)...  10.8 us
    unnamed x30, local copies, waits for them, and re-layouts  10.2 us
  transfers between devices with their start and end apart: 30, of which 14 were waited for; matrix products, arithmetic and copies ran while one was open for 15% of the time, Pallas kernels for 7%

profile of v2, /device:TPU:0, one launch (start us, length us, event | category | flops | bytes accessed | tf_op | source)
XLA Modules:
  0.0 332.3 jit_solution(5725756971701322226)
XLA Ops:
  4.3 3.0 fusion.8
  7.3 4.0 %collective-permute-start.5 = (bf16[4096,128]{1,0:T(8,128)(2,1)}, bf16[4096,128]{1,0:T(8,128)(2,1)}, u32[]{:S(2)}, u32[]{:S(2)}) collective-permute-start(bf16[4096,128]{1,0:T(8,128)(2,1)} %get-tuple-element.49), channel_id=1, source_target_pairs={{0,16},{2,18},{4,20},{6,22},{8,24},{10,26},{12,28},{14,30},{16,0},... | collective-permute-start | bytes 3145736 | tf_op jit(solution)/shard_map/ppermute | solution.py:20
  11.5 2.8 copy-done
  14.3 10.8 %mixed_and_states.1 = (bf16[256,4096]{1,0:T(8,128)(2,1)S(1)}, f32[16,32,128]{2,1,0:T(8,128)S(1)}) custom-call(bf16[3,256,4096]{2,1,0:T(8,128)(2,1)S(1)} %bitcast.79, bf16[3,256,4096]{2,1,0:T(8,128)(2,1)S(1)} %bitcast.80, f32[3,8,4096]{2,1,0:T(8,128)S(1)} %pad_convert_fusion.halo_ref, f32[9,4096]{1,0:T(8,128)S(1)} %reshape.13.taps_ref, ...), custom_call_target="tpu_custom_call" | custom-call | flops 1048576 | bytes 256 | tf_op jit(solution)/shard_map/mixed_and_states/pallas_call | solution.py:132
  31.4 28.1 %collective-permute-done.4 = f32[16,32,128]{2,1,0:T(8,128)S(1)} collective-permute-done((f32[16,32,128]{2,1,0:T(8,128)}, f32[16,32,128]{2,1,0:T(8,128)S(1)}, u32[]{:S(2)}, u32[]{:S(2)}) %collective-permute-start.4) | collective-permute-done | bytes 262176 | tf_op jit(solution)/shard_map/ppermute | solution.py:20
  59.6 4.9 %collective-permute-done.3 = f32[16,32,128]{2,1,0:T(8,128)} collective-permute-done((f32[16,32,128]{2,1,0:T(8,128)}, f32[16,32,128]{2,1,0:T(8,128)}, u32[]{:S(2)}, u32[]{:S(2)}) %collective-permute-start.3) | collective-permute-done | bytes 262176 | tf_op jit(solution)/shard_map/ppermute | solution.py:20
  67.3 3.0 slice.62
  71.3 9.8 %collective-permute-done.6 = f32[16,32,128]{2,1,0:T(8,128)} collective-permute-done((f32[16,32,128]{2,1,0:T(8,128)}, f32[16,32,128]{2,1,0:T(8,128)}, u32[]{:S(2)}, u32[]{:S(2)}) %collective-permute-start.6) | collective-permute-done | bytes 262176 | tf_op jit(solution)/shard_map/ppermute | solution.py:20
  82.5 2.8 copy-done.1
  85.3 6.7 %gated_rows.2.refs_0_ = bf16[256,2048]{1,0:T(8,128)(2,1)S(1)} custom-call(bf16[3,256,4096]{2,1,0:T(8,128)(2,1)S(1)} %bitcast.81, f32[3,8,4096]{2,1,0:T(8,128)S(1)} %pad_convert_fusion.halo_ref, f32[9,4096]{1,0:T(8,128)S(1)} %reshape.13.taps_ref, bf16[256,4096]{1,0:T(8,128)(2,1)S(1)} %get-tuple-element.25.mixed_ref, f32[1,4096]{1,0:T(1,128)S(1)} %bitcast.88, ...), custom_call_target="tpu_custom_call" | custom-call | flops 1048576 | bytes 256 | tf_op jit(solution)/shard_map/gated_rows/pallas_call | solution.py:162
  94.4 7.5 %gated_rows.3.refs_2_ = bf16[256,2048]{1,0:T(8,128)(2,1)} custom-call(bf16[3,256,4096]{2,1,0:T(8,128)(2,1)S(1)} %bitcast.82, f32[3,8,4096]{2,1,0:T(8,128)S(1)} %pad_convert_fusion.halo_ref, f32[9,4096]{1,0:T(8,128)S(1)} %reshape.13.taps_ref, bf16[256,4096]{1,0:T(8,128)(2,1)S(1)} %get-tuple-element.25.mixed_ref, f32[1,4096]{1,0:T(1,128)S(1)} %bitcast.89, ...), custom_call_target="tpu_custom_call" | custom-call | flops 1048576 | bytes 256 | tf_op jit(solution)/shard_map/gated_rows/pallas_call | solution.py:162
  103.9 14.3 %collective-permute-done.9.refs_1_ = bf16[256,2048]{1,0:T(8,128)(2,1)S(1)} collective-permute-done((bf16[256,2048]{1,0:T(8,128)(2,1)S(1)}, bf16[256,2048]{1,0:T(8,128)(2,1)S(1)}, u32[]{:S(2)}, u32[]{:S(2)}) %collective-permute-start.9) | collective-permute-done | bytes 1048608 | tf_op jit(solution)/shard_map/ppermute | solution.py:20
  119.2 20.5 %collective-permute-done.8.refs_0_ = bf16[256,2048]{1,0:T(8,128)(2,1)} collective-permute-done((bf16[256,2048]{1,0:T(8,128)(2,1)S(1)}, bf16[256,2048]{1,0:T(8,128)(2,1)}, u32[]{:S(2)}, u32[]{:S(2)}) %collective-permute-start.8) | collective-permute-done | bytes 1048608 | tf_op jit(solution)/shard_map/ppermute | solution.py:20
  141.7 67.7 %collective-permute-done.12 = bf16[4096,256]{1,0:T(8,128)(2,1)} collective-permute-done((bf16[4096,256]{1,0:T(8,128)(2,1)}, bf16[4096,256]{1,0:T(8,128)(2,1)}, u32[]{:S(2)}, u32[]{:S(2)}) %collective-permute-start.12) | collective-permute-done | bytes 2097184 | tf_op jit(solution)/shard_map/ppermute | solution.py:20
  211.9 2.8 joined.2
  214.8 3.0 convolution_convert_fusion.7
  220.0 2.3 convolution_convert_fusion.3
  222.3 4.5 %convolution_convert_fusion.2 = bf16[512,512]{1,0:T(8,128)(2,1)S(1)} fusion(bf16[512,4096]{1,0:T(8,128)(2,1)S(1)} %joined.2, bf16[4096,512]{1,0:T(8,128)(2,1)} %collective-permute-done.7), kind=kOutput, calls=%fused_computation.4 | convolution fusion | flops 2147745792 | bytes 8912896 | tf_op jit(solution)/shard_map/dot_general | solution.py:357
  226.9 2.5 convolution_convert_fusion.15
  232.2 11.4 %collective-permute-done.16.refs_3_ = bf16[256,2048]{1,0:T(8,128)(2,1)S(1)} collective-permute-done((bf16[256,2048]{1,0:T(8,128)(2,1)S(1)}, bf16[256,2048]{1,0:T(8,128)(2,1)S(1)}, u32[]{:S(2)}, u32[]{:S(2)}) %collective-permute-start.16) | collective-permute-done | bytes 1048608 | tf_op jit(solution)/shard_map/ppermute | solution.py:20
  245.7 4.5 %convolution_convert_fusion = bf16[512,512]{1,0:T(8,128)(2,1)S(1)} fusion(bf16[512,4096]{1,0:T(8,128)(2,1)S(1)} %joined.3, bf16[4096,512]{1,0:T(8,128)(2,1)} %collective-permute-done.7), kind=kOutput, calls=%fused_computation.2 | convolution fusion | flops 2147745792 | bytes 8912896 | tf_op jit(solution)/shard_map/dot_general | solution.py:357
  250.2 2.5 convolution_convert_fusion.12
  252.7 2.3 convolution_convert_fusion.1
  258.0 2.9 convolution_convert_fusion.5
  265.5 10.0 %collective-permute-done.17 = bf16[512,768]{1,0:T(8,128)(2,1)S(1)} collective-permute-done((bf16[512,768]{1,0:T(8,128)(2,1)S(1)}, bf16[512,768]{1,0:T(8,128)(2,1)S(1)}, u32[]{:S(2)}, u32[]{:S(2)}) %collective-permute-start.17) | collective-permute-done | bytes 786464 | tf_op jit(solution)/shard_map/ppermute | solution.py:20
  277.7 13.5 %collective-permute-done.23 = bf16[512,768]{1,0:T(8,128)(2,1)S(1)} collective-permute-done((bf16[512,768]{1,0:T(8,128)(2,1)S(1)}, bf16[512,768]{1,0:T(8,128)(2,1)S(1)}, u32[]{:S(2)}, u32[]{:S(2)}) %collective-permute-start.23) | collective-permute-done | bytes 786464 | tf_op jit(solution)/shard_map/ppermute | solution.py:20
  291.7 3.1 collective-permute-start.24
  300.0 4.6 %collective-permute-done.27 = bf16[256,768]{1,0:T(8,128)(2,1)S(1)} collective-permute-done((bf16[256,768]{1,0:T(8,128)(2,1)S(1)}, bf16[256,768]{1,0:T(8,128)(2,1)S(1)}, u32[]{:S(2)}, u32[]{:S(2)}) %collective-permute-start.27) | collective-permute-done | bytes 393248 | tf_op jit(solution)/shard_map/ppermute | solution.py:20
  304.6 6.4 %collective-permute-done.24 = bf16[256,768]{1,0:T(8,128)(2,1)S(1)} collective-permute-done((bf16[256,768]{1,0:T(8,128)(2,1)S(1)}, bf16[256,768]{1,0:T(8,128)(2,1)S(1)}, u32[]{:S(2)}, u32[]{:S(2)}) %collective-permute-start.24) | collective-permute-done | bytes 393248 | tf_op jit(solution)/shard_map/ppermute | solution.py:20
  315.0 3.7 %collective-permute-done.22 = bf16[256,256]{1,0:T(8,128)(2,1)S(1)} collective-permute-done((bf16[256,256]{1,0:T(8,128)(2,1)S(1)}, bf16[256,256]{1,0:T(8,128)(2,1)S(1)}, u32[]{:S(2)}, u32[]{:S(2)}) %collective-permute-start.22) | collective-permute-done | bytes 131104 | tf_op jit(solution)/shard_map/ppermute | solution.py:20
  319.0 6.0 %output_rows.1 = (bf16[256,4096]{1,0:T(8,128)(2,1)}, bf16[528,256]{1,0:T(8,128)(2,1)S(1)}) custom-call(s32[8]{0:T(128)S(1)} %iota_xor_fusion.order_ref, bf16[8,256,512]{2,1,0:T(8,128)(2,1)S(1)} %fusion.7.added_ref, bf16[256,4096]{1,0:T(8,128)(2,1)S(1)} %copy-done.5, f32[1,4096]{1,0:T(1,128)S(1)} %bitcast.90, bf16[512,4096]{1,0:T(8,128)(2,1)S(1)} %copy-done.2), custom_call_target="tpu_custom_call" | custom-call | flops 1073741824 | bytes 10485760 | tf_op jit(solution)/shard_map/output_rows/pallas_call | solution.py:250
  326.6 4.9 %collective-permute-done.29.second_ref = bf16[528,256]{1,0:T(8,128)(2,1)S(1)} collective-permute-done((bf16[528,256]{1,0:T(8,128)(2,1)S(1)}, bf16[528,256]{1,0:T(8,128)(2,1)S(1)}, u32[]{:S(2)}, u32[]{:S(2)}) %collective-permute-start.29) | collective-permute-done | bytes 270368 | tf_op jit(solution)/shard_map/ppermute | solution.py:20
  (126 shorter events, 54.2 us)
Async XLA Ops:
  0.6 81.8 %collective-permute-start.7 = (bf16[4096,512]{1,0:T(8,128)(2,1)}, bf16[4096,512]{1,0:T(8,128)(2,1)}, u32[]{:S(2)}, u32[]{:S(2)}) collective-permute-start(bf16[4096,512]{1,0:T(8,128)(2,1)} %param.16), channel_id=1, source_target_pairs={{0,2},{2,0},{4,6},{6,4},{8,10},{10,8},{12,14},{14,12},{16,18},{18,... | collective-permute-start | bytes 12582920 | tf_op jit(solution)/shard_map/ppermute | solution.py:20
  2.2 9.3 %collective-permute-start = (bf16[2,3,4096]{2,0,1:T(2,128)(2,1)S(1)}, bf16[2,3,4096]{2,0,1:T(2,128)(2,1)S(1)}, u32[]{:S(2)}, u32[]{:S(2)}) collective-permute-start(bf16[2,3,4096]{2,0,1:T(2,128)(2,1)S(1)} %slice.60), channel_id=1, source_target_pairs={{0,2},{2,4},{4,6},{6,8},{8,10},{10,12},{12,14},{14,16},{16,18},{18... | collective-permute-start | bytes 147464 | tf_op jit(solution)/shard_map/ppermute | solution.py:26
  7.3 59.2 %collective-permute-start.5 = (bf16[4096,128]{1,0:T(8,128)(2,1)}, bf16[4096,128]{1,0:T(8,128)(2,1)}, u32[]{:S(2)}, u32[]{:S(2)}) collective-permute-start(bf16[4096,128]{1,0:T(8,128)(2,1)} %get-tuple-element.49), channel_id=1, source_target_pairs={{0,16},{2,18},{4,20},{6,22},{8,24},{10,26},{12,28},{14,30},{16,0},... | collective-permute-start | bytes 3145736 | tf_op jit(solution)/shard_map/ppermute | solution.py:20
  25.1 2.1 collective-permute-start.1
  27.9 31.6 %collective-permute-start.4 = (f32[16,32,128]{2,1,0:T(8,128)}, f32[16,32,128]{2,1,0:T(8,128)S(1)}, u32[]{:S(2)}, u32[]{:S(2)}) collective-permute-start(f32[16,32,128]{2,1,0:T(8,128)} %multiply_add_fusion.1), channel_id=1, source_target_pairs={{0,12},{2,14},{4,8},{6,10},{8,4},{10,6},{12,0},{14,2},{16,28},{18,... | collective-permute-start | bytes 786440 | tf_op jit(solution)/shard_map/ppermute | solution.py:20
  30.0 34.5 %collective-permute-start.3 = (f32[16,32,128]{2,1,0:T(8,128)}, f32[16,32,128]{2,1,0:T(8,128)}, u32[]{:S(2)}, u32[]{:S(2)}) collective-permute-start(f32[16,32,128]{2,1,0:T(8,128)} %multiply_add_fusion.1), channel_id=1, source_target_pairs={{0,8},{2,10},{4,12},{6,14},{8,0},{10,2},{12,4},{14,6},{16,24},{18,... | collective-permute-start | bytes 786440 | tf_op jit(solution)/shard_map/ppermute | solution.py:20
  31.0 33.5 %collective-permute-start.2 = (f32[16,32,128]{2,1,0:T(8,128)}, f32[16,32,128]{2,1,0:T(8,128)}, u32[]{:S(2)}, u32[]{:S(2)}) collective-permute-start(f32[16,32,128]{2,1,0:T(8,128)} %multiply_add_fusion.1), channel_id=1, source_target_pairs={{0,4},{2,6},{4,0},{6,2},{8,12},{10,14},{12,8},{14,10},{16,20},{18,... | collective-permute-start | bytes 786440 | tf_op jit(solution)/shard_map/ppermute | solution.py:20
  66.5 14.6 %collective-permute-start.6 = (f32[16,32,128]{2,1,0:T(8,128)}, f32[16,32,128]{2,1,0:T(8,128)}, u32[]{:S(2)}, u32[]{:S(2)}) collective-permute-start(f32[16,32,128]{2,1,0:T(8,128)} %multiply_add_fusion), channel_id=1, source_target_pairs={{0,16},{2,18},{4,20},{6,22},{8,24},{10,26},{12,28},{14,30},{16,0},... | collective-permute-start | bytes 786440 | tf_op jit(solution)/shard_map/ppermute | solution.py:20
  70.3 12.2 %copy-start.8 = (f32[4096]{0:T(1024)S(1)}, f32[4096]{0:T(1024)}, u32[]{:S(2)}) copy-start(f32[4096]{0:T(1024)} %param.15) | copy-start | bytes 49156
  92.0 26.1 %collective-permute-start.9 = (bf16[256,2048]{1,0:T(8,128)(2,1)S(1)}, bf16[256,2048]{1,0:T(8,128)(2,1)S(1)}, u32[]{:S(2)}, u32[]{:S(2)}) collective-permute-start(bf16[256,2048]{1,0:T(8,128)(2,1)S(1)} %gated_rows.2.refs_0_), channel_id=1, source_target_pairs={{0,4},{2,6},{4,0},{6,2},{8,12},{10,14},{12,8},{14,10},{16,20},{18,... | collective-permute-start | bytes 3145736 | tf_op jit(solution)/shard_map/ppermute | solution.py:20
  92.1 47.5 %collective-permute-start.8 = (bf16[256,2048]{1,0:T(8,128)(2,1)S(1)}, bf16[256,2048]{1,0:T(8,128)(2,1)}, u32[]{:S(2)}, u32[]{:S(2)}) collective-permute-start(bf16[256,2048]{1,0:T(8,128)(2,1)S(1)} %gated_rows.2.refs_0_), channel_id=1, source_target_pairs={{0,8},{2,10},{4,12},{6,14},{8,0},{10,2},{12,4},{14,6},{16,24},{18,... | collective-permute-start | bytes 3145736 | tf_op jit(solution)/shard_map/ppermute | solution.py:20
  92.2 117.2 %collective-permute-start.12 = (bf16[4096,256]{1,0:T(8,128)(2,1)}, bf16[4096,256]{1,0:T(8,128)(2,1)}, u32[]{:S(2)}, u32[]{:S(2)}) collective-permute-start(bf16[4096,256]{1,0:T(8,128)(2,1)} %slice.62), channel_id=1, source_target_pairs={{0,16},{2,18},{4,20},{6,22},{8,24},{10,26},{12,28},{14,30},{16,0},... | collective-permute-start | bytes 6291464 | tf_op jit(solution)/shard_map/ppermute | solution.py:20
  101.9 107.5 %collective-permute-start.11 = (bf16[256,2048]{1,0:T(8,128)(2,1)}, bf16[256,2048]{1,0:T(8,128)(2,1)S(1)}, u32[]{:S(2)}, u32[]{:S(2)}) collective-permute-start(bf16[256,2048]{1,0:T(8,128)(2,1)} %gated_rows.3.refs_2_), channel_id=1, source_target_pairs={{0,4},{2,6},{4,0},{6,2},{8,12},{10,14},{12,8},{14,10},{16,20},{18,... | collective-permute-start | bytes 3145736 | tf_op jit(solution)/shard_map/ppermute | solution.py:20
  103.8 105.5 %collective-permute-start.10 = (bf16[256,2048]{1,0:T(8,128)(2,1)}, bf16[256,2048]{1,0:T(8,128)(2,1)S(1)}, u32[]{:S(2)}, u32[]{:S(2)}) collective-permute-start(bf16[256,2048]{1,0:T(8,128)(2,1)} %gated_rows.3.refs_2_), channel_id=1, source_target_pairs={{0,8},{2,10},{4,12},{6,14},{8,0},{10,2},{12,4},{14,6},{16,24},{18,... | collective-permute-start | bytes 3145736 | tf_op jit(solution)/shard_map/ppermute | solution.py:20
  139.7 69.7 %collective-permute-start.13 = (bf16[256,2048]{1,0:T(8,128)(2,1)}, bf16[256,2048]{1,0:T(8,128)(2,1)S(1)}, u32[]{:S(2)}, u32[]{:S(2)}) collective-permute-start(bf16[256,2048]{1,0:T(8,128)(2,1)} %collective-permute-done.8.refs_0_), channel_id=1, source_target_pairs={{0,4},{2,6},{4,0},{6,2},{8,12},{10,14},{12,8},{14,10},{16,20},{18,... | collective-permute-start | bytes 3145736 | tf_op jit(solution)/shard_map/ppermute | solution.py:20
  141.6 121.2 %collective-permute-start.18 = (bf16[4096,128]{1,0:T(8,128)(2,1)}, bf16[4096,128]{1,0:T(8,128)(2,1)S(1)}, u32[]{:S(2)}, u32[]{:S(2)}) collective-permute-start(bf16[4096,128]{1,0:T(8,128)(2,1)} %get-tuple-element.42), channel_id=1, source_target_pairs={{0,16},{2,18},{4,20},{6,22},{8,24},{10,26},{12,28},{14,30},{16,0},... | collective-permute-start | bytes 3145736 | tf_op jit(solution)/shard_map/ppermute | solution.py:20
  209.4 21.3 %collective-permute-start.15 = (bf16[4096,256]{1,0:T(8,128)(2,1)}, bf16[4096,256]{1,0:T(8,128)(2,1)S(1)}, u32[]{:S(2)}, u32[]{:S(2)}) collective-permute-start(bf16[4096,256]{1,0:T(8,128)(2,1)} %collective-permute-done.12), channel_id=1, source_target_pairs={{0,2},{2,0},{4,6},{6,4},{8,10},{10,8},{12,14},{14,12},{16,18},{18,... | collective-permute-start | bytes 6291464 | tf_op jit(solution)/shard_map/ppermute | solution.py:20
  217.8 25.8 %collective-permute-start.16 = (bf16[256,2048]{1,0:T(8,128)(2,1)S(1)}, bf16[256,2048]{1,0:T(8,128)(2,1)S(1)}, u32[]{:S(2)}, u32[]{:S(2)}) collective-permute-start(bf16[256,2048]{1,0:T(8,128)(2,1)S(1)} %collective-permute-done.10.refs_2_), channel_id=1, source_target_pairs={{0,4},{2,6},{4,0},{6,2},{8,12},{10,14},{12,8},{14,10},{16,20},{18,... | collective-permute-start | bytes 3145736 | tf_op jit(solution)/shard_map/ppermute | solution.py:20
  219.8 9.7 %collective-permute-start.14 = (bf16[4096,128]{1,0:T(8,128)(2,1)}, bf16[4096,128]{1,0:T(8,128)(2,1)S(1)}, u32[]{:S(2)}, u32[]{:S(2)}) collective-permute-start(bf16[4096,128]{1,0:T(8,128)(2,1)} %collective-permute-done.5), channel_id=1, source_target_pairs={{0,2},{2,0},{4,6},{6,4},{8,10},{10,8},{12,14},{14,12},{16,18},{18,... | collective-permute-start | bytes 3145736 | tf_op jit(solution)/shard_map/ppermute | solution.py:20
  255.0 20.5 %collective-permute-start.17 = (bf16[512,768]{1,0:T(8,128)(2,1)S(1)}, bf16[512,768]{1,0:T(8,128)(2,1)S(1)}, u32[]{:S(2)}, u32[]{:S(2)}) collective-permute-start(bf16[512,768]{1,0:T(8,128)(2,1)S(1)} %broadcast_select_fusion.1), channel_id=1, source_target_pairs={{0,1},{1,0},{2,3},{3,2},{4,5},{5,4},{6,7},{7,6},{8,9},{9,8},{10,11... | collective-permute-start | bytes 2359304 | tf_op jit(solution)/shard_map/ppermute | solution.py:20
  262.3 28.9 %collective-permute-start.23 = (bf16[512,768]{1,0:T(8,128)(2,1)S(1)}, bf16[512,768]{1,0:T(8,128)(2,1)S(1)}, u32[]{:S(2)}, u32[]{:S(2)}) collective-permute-start(bf16[512,768]{1,0:T(8,128)(2,1)S(1)} %broadcast_select_fusion), channel_id=1, source_target_pairs={{0,1},{1,0},{2,3},{3,2},{4,5},{5,4},{6,7},{7,6},{8,9},{9,8},{10,11... | collective-permute-start | bytes 2359304 | tf_op jit(solution)/shard_map/ppermute | solution.py:20
  264.2 30.6 %collective-permute-start.19 = (bf16[4096,128]{1,0:T(8,128)(2,1)S(1)}, bf16[4096,128]{1,0:T(8,128)(2,1)S(1)}, u32[]{:S(2)}, u32[]{:S(2)}) collective-permute-start(bf16[4096,128]{1,0:T(8,128)(2,1)S(1)} %collective-permute-done.18), channel_id=1, source_target_pairs={{0,2},{2,0},{4,6},{6,4},{8,10},{10,8},{12,14},{14,12},{16,18},{18,... | collective-permute-start | bytes 3145736 | tf_op jit(solution)/shard_map/ppermute | solution.py:20
  275.9 24.0 %collective-permute-start.21 = (bf16[256,768]{1,0:T(8,128)(2,1)S(1)}, bf16[256,768]{1,0:T(8,128)(2,1)S(1)}, u32[]{:S(2)}, u32[]{:S(2)}) collective-permute-start(bf16[256,768]{1,0:T(8,128)(2,1)S(1)} %slice.82), channel_id=1, source_target_pairs={{0,4},{2,6},{4,0},{6,2},{8,12},{10,14},{12,8},{14,10},{16,20},{18,... | collective-permute-start | bytes 1179656 | tf_op jit(solution)/shard_map/ppermute | solution.py:20
  291.6 13.0 %collective-permute-start.27 = (bf16[256,768]{1,0:T(8,128)(2,1)S(1)}, bf16[256,768]{1,0:T(8,128)(2,1)S(1)}, u32[]{:S(2)}, u32[]{:S(2)}) collective-permute-start(bf16[256,768]{1,0:T(8,128)(2,1)S(1)} %get-tuple-element.50), channel_id=1, source_target_pairs={{0,12},{2,14},{4,8},{6,10},{8,4},{10,6},{12,0},{14,2},{16,28},{18,... | collective-permute-start | bytes 1179656 | tf_op jit(solution)/shard_map/ppermute | solution.py:20
  291.7 19.3 %collective-permute-start.24 = (bf16[256,768]{1,0:T(8,128)(2,1)S(1)}, bf16[256,768]{1,0:T(8,128)(2,1)S(1)}, u32[]{:S(2)}, u32[]{:S(2)}) collective-permute-start(bf16[256,768]{1,0:T(8,128)(2,1)S(1)} %get-tuple-element.51), channel_id=1, source_target_pairs={{0,8},{2,10},{4,12},{6,14},{8,0},{10,2},{12,4},{14,6},{16,24},{18,... | collective-permute-start | bytes 1179656 | tf_op jit(solution)/shard_map/ppermute | solution.py:20
  296.1 15.1 %collective-permute-start.25 = (bf16[512,256]{1,0:T(8,128)(2,1)S(1)}, bf16[512,256]{1,0:T(8,128)(2,1)S(1)}, u32[]{:S(2)}, u32[]{:S(2)}) collective-permute-start(bf16[512,256]{1,0:T(8,128)(2,1)S(1)} %broadcast_select_fusion.2), channel_id=1, source_target_pairs={{0,1},{1,0},{2,3},{3,2},{4,5},{5,4},{6,7},{7,6},{8,9},{9,8},{10,11... | collective-permute-start | bytes 786440 | tf_op jit(solution)/shard_map/ppermute | solution.py:20
  299.4 11.6 %collective-permute-start.20 = (bf16[512,256]{1,0:T(8,128)(2,1)S(1)}, bf16[512,256]{1,0:T(8,128)(2,1)S(1)}, u32[]{:S(2)}, u32[]{:S(2)}) collective-permute-start(bf16[512,256]{1,0:T(8,128)(2,1)S(1)} %broadcast_select_fusion.3), channel_id=1, source_target_pairs={{0,1},{1,0},{2,3},{3,2},{4,5},{5,4},{6,7},{7,6},{8,9},{9,8},{10,11... | collective-permute-start | bytes 786440 | tf_op jit(solution)/shard_map/ppermute | solution.py:20
  311.4 7.5 %collective-permute-start.28 = (bf16[256,256]{1,0:T(8,128)(2,1)S(1)}, bf16[256,256]{1,0:T(8,128)(2,1)S(1)}, u32[]{:S(2)}, u32[]{:S(2)}) collective-permute-start(bf16[256,256]{1,0:T(8,128)(2,1)S(1)} %get-tuple-element.60), channel_id=1, source_target_pairs={{0,12},{2,14},{4,8},{6,10},{8,4},{10,6},{12,0},{14,2},{16,28},{18,... | collective-permute-start | bytes 393224 | tf_op jit(solution)/shard_map/ppermute | solution.py:20
  311.7 7.1 %collective-permute-start.26 = (bf16[256,256]{1,0:T(8,128)(2,1)S(1)}, bf16[256,256]{1,0:T(8,128)(2,1)S(1)}, u32[]{:S(2)}, u32[]{:S(2)}) collective-permute-start(bf16[256,256]{1,0:T(8,128)(2,1)S(1)} %get-tuple-element.61), channel_id=1, source_target_pairs={{0,8},{2,10},{4,12},{6,14},{8,0},{10,2},{12,4},{14,6},{16,24},{18,... | collective-permute-start | bytes 393224 | tf_op jit(solution)/shard_map/ppermute | solution.py:20
  313.4 5.3 %collective-permute-start.22 = (bf16[256,256]{1,0:T(8,128)(2,1)S(1)}, bf16[256,256]{1,0:T(8,128)(2,1)S(1)}, u32[]{:S(2)}, u32[]{:S(2)}) collective-permute-start(bf16[256,256]{1,0:T(8,128)(2,1)S(1)} %slice.83), channel_id=1, source_target_pairs={{0,4},{2,6},{4,0},{6,2},{8,12},{10,14},{12,8},{14,10},{16,20},{18,... | collective-permute-start | bytes 393224 | tf_op jit(solution)/shard_map/ppermute | solution.py:20
  319.0 12.4 %copy-start.10 = (s32[256]{0:T(256)S(1)}, s32[256]{0:T(256)}, u32[]{:S(2)}) copy-start(s32[256]{0:T(256)} %param.19) | copy-start | bytes 3076
  325.0 6.5 %collective-permute-start.29 = (bf16[528,256]{1,0:T(8,128)(2,1)S(1)}, bf16[528,256]{1,0:T(8,128)(2,1)S(1)}, u32[]{:S(2)}, u32[]{:S(2)}) collective-permute-start(bf16[528,256]{1,0:T(8,128)(2,1)S(1)} %get-tuple-element.47.first_ref), channel_id=1, source_target_pairs={{0,1},{1,0},{2,3},{3,2},{4,5},{5,4},{6,7},{7,6},{8,9},{9,8},{10,11... | collective-permute-start | bytes 811016 | tf_op jit(solution)/shard_map/ppermute | solution.py:20
  (12 other events, 58.4 us)

commit v3 on v1

--- a/solution.py
+++ b/solution.py
@@ -155,25 +155,25 @@
     )(streams, streams, halo, taps, rates)
 
 
-def gated_rows(streams, halo, taps, mixed, skip, rates, residues, entering, base, steps):
+def gated_rows(streams, halo, taps, mixed, skip, rates, residues, entering):
     rows, width = mixed.shape
     modes = rates.shape[0]
-    modal = pl.BlockSpec((modes, SUBLANES, LANES), lambda g: (0, base + g, 0))
+    modal = pl.BlockSpec((modes, SUBLANES, LANES), lambda g: (0, g, 0))
     return pl.pallas_call(
         gated_kernel,
-        grid=(steps,),
+        grid=(width // GROUP,),
         in_specs=[
-            pl.BlockSpec((1, rows, GROUP), lambda g: (0, 0, base + g)),
-            pl.BlockSpec((3, SUBLANES, GROUP), lambda g: (0, 0, base + g)),
-            pl.BlockSpec((taps.shape[0], GROUP), lambda g: (0, base + g)),
-            pl.BlockSpec((rows, GROUP), lambda g: (0, base + g)),
-            pl.BlockSpec((1, GROUP), lambda g: (0, base + g)),
+            pl.BlockSpec((1, rows, GROUP), lambda g: (0, 0, g)),
+            pl.BlockSpec((3, SUBLANES, GROUP), lambda g: (0, 0, g)),
+            pl.BlockSpec((taps.shape[0], GROUP), lambda g: (0, g)),
+            pl.BlockSpec((rows, GROUP), lambda g: (0, g)),
+            pl.BlockSpec((1, GROUP), lambda g: (0, g)),
             modal,
             modal,
             modal,
         ],
         out_specs=pl.BlockSpec((rows, GROUP), lambda g: (0, g)),
-        out_shape=jax.ShapeDtypeStruct((rows, steps * GROUP), BF16),
+        out_shape=jax.ShapeDtypeStruct((rows, width), BF16),
         scratch_shapes=[
             pltpu.VMEM((rows + SUBLANES, GROUP), F32),
             pltpu.VMEM((rows // SUBLANES, SUBLANES * SUBLANES, LANES), F32),
@@ -185,18 +185,16 @@
     )(streams, halo, taps, mixed, skip, rates, residues, entering)
 
 
-def entering_states(end, rates, rows, merges, before_last=()):
+def entering_states(end, rates, rows, merges, before=None):
     place = lax.axis_index("seq")
     total, entering = end, jnp.zeros_like(end)
     held = []
     for bits in merges:
         span, count = 1 << bits[0], 1 << len(bits)
-        last = bits == merges[-1]
-        if last and before_last:
-            total, *held = tied(total, *before_last)
-        extra = span >> 1 if last and count == 2 else 0
+        if before and bits in before:
+            total, *held = tied(total, *before[bits])
         others = [
-            (mask, xor_permute(total, "seq", (mask * span) | extra)) for mask in range(1, count)
+            (mask, xor_permute(total, "seq", mask * span)) for mask in range(1, count)
         ]
         own = (place // span) % count
         inside = (place % span) * rows
@@ -316,98 +314,77 @@
     return total, xor_permute(total, "chan", span)
 
 
-def placed_pairs(count, chans, per_chan, same, seq_mask, chan_mask):
+def tied(*values):
+    return lax.optimization_barrier(values)
+
+
+def column_pieces(weight, cuts):
+    return [lax.slice_in_dim(weight, first, last, axis=1) for first, last in itertools.pairwise(cuts)]
+
+
+def product(rows, weight):
+    return jnp.dot(rows, weight, preferred_element_type=F32).astype(BF16)
+
+
+def added_up(kept, other):
+    return (kept.astype(F32) + other.astype(F32)).astype(BF16)
+
+
+def placed_permute(value, same, seq_mask, chan_mask):
+    count, chans = lax.axis_size("seq"), lax.axis_size("chan")
     pairs = []
     for place, chan in itertools.product(range(count), range(chans)):
-        if (place // per_chan == chan) == same:
+        if (place // (count // chans) == chan) == same:
             target = (place ^ seq_mask) * chans + (chan ^ chan_mask)
             pairs.append((place * chans + chan, target))
-    return pairs
-
-
-def tied(*values):
-    return lax.optimization_barrier(values)
-
-
-def far_pieces(out_weight, cuts):
-    return [
-        lax.slice_in_dim(out_weight, first, last, axis=1)
-        for first, last in itertools.pairwise(cuts)
-    ]
-
-
-def joined(*rows):
-    return tied(jnp.concatenate([jnp.concatenate(parts, axis=1) for parts in rows], axis=0))[0]
-
-
-def product(rows, *weights):
-    outs = [jnp.dot(rows, weight, preferred_element_type=F32).astype(BF16) for weight in weights]
-    return outs[0] if len(outs) == 1 else jnp.concatenate(outs, axis=1)
+    return lax.ppermute(value, ("seq", "chan"), pairs)
 
 
 def projected_fast(gated, out_weight, core_weight, far):
     count, chans = lax.axis_size("seq"), lax.axis_size("chan")
     per_chan = count // chans
-    rows, block = gated[0].shape[0], out_weight.shape[1]
-    core, side, low = 1, 2, 4
-
-    below = [xor_permute(part, "seq", low) for part in gated]
-    beside = [xor_permute(gated[0], "seq", side)]
-    later, far[1] = tied(gated[1], far[1])
-    beside.append(xor_permute(later, "seq", side))
-    below[0], beside[1] = tied(below[0], beside[1])
-    across = [xor_permute(below[0], "seq", side)]
-    beside[0], far[2], far[0] = tied(beside[0], far[2], far[0])
-    first = joined(gated, beside)
-    near_first = product(first, out_weight, core_weight)
-    below[1], across[0], waiting = tied(below[1], across[0], far[3])
-    far[3] = xor_permute(waiting, "seq", per_chan)
-    across.append(xor_permute(below[1], "seq", side))
-    second = joined(below, across)
-
-    def reduced(partial, masks, same, after=None):
-        pairs = placed_pairs(count, chans, per_chan, not same, 0, 1)
-        other = lax.ppermute(partial, ("seq", "chan"), pairs)
-        if after is not None:
-            other, _ = tied(other, after)
-        total = (partial.astype(F32) + other.astype(F32)).astype(BF16)
-        back = []
-        for at, mask in enumerate(masks):
-            mine = total[at * rows : (at + 1) * rows]
-            if mask:
-                pairs = placed_pairs(count, chans, per_chan, same, mask, 0)
-                mine = lax.ppermute(mine, ("seq", "chan"), pairs)
-            back.append(mine)
-        return back
-
-    far_core = [xor_permute(piece, "seq", core) for piece in far[:-1]]
-    near_back = reduced(near_first, (0, side), True)
-    early = jnp.concatenate(far[:-1] + far_core, axis=1)
-    early_first = product(first, early)
-    near_second = product(second, out_weight, core_weight)
-    early_second = product(second, early)
-    last, *_ = tied(far[-1], early_second, near_second)
-    last_core = xor_permute(last, "seq", core)
-    last = jnp.concatenate([last, last_core], axis=1)
-    last_all = jnp.concatenate([product(first, last), product(second, last)], axis=0)
-    near_back += reduced(near_second, (low, low | side), True, last_all)
-    early_back = reduced(early_first, (0, side), False)
-    early_back += reduced(early_second, (low, low | side), False, last_all)
-    last_back = reduced(last_all, (0, side, low, low | side), False)
+    rows, block = gated.shape[0], out_weight.shape[1]
+    core, side, low, top = 1, 2, 4, per_chan
     here = lax.axis_index("seq") // per_chan == lax.axis_index("chan")
-    cut = block - last_core.shape[1]
+    part = rows // 2
+
+    halves = [gated[:part], gated[part:]]
+    above = [xor_permute(half, "seq", top) for half in halves]
+    beside = xor_permute(gated, "seq", side)
+    across = [xor_permute(above[0], "seq", side)]
+    near = jnp.concatenate([out_weight, core_weight], axis=1)
+    first = tied(jnp.concatenate([gated, beside], axis=0))[0]
+    near_first = product(first, near)
+    second = [tied(jnp.concatenate([above[0], across[0]], axis=0))[0]]
+    near_second = [product(second[0], near)]
+    above[1], far[1], _, _ = tied(above[1], far[1], near_first, near_second[0])
+    across.append(xor_permute(above[1], "seq", side))
+    far_all = jnp.concatenate(far + [xor_permute(piece, "seq", core) for piece in far], axis=1)
+    second.append(tied(jnp.concatenate([above[1], across[1]], axis=0))[0])
+    near_second.append(product(second[1], near))
+
+    def first_sums(partial):
+        total = added_up(partial, placed_permute(partial, False, 0, 1))
+        return total[:rows], placed_permute(total[rows:], True, side, 0)
+
+    def second_sums(close, distant):
+        other = xor_permute(jnp.where(here, distant, close), "chan", 1)
+        total = added_up(jnp.where(here, close, distant), other)
+        back = [xor_permute(total[:part], "seq", top), xor_permute(total[part:], "seq", top | side)]
+        hop = placed_permute(jnp.concatenate(back, axis=1), True, 0, 1)
+        return back, jnp.split(hop, 2, axis=1)
+
+    far_second = [product(rows_all, far_all) for rows_all in second]
+    sums = [second_sums(*pair) for pair in zip(near_second, far_second)]
+    near_sums = first_sums(near_first)
+    far_sums = first_sums(product(first, far_all))
     blocks = {}
-    for at, mask in enumerate((0, side, low, low | side)):
-        for half in range(2):
-            near_block = near_back[at][:, half * block : (half + 1) * block]
-            late_block = jnp.concatenate(
-                [
-                    early_back[at][:, half * cut : (half + 1) * cut],
-                    last_back[at][:, half * (block - cut) : (half + 1) * (block - cut)],
-                ],
-                axis=1,
-            )
-            blocks[mask | (half * core)] = jnp.where(here, near_block, late_block)
+    for half, mask in itertools.product(range(2), (0, side)):
+        span = slice(half * block, (half + 1) * block)
+        at = mask // side
+        for extra, own, moved in ((0, near_sums, 0), (low, far_sums, 1)):
+            late = jnp.concatenate([pair[moved][at][:, span] for pair in sums], axis=0)
+            blocks[mask | extra | (half * core)] = jnp.where(here, own[at][:, span], late)
     added = jnp.stack([blocks[mask] for mask in range(per_chan)])
     order = jnp.arange(per_chan, dtype=jnp.int32) ^ (lax.axis_index("seq") % per_chan)
     return added, order
@@ -455,41 +432,26 @@
     top = count // chans
     if fast:
         block = out_weight.shape[1]
-        far = far_pieces(out_weight, range(0, block + 1, block // 4))
-        far = [xor_permute(piece, "seq", top) for piece in far[:3]] + far[3:]
+        low = top // 2
+        far = column_pieces(out_weight, (0, block // 4, block))
+        far[0] = xor_permute(far[0], "seq", low)
         core_weight = xor_permute(out_weight, "seq", 1)
 
     mixed, end = mixed_and_states(streams, halo, taps, rates)
     bits = range(count.bit_length() - 1)
-    merges = [(0,), (1, 2), (3,)] if fast else [(bit,) for bit in bits]
-    entering, held = entering_states(end, rates, rows, merges, far[:1] if fast else ())
+    merges = [(bit,) for bit in bits]
+    before = {(2,): far[:1]} if fast else None
+    entering, held = entering_states(end, rates, rows, merges, before)
     if fast:
-        far = held + far[1:]
+        entering, *waiting = tied(entering, *far[1:])
+        far = held + [xor_permute(piece, "seq", low) for piece in waiting]
     if fast:
         entering, core_weight = tied(entering, core_weight)
-    groups = width // GROUP
-    edges = (0, groups // 2, groups) if fast else (0, groups)
-    gated = []
-    for base, stop in itertools.pairwise(edges):
-        gated.append(
-            gated_rows(
-                streams,
-                halo,
-                taps,
-                mixed,
-                skip_gain[None, :],
-                rates,
-                weights,
-                entering,
-                base,
-                stop - base,
-            )
-        )
-        entering, _ = tied(entering, gated[-1])
+    gated = gated_rows(streams, halo, taps, mixed, skip_gain[None, :], rates, weights, entering)
     if fast:
         added, order = projected_fast(gated, out_weight, core_weight, far)
     else:
-        added, order = projected_plain(gated[0], out_weight)
+        added, order = projected_plain(gated, out_weight)
     block_out, packed = output_rows(order, added, residual_in, final_gain[None, :], embedding)
     first, second = summed_over_chan(packed)
     return block_out, log_likelihood(first, second, next_ids, float(width * chans))

time: 361 us -> 329 us (0.911)
  starting transfers between devices: 127 us -> 42.3 us
  waiting for transfers between devices: 131 us -> 196 us
  other arithmetic: 26.2 us -> 7.24 us
  local copies, waits for them, and re-layouts: 18.9 us -> 31.4 us
  matrix products: 23.5 us -> 19.3 us
    ppermute x21, waiting for transfers between devices: 104 us -> 183 us  [xor_permute(): lax.ppermute(value, axis, [(source, source ^ mask) for source in range(co...]
    ppermute x21, starting transfers between devices: 87 us -> 24.3 us  [xor_permute(): lax.ppermute(value, axis, [(source, source ^ mask) for source in range(co...]
    ppermute x14 -> x6, starting transfers between devices: 37.5 us -> 16 us  [placed_permute(): return lax.ppermute(value, ('seq', 'chan'), pairs)]
    concatenate x5, other arithmetic: 18.2 us -> 0.97 us  [the longest x1 0.49 us: projected_fast(): first = tied(jnp.concatenate([gated, beside], axis=0))[0]]
    ppermute x14 -> x6, waiting for transfers between devices: 26.2 us -> 13 us  [placed_permute(): return lax.ppermute(value, ('seq', 'chan'), pairs)]
    concatenate x2, local copies, waits for them, and re-layouts: 0.5 us -> 5.93 us  [the longest x1 3.12 us: projected_fast(): near = jnp.concatenate([out_weight, core_weight], axis=1)]
    unnamed x42 -> x38, local copies, waits for them, and re-layouts: 12.6 us -> 16.9 us
    dot_general x8 -> x6, matrix products: 23.5 us -> 19.3 us  [product(): return jnp.dot(rows, weight, preferred_element_type=F32).astype(BF16)]
  transfers between devices with their start and end apart: 36 -> 28, of which waited for: 14 -> 15; matrix products, arithmetic and copies ran while one was open for 17% -> 15% of each run, Pallas kernels for 7% -> 3%
where the time goes in v3:
time: 329 us; the launch traced here: 328 us
  waiting for transfers between devices  196 us (60%)
  starting transfers between devices  42.3 us (13%)
  local copies, waits for them, and re-layouts  31.4 us (10%)
  Pallas kernels  31 us (9%)
  matrix products  19.3 us (6%)
  other arithmetic  7.24 us (2%)
    ppermute x21, waiting for transfers between devices, xor_permute(): lax.ppermute(value, axis, [(source, source ^ mask) for source in range(co...  183 us
    ppermute x21, starting transfers between devices, xor_permute(): lax.ppermute(value, axis, [(source, source ^ mask) for source in range(co...  24.3 us
    dot_general x6, matrix products, product(): return jnp.dot(rows, weight, preferred_element_type=F32).astype(BF16)  19.3 us
    unnamed x38, local copies, waits for them, and re-layouts  16.9 us
    ppermute x6, starting transfers between devices, placed_permute(): return lax.ppermute(value, ('seq', 'chan'), pairs)  16 us
    pallas_call x1, Pallas kernels, gated_rows(): pl.pallas_call(gated_kernel, grid=(width // GROUP,), in_specs=[pl.BlockSp...  13.4 us
    ppermute x6, waiting for transfers between devices, placed_permute(): return lax.ppermute(value, ('seq', 'chan'), pairs)  13 us
    pallas_call x1, Pallas kernels, mixed_and_states(): pl.pallas_call(states_kernel, grid=(width // GROUP,), in_specs=[stream(1)...  10.8 us
  transfers between devices with their start and end apart: 28, of which 15 were waited for; matrix products, arithmetic and copies ran while one was open for 15% of the time, Pallas kernels for 3%

profile of v3, /device:TPU:0, one launch (start us, length us, event | category | flops | bytes accessed | tf_op | source)
XLA Modules:
  0.0 328.4 jit_solution(17165078366232021340)
XLA Ops:
  6.4 3.0 collective-permute-start.3
  11.5 2.8 copy-done
  14.3 10.8 %mixed_and_states.1 = (bf16[256,4096]{1,0:T(8,128)(2,1)S(1)}, f32[16,32,128]{2,1,0:T(8,128)S(1)}) custom-call(bf16[3,256,4096]{2,1,0:T(8,128)(2,1)S(1)} %bitcast.60, bf16[3,256,4096]{2,1,0:T(8,128)(2,1)S(1)} %bitcast.61, f32[3,8,4096]{2,1,0:T(8,128)S(1)} %pad_convert_fusion.halo_ref, f32[9,4096]{1,0:T(8,128)S(1)} %reshape.13.taps_ref, ...), custom_call_target="tpu_custom_call" | custom-call | flops 1048576 | bytes 256 | tf_op jit(solution)/shard_map/mixed_and_states/pallas_call | solution.py:132
  29.9 7.1 %collective-permute-done.2 = f32[16,32,128]{2,1,0:T(8,128)} collective-permute-done((f32[16,32,128]{2,1,0:T(8,128)S(1)}, f32[16,32,128]{2,1,0:T(8,128)}, u32[]{:S(2)}, u32[]{:S(2)}) %collective-permute-start.2) | collective-permute-done | bytes 262176 | tf_op jit(solution)/shard_map/ppermute | solution.py:20
  38.6 7.3 %collective-permute-done.4 = f32[16,32,128]{2,1,0:T(8,128)S(1)} collective-permute-done((f32[16,32,128]{2,1,0:T(8,128)S(1)}, f32[16,32,128]{2,1,0:T(8,128)S(1)}, u32[]{:S(2)}, u32[]{:S(2)}) %collective-permute-start.4) | collective-permute-done | bytes 262176 | tf_op jit(solution)/shard_map/ppermute | solution.py:20
  46.7 2.6 collective-permute-start.5
  49.3 3.9 %slice.121 = bf16[4096,384]{1,0:T(8,128)(2,1)} slice(bf16[4096,512]{1,0:T(8,128)(2,1)} %param.16), slice={[0:4096], [128:512]} | slice | bytes 6291456 | tf_op jit(solution)/shard_map/slice | solution.py:322
  54.2 6.1 %collective-permute-done.5 = f32[16,32,128]{2,1,0:T(8,128)} collective-permute-done((f32[16,32,128]{2,1,0:T(8,128)}, f32[16,32,128]{2,1,0:T(8,128)}, u32[]{:S(2)}, u32[]{:S(2)}) %collective-permute-start.5) | collective-permute-done | bytes 262176 | tf_op jit(solution)/shard_map/ppermute | solution.py:20
  61.6 2.8 copy-done.1
  64.4 13.4 %gated_rows.1 = bf16[256,4096]{1,0:T(8,128)(2,1)S(1)} custom-call(bf16[3,256,4096]{2,1,0:T(8,128)(2,1)S(1)} %bitcast.62, f32[3,8,4096]{2,1,0:T(8,128)S(1)} %pad_convert_fusion.halo_ref, f32[9,4096]{1,0:T(8,128)S(1)} %reshape.13.taps_ref, bf16[256,4096]{1,0:T(8,128)(2,1)S(1)} %get-tuple-element.14.mixed_ref, f32[1,4096]{1,0:T(1,128)S(1)} %bitcast.66, ...), custom_call_target="tpu_custom_call" | custom-call | flops 1048576 | bytes 256 | tf_op jit(solution)/shard_map/gated_rows/pallas_call | solution.py:162
  84.7 3.1 constant_dynamic-update-slice_fusion
  87.8 40.1 %collective-permute-done.9 = bf16[128,4096]{1,0:T(8,128)(2,1)S(1)} collective-permute-done((bf16[128,4096]{1,0:T(8,128)(2,1)S(1)}, bf16[128,4096]{1,0:T(8,128)(2,1)S(1)}, u32[]{:S(2)}, u32[]{:S(2)}) %collective-permute-start.9) | collective-permute-done | bytes 1048608 | tf_op jit(solution)/shard_map/ppermute | solution.py:20
  128.6 5.5 %convolution_convert_fusion.1 = bf16[512,1024]{1,0:T(8,128)(2,1)} fusion(bf16[512,4096]{1,0:T(8,128)(2,1)S(1)} %pad_maximum_fusion, bf16[4096,1024]{1,0:T(8,128)(2,1)S(1)} %constant_dynamic-update-slice_fusion), kind=kOutput, calls=%fused_computation.6 | convolution fusion | flops 4295491584 | bytes 13631488 | tf_op jit(solution)/shard_map/dot_general | solution.py:326
  134.1 18.7 %collective-permute-done.10 = bf16[128,4096]{1,0:T(8,128)(2,1)S(1)} collective-permute-done((bf16[128,4096]{1,0:T(8,128)(2,1)S(1)}, bf16[128,4096]{1,0:T(8,128)(2,1)S(1)}, u32[]{:S(2)}, u32[]{:S(2)}) %collective-permute-start.10) | collective-permute-done | bytes 1048608 | tf_op jit(solution)/shard_map/ppermute | solution.py:20
  155.4 41.1 %collective-permute-done.12 = bf16[4096,384]{1,0:T(8,128)(2,1)} collective-permute-done((bf16[4096,384]{1,0:T(8,128)(2,1)S(1)}, bf16[4096,384]{1,0:T(8,128)(2,1)}, u32[]{:S(2)}, u32[]{:S(2)}) %collective-permute-start.12) | collective-permute-done | bytes 3145760 | tf_op jit(solution)/shard_map/ppermute | solution.py:20
  201.8 3.0 constant_dynamic-update-slice_fusion.4
  206.7 16.5 %collective-permute-done.17 = bf16[128,4096]{1,0:T(8,128)(2,1)S(1)} collective-permute-done((bf16[128,4096]{1,0:T(8,128)(2,1)}, bf16[128,4096]{1,0:T(8,128)(2,1)S(1)}, u32[]{:S(2)}, u32[]{:S(2)}) %collective-permute-start.17) | collective-permute-done | bytes 1048608 | tf_op jit(solution)/shard_map/ppermute | solution.py:20
  225.8 2.8 constant_dynamic-update-slice_fusion.2
  236.0 3.4 %collective-permute-start.20 = (bf16[256,1024]{1,0:T(8,128)(2,1)S(1)}, bf16[256,1024]{1,0:T(8,128)(2,1)S(1)}, u32[]{:S(2)}, u32[]{:S(2)}) collective-permute-start(bf16[256,1024]{1,0:T(8,128)(2,1)S(1)} %slice.164), channel_id=1, source_target_pairs={{0,4},{2,6},{4,0},{6,2},{8,12},{10,14},{12,8},{14,10},{17,21},{19,... | collective-permute-start | bytes 1572872 | tf_op jit(solution)/shard_map/ppermute | solution.py:340
  239.3 6.5 %collective-permute-done.18 = bf16[256,1024]{1,0:T(8,128)(2,1)S(1)} collective-permute-done((bf16[256,1024]{1,0:T(8,128)(2,1)S(1)}, bf16[256,1024]{1,0:T(8,128)(2,1)S(1)}, u32[]{:S(2)}, u32[]{:S(2)}) %collective-permute-start.18) | collective-permute-done | bytes 524320 | tf_op jit(solution)/shard_map/ppermute | solution.py:20
  246.4 9.4 %collective-permute-done.15 = bf16[256,1024]{1,0:T(8,128)(2,1)S(1)} collective-permute-done((bf16[256,1024]{1,0:T(8,128)(2,1)S(1)}, bf16[256,1024]{1,0:T(8,128)(2,1)S(1)}, u32[]{:S(2)}, u32[]{:S(2)}) %collective-permute-start.15) | collective-permute-done | bytes 524320 | tf_op jit(solution)/shard_map/ppermute | solution.py:20
  256.4 3.4 %collective-permute-start.22 = (bf16[128,1024]{1,0:T(8,128)(2,1)S(1)}, bf16[128,1024]{1,0:T(8,128)(2,1)S(1)}, u32[]{:S(2)}, u32[]{:S(2)}) collective-permute-start(bf16[128,1024]{1,0:T(8,128)(2,1)S(1)} %get-tuple-element.38), channel_id=1, source_target_pairs={{0,20},{2,22},{4,16},{6,18},{8,28},{10,30},{12,24},{14,26},{16,4},... | collective-permute-start | bytes 786440 | tf_op jit(solution)/shard_map/ppermute | solution.py:20
  260.2 4.5 %convolution_convert_fusion = bf16[512,1024]{1,0:T(8,128)(2,1)S(1)} fusion(bf16[512,4096]{1,0:T(8,128)(2,1)S(1)} %copy-done.9, bf16[4096,1024]{1,0:T(8,128)(2,1)S(1)} %constant_dynamic-update-slice_fusion.2), kind=kOutput, calls=%fused_computation.5 | convolution fusion | flops 4295491584 | bytes 13631488 | tf_op jit(solution)/shard_map/dot_general | solution.py:326
  266.0 21.0 %collective-permute-done.22 = bf16[128,1024]{1,0:T(8,128)(2,1)S(1)} collective-permute-done((bf16[128,1024]{1,0:T(8,128)(2,1)S(1)}, bf16[128,1024]{1,0:T(8,128)(2,1)S(1)}, u32[]{:S(2)}, u32[]{:S(2)}) %collective-permute-start.22) | collective-permute-done | bytes 262176 | tf_op jit(solution)/shard_map/ppermute | solution.py:20
  287.1 3.5 %collective-permute-start.25 = (bf16[128,2048]{1,0:T(8,128)(2,1)S(1)}, bf16[128,2048]{1,0:T(8,128)(2,1)S(1)}, u32[]{:S(2)}, u32[]{:S(2)}) collective-permute-start(bf16[128,2048]{1,0:T(8,128)(2,1)S(1)} %pad_maximum_fusion.4), channel_id=1, source_target_pairs={{0,1},{2,3},{4,5},{6,7},{8,9},{10,11},{12,13},{14,15},{17,16},{19,... | collective-permute-start | bytes 1572872 | tf_op jit(solution)/shard_map/ppermute | solution.py:340
  292.6 3.5 %collective-permute-start.24 = (bf16[128,2048]{1,0:T(8,128)(2,1)S(1)}, bf16[128,2048]{1,0:T(8,128)(2,1)S(1)}, u32[]{:S(2)}, u32[]{:S(2)}) collective-permute-start(bf16[128,2048]{1,0:T(8,128)(2,1)S(1)} %pad_maximum_fusion.3), channel_id=1, source_target_pairs={{0,1},{2,3},{4,5},{6,7},{8,9},{10,11},{12,13},{14,15},{17,16},{19,... | collective-permute-start | bytes 1572872 | tf_op jit(solution)/shard_map/ppermute | solution.py:340
  297.0 2.9 collective-permute-start.26
  299.9 2.9 collective-permute-done.25
  302.9 10.1 %collective-permute-done.24 = bf16[128,2048]{1,0:T(8,128)(2,1)S(1)} collective-permute-done((bf16[128,2048]{1,0:T(8,128)(2,1)S(1)}, bf16[128,2048]{1,0:T(8,128)(2,1)S(1)}, u32[]{:S(2)}, u32[]{:S(2)}) %collective-permute-start.24) | collective-permute-done | bytes 524320 | tf_op jit(solution)/shard_map/ppermute | solution.py:340
  313.5 5.9 %output_rows.1 = (bf16[256,4096]{1,0:T(8,128)(2,1)}, bf16[528,256]{1,0:T(8,128)(2,1)S(1)}) custom-call(s32[8]{0:T(128)S(1)} %iota_xor_fusion.order_ref, bf16[8,256,512]{2,1,0:T(8,128)(2,1)S(1)} %fusion.1.added_ref, bf16[256,4096]{1,0:T(8,128)(2,1)S(1)} %copy-done.3, f32[1,4096]{1,0:T(1,128)S(1)} %bitcast.67, bf16[512,4096]{1,0:T(8,128)(2,1)S(1)} %copy-done.2), custom_call_target="tpu_custom_call" | custom-call | flops 1073741824 | bytes 10485760 | tf_op jit(solution)/shard_map/output_rows/pallas_call | solution.py:249
  319.4 2.5 collective-permute-start.27
  321.9 5.7 %collective-permute-done.27.second_ref = bf16[528,256]{1,0:T(8,128)(2,1)S(1)} collective-permute-done((bf16[528,256]{1,0:T(8,128)(2,1)S(1)}, bf16[528,256]{1,0:T(8,128)(2,1)S(1)}, u32[]{:S(2)}, u32[]{:S(2)}) %collective-permute-start.27) | collective-permute-done | bytes 270368 | tf_op jit(solution)/shard_map/ppermute | solution.py:20
  (112 shorter events, 51.5 us)
Async XLA Ops:
  0.6 61.0 %collective-permute-start.6 = (bf16[4096,512]{1,0:T(8,128)(2,1)}, bf16[4096,512]{1,0:T(8,128)(2,1)}, u32[]{:S(2)}, u32[]{:S(2)}) collective-permute-start(bf16[4096,512]{1,0:T(8,128)(2,1)} %param.16), channel_id=1, source_target_pairs={{0,2},{2,0},{4,6},{6,4},{8,10},{10,8},{12,14},{14,12},{16,18},{18,... | collective-permute-start | bytes 12582920 | tf_op jit(solution)/shard_map/ppermute | solution.py:20
  2.1 9.3 %collective-permute-start = (bf16[2,3,4096]{2,0,1:T(2,128)(2,1)S(1)}, bf16[2,3,4096]{2,0,1:T(2,128)(2,1)S(1)}, u32[]{:S(2)}, u32[]{:S(2)}) collective-permute-start(bf16[2,3,4096]{2,0,1:T(2,128)(2,1)S(1)} %slice.119), channel_id=1, source_target_pairs={{0,2},{2,4},{4,6},{6,8},{8,10},{10,12},{12,14},{14,16},{16,18},{18... | collective-permute-start | bytes 147464 | tf_op jit(solution)/shard_map/ppermute | solution.py:26
  6.4 31.7 %collective-permute-start.3 = (bf16[4096,128]{1,0:T(8,128)(2,1)}, bf16[4096,128]{1,0:T(8,128)(2,1)}, u32[]{:S(2)}, u32[]{:S(2)}) collective-permute-start(bf16[4096,128]{1,0:T(8,128)(2,1)} %slice.120), channel_id=1, source_target_pairs={{0,8},{2,10},{4,12},{6,14},{8,0},{10,2},{12,4},{14,6},{16,24},{18,... | collective-permute-start | bytes 3145736 | tf_op jit(solution)/shard_map/ppermute | solution.py:20
  25.0 2.2 collective-permute-start.1
  28.3 8.8 %collective-permute-start.2 = (f32[16,32,128]{2,1,0:T(8,128)S(1)}, f32[16,32,128]{2,1,0:T(8,128)}, u32[]{:S(2)}, u32[]{:S(2)}) collective-permute-start(f32[16,32,128]{2,1,0:T(8,128)S(1)} %multiply_add_fusion.2), channel_id=1, source_target_pairs={{0,4},{2,6},{4,0},{6,2},{8,12},{10,14},{12,8},{14,10},{16,20},{18,... | collective-permute-start | bytes 786440 | tf_op jit(solution)/shard_map/ppermute | solution.py:20
  38.1 7.8 %collective-permute-start.4 = (f32[16,32,128]{2,1,0:T(8,128)S(1)}, f32[16,32,128]{2,1,0:T(8,128)S(1)}, u32[]{:S(2)}, u32[]{:S(2)}) collective-permute-start(f32[16,32,128]{2,1,0:T(8,128)S(1)} %multiply_add_fusion.1), channel_id=1, source_target_pairs={{0,8},{2,10},{4,12},{6,14},{8,0},{10,2},{12,4},{14,6},{16,24},{18,... | collective-permute-start | bytes 786440 | tf_op jit(solution)/shard_map/ppermute | solution.py:20
  46.7 13.6 %collective-permute-start.5 = (f32[16,32,128]{2,1,0:T(8,128)}, f32[16,32,128]{2,1,0:T(8,128)}, u32[]{:S(2)}, u32[]{:S(2)}) collective-permute-start(f32[16,32,128]{2,1,0:T(8,128)} %multiply_add_fusion), channel_id=1, source_target_pairs={{0,16},{2,18},{4,20},{6,22},{8,24},{10,26},{12,28},{14,30},{16,0},... | collective-permute-start | bytes 786440 | tf_op jit(solution)/shard_map/ppermute | solution.py:20
  77.9 50.3 %collective-permute-start.7 = (bf16[256,4096]{1,0:T(8,128)(2,1)S(1)}, bf16[256,4096]{1,0:T(8,128)(2,1)S(1)}, u32[]{:S(2)}, u32[]{:S(2)}) collective-permute-start(bf16[256,4096]{1,0:T(8,128)(2,1)S(1)} %gated_rows.1), channel_id=1, source_target_pairs={{0,4},{2,6},{4,0},{6,2},{8,12},{10,14},{12,8},{14,10},{16,20},{18,... | collective-permute-start | bytes 6291464 | tf_op jit(solution)/shard_map/ppermute | solution.py:20
  79.7 48.1 %collective-permute-start.9 = (bf16[128,4096]{1,0:T(8,128)(2,1)S(1)}, bf16[128,4096]{1,0:T(8,128)(2,1)S(1)}, u32[]{:S(2)}, u32[]{:S(2)}) collective-permute-start(bf16[128,4096]{1,0:T(8,128)(2,1)S(1)} %get-tuple-element.26), channel_id=1, source_target_pairs={{0,16},{2,18},{4,20},{6,22},{8,24},{10,26},{12,28},{14,30},{16,0},... | collective-permute-start | bytes 3145736 | tf_op jit(solution)/shard_map/ppermute | solution.py:20
  81.7 114.8 %collective-permute-start.12 = (bf16[4096,384]{1,0:T(8,128)(2,1)S(1)}, bf16[4096,384]{1,0:T(8,128)(2,1)}, u32[]{:S(2)}, u32[]{:S(2)}) collective-permute-start(bf16[4096,384]{1,0:T(8,128)(2,1)S(1)} %copy-done.10), channel_id=1, source_target_pairs={{0,8},{2,10},{4,12},{6,14},{8,0},{10,2},{12,4},{14,6},{16,24},{18,... | collective-permute-start | bytes 9437192 | tf_op jit(solution)/shard_map/ppermute | solution.py:20
  83.4 113.0 %collective-permute-start.11 = (bf16[128,4096]{1,0:T(8,128)(2,1)S(1)}, bf16[128,4096]{1,0:T(8,128)(2,1)S(1)}, u32[]{:S(2)}, u32[]{:S(2)}) collective-permute-start(bf16[128,4096]{1,0:T(8,128)(2,1)S(1)} %get-tuple-element.27), channel_id=1, source_target_pairs={{0,16},{2,18},{4,20},{6,22},{8,24},{10,26},{12,28},{14,30},{16,0},... | collective-permute-start | bytes 3145736 | tf_op jit(solution)/shard_map/ppermute | solution.py:20
  87.8 65.2 %copy-start.11 = (bf16[4096,1024]{1,0:T(8,128)(2,1)}, bf16[4096,1024]{1,0:T(8,128)(2,1)S(1)}, u32[]{:S(2)}) copy-start(bf16[4096,1024]{1,0:T(8,128)(2,1)S(1)} %constant_dynamic-update-slice_fusion) | copy-start | bytes 25165828
  127.8 24.9 %collective-permute-start.10 = (bf16[128,4096]{1,0:T(8,128)(2,1)S(1)}, bf16[128,4096]{1,0:T(8,128)(2,1)S(1)}, u32[]{:S(2)}, u32[]{:S(2)}) collective-permute-start(bf16[128,4096]{1,0:T(8,128)(2,1)S(1)} %collective-permute-done.9), channel_id=1, source_target_pairs={{0,4},{2,6},{4,0},{6,2},{8,12},{10,14},{12,8},{14,10},{16,20},{18,... | collective-permute-start | bytes 3145736 | tf_op jit(solution)/shard_map/ppermute | solution.py:20
  196.5 29.3 %collective-permute-start.14 = (bf16[4096,384]{1,0:T(8,128)(2,1)}, bf16[4096,384]{1,0:T(8,128)(2,1)}, u32[]{:S(2)}, u32[]{:S(2)}) collective-permute-start(bf16[4096,384]{1,0:T(8,128)(2,1)} %collective-permute-done.12), channel_id=1, source_target_pairs={{0,2},{2,0},{4,6},{6,4},{8,10},{10,8},{12,14},{14,12},{16,18},{18,... | collective-permute-start | bytes 9437192 | tf_op jit(solution)/shard_map/ppermute | solution.py:20
  197.4 7.4 %collective-permute-start.13 = (bf16[4096,128]{1,0:T(8,128)(2,1)}, bf16[4096,128]{1,0:T(8,128)(2,1)}, u32[]{:S(2)}, u32[]{:S(2)}) collective-permute-start(bf16[4096,128]{1,0:T(8,128)(2,1)} %collective-permute-done.3), channel_id=1, source_target_pairs={{0,2},{2,0},{4,6},{6,4},{8,10},{10,8},{12,14},{14,12},{16,18},{18,... | collective-permute-start | bytes 3145736 | tf_op jit(solution)/shard_map/ppermute | solution.py:20
  197.4 25.8 %collective-permute-start.17 = (bf16[128,4096]{1,0:T(8,128)(2,1)}, bf16[128,4096]{1,0:T(8,128)(2,1)S(1)}, u32[]{:S(2)}, u32[]{:S(2)}) collective-permute-start(bf16[128,4096]{1,0:T(8,128)(2,1)} %copy-done.14), channel_id=1, source_target_pairs={{0,4},{2,6},{4,0},{6,2},{8,12},{10,14},{12,8},{14,10},{16,20},{18,... | collective-permute-start | bytes 3145736 | tf_op jit(solution)/shard_map/ppermute | solution.py:20
  200.2 23.0 %copy-start.15 = (bf16[128,4096]{1,0:T(8,128)(2,1)S(1)}, bf16[128,4096]{1,0:T(8,128)(2,1)}, u32[]{:S(2)}) copy-start(bf16[128,4096]{1,0:T(8,128)(2,1)} %copy-done.14) | copy-start | bytes 3145732
  200.2 35.3 %collective-permute-start.8 = (bf16[512,1024]{1,0:T(8,128)(2,1)}, bf16[512,1024]{1,0:T(8,128)(2,1)S(1)}, u32[]{:S(2)}, u32[]{:S(2)}) collective-permute-start(bf16[512,1024]{1,0:T(8,128)(2,1)} %convolution_convert_fusion.1), channel_id=1, source_target_pairs={{1,0},{3,2},{5,4},{7,6},{9,8},{11,10},{13,12},{15,14},{16,17},{18,... | collective-permute-start | bytes 3145736 | tf_op jit(solution)/shard_map/ppermute | solution.py:340
  201.8 21.6 %copy-start.12 = (bf16[4096,1024]{1,0:T(8,128)(2,1)S(1)}, bf16[4096,1024]{1,0:T(8,128)(2,1)}, u32[]{:S(2)}) copy-start(bf16[4096,1024]{1,0:T(8,128)(2,1)} %copy-done.11) | copy-start | bytes 25165828
  231.0 14.9 %collective-permute-start.18 = (bf16[256,1024]{1,0:T(8,128)(2,1)S(1)}, bf16[256,1024]{1,0:T(8,128)(2,1)S(1)}, u32[]{:S(2)}, u32[]{:S(2)}) collective-permute-start(bf16[256,1024]{1,0:T(8,128)(2,1)S(1)} %get-tuple-element.48), channel_id=1, source_target_pairs={{0,1},{1,0},{2,3},{3,2},{4,5},{5,4},{6,7},{7,6},{8,9},{9,8},{10,11... | collective-permute-start | bytes 1572872 | tf_op jit(solution)/shard_map/ppermute | solution.py:20
  234.9 20.9 %collective-permute-start.15 = (bf16[256,1024]{1,0:T(8,128)(2,1)S(1)}, bf16[256,1024]{1,0:T(8,128)(2,1)S(1)}, u32[]{:S(2)}, u32[]{:S(2)}) collective-permute-start(bf16[256,1024]{1,0:T(8,128)(2,1)S(1)} %get-tuple-element.50), channel_id=1, source_target_pairs={{0,1},{1,0},{2,3},{3,2},{4,5},{5,4},{6,7},{7,6},{8,9},{9,8},{10,11... | collective-permute-start | bytes 1572872 | tf_op jit(solution)/shard_map/ppermute | solution.py:20
  236.0 60.4 %collective-permute-start.20 = (bf16[256,1024]{1,0:T(8,128)(2,1)S(1)}, bf16[256,1024]{1,0:T(8,128)(2,1)S(1)}, u32[]{:S(2)}, u32[]{:S(2)}) collective-permute-start(bf16[256,1024]{1,0:T(8,128)(2,1)S(1)} %slice.164), channel_id=1, source_target_pairs={{0,4},{2,6},{4,0},{6,2},{8,12},{10,14},{12,8},{14,10},{17,21},{19,... | collective-permute-start | bytes 1572872 | tf_op jit(solution)/shard_map/ppermute | solution.py:340
  246.2 18.5 %collective-permute-start.19 = (bf16[128,1024]{1,0:T(8,128)(2,1)S(1)}, bf16[128,1024]{1,0:T(8,128)(2,1)S(1)}, u32[]{:S(2)}, u32[]{:S(2)}) collective-permute-start(bf16[128,1024]{1,0:T(8,128)(2,1)S(1)} %get-tuple-element.39), channel_id=1, source_target_pairs={{0,16},{2,18},{4,20},{6,22},{8,24},{10,26},{12,28},{14,30},{16,0},... | collective-permute-start | bytes 786440 | tf_op jit(solution)/shard_map/ppermute | solution.py:20
  256.1 34.4 %collective-permute-start.16 = (bf16[128,1024]{1,0:T(8,128)(2,1)S(1)}, bf16[128,1024]{1,0:T(8,128)(2,1)S(1)}, u32[]{:S(2)}, u32[]{:S(2)}) collective-permute-start(bf16[128,1024]{1,0:T(8,128)(2,1)S(1)} %get-tuple-element.37), channel_id=1, source_target_pairs={{0,16},{2,18},{4,20},{6,22},{8,24},{10,26},{12,28},{14,30},{16,0},... | collective-permute-start | bytes 786440 | tf_op jit(solution)/shard_map/ppermute | solution.py:20
  256.4 30.7 %collective-permute-start.22 = (bf16[128,1024]{1,0:T(8,128)(2,1)S(1)}, bf16[128,1024]{1,0:T(8,128)(2,1)S(1)}, u32[]{:S(2)}, u32[]{:S(2)}) collective-permute-start(bf16[128,1024]{1,0:T(8,128)(2,1)S(1)} %get-tuple-element.38), channel_id=1, source_target_pairs={{0,20},{2,22},{4,16},{6,18},{8,28},{10,30},{12,24},{14,26},{16,4},... | collective-permute-start | bytes 786440 | tf_op jit(solution)/shard_map/ppermute | solution.py:20
  259.8 32.8 %collective-permute-start.21 = (bf16[128,1024]{1,0:T(8,128)(2,1)S(1)}, bf16[128,1024]{1,0:T(8,128)(2,1)S(1)}, u32[]{:S(2)}, u32[]{:S(2)}) collective-permute-start(bf16[128,1024]{1,0:T(8,128)(2,1)S(1)} %get-tuple-element.36), channel_id=1, source_target_pairs={{0,20},{2,22},{4,16},{6,18},{8,28},{10,30},{12,24},{14,26},{16,4},... | collective-permute-start | bytes 786440 | tf_op jit(solution)/shard_map/ppermute | solution.py:20
  264.7 31.8 %collective-permute-start.23 = (bf16[512,1024]{1,0:T(8,128)(2,1)S(1)}, bf16[512,1024]{1,0:T(8,128)(2,1)S(1)}, u32[]{:S(2)}, u32[]{:S(2)}) collective-permute-start(bf16[512,1024]{1,0:T(8,128)(2,1)S(1)} %convolution_convert_fusion), channel_id=1, source_target_pairs={{1,0},{3,2},{5,4},{7,6},{9,8},{11,10},{13,12},{15,14},{16,17},{18,... | collective-permute-start | bytes 3145736 | tf_op jit(solution)/shard_map/ppermute | solution.py:340
  287.1 15.7 %collective-permute-start.25 = (bf16[128,2048]{1,0:T(8,128)(2,1)S(1)}, bf16[128,2048]{1,0:T(8,128)(2,1)S(1)}, u32[]{:S(2)}, u32[]{:S(2)}) collective-permute-start(bf16[128,2048]{1,0:T(8,128)(2,1)S(1)} %pad_maximum_fusion.4), channel_id=1, source_target_pairs={{0,1},{2,3},{4,5},{6,7},{8,9},{10,11},{12,13},{14,15},{17,16},{19,... | collective-permute-start | bytes 1572872 | tf_op jit(solution)/shard_map/ppermute | solution.py:340
  292.6 20.4 %collective-permute-start.24 = (bf16[128,2048]{1,0:T(8,128)(2,1)S(1)}, bf16[128,2048]{1,0:T(8,128)(2,1)S(1)}, u32[]{:S(2)}, u32[]{:S(2)}) collective-permute-start(bf16[128,2048]{1,0:T(8,128)(2,1)S(1)} %pad_maximum_fusion.3), channel_id=1, source_target_pairs={{0,1},{2,3},{4,5},{6,7},{8,9},{10,11},{12,13},{14,15},{17,16},{19,... | collective-permute-start | bytes 1572872 | tf_op jit(solution)/shard_map/ppermute | solution.py:340
  297.0 16.4 %copy-start.2 = (bf16[512,4096]{1,0:T(8,128)(2,1)S(1)}, bf16[512,4096]{1,0:T(8,128)(2,1)}, u32[]{:S(2)}) copy-start(bf16[512,4096]{1,0:T(8,128)(2,1)} %table_ref.1) | copy-start | bytes 12582916
  297.0 16.2 %collective-permute-start.26 = (bf16[256,1024]{1,0:T(8,128)(2,1)S(1)}, bf16[256,1024]{1,0:T(8,128)(2,1)S(1)}, u32[]{:S(2)}, u32[]{:S(2)}) collective-permute-start(bf16[256,1024]{1,0:T(8,128)(2,1)S(1)} %slice.179), channel_id=1, source_target_pairs={{0,4},{2,6},{4,0},{6,2},{8,12},{10,14},{12,8},{14,10},{17,21},{19,... | collective-permute-start | bytes 1572872 | tf_op jit(solution)/shard_map/ppermute | solution.py:340
  319.4 8.2 %collective-permute-start.27 = (bf16[528,256]{1,0:T(8,128)(2,1)S(1)}, bf16[528,256]{1,0:T(8,128)(2,1)S(1)}, u32[]{:S(2)}, u32[]{:S(2)}) collective-permute-start(bf16[528,256]{1,0:T(8,128)(2,1)S(1)} %get-tuple-element.25.first_ref), channel_id=1, source_target_pairs={{0,1},{1,0},{2,3},{3,2},{4,5},{5,4},{6,7},{7,6},{8,9},{9,8},{10,11... | collective-permute-start | bytes 811016 | tf_op jit(solution)/shard_map/ppermute | solution.py:20
  (12 other events, 94.4 us)

commit v4 on v3

--- a/solution.py
+++ b/solution.py
@@ -185,7 +185,7 @@
     )(streams, halo, taps, mixed, skip, rates, residues, entering)
 
 
-def entering_states(end, rates, rows, merges, before=None):
+def entering_states(end, rates, rows, merges, before=None, after=()):
     place = lax.axis_index("seq")
     total, entering = end, jnp.zeros_like(end)
     held = []
@@ -196,6 +196,10 @@
         others = [
             (mask, xor_permute(total, "seq", mask * span)) for mask in range(1, count)
         ]
+        if before and bits in before:
+            value, *waiting = tied(others[0][1], *after)
+            others = [(1, value)]
+            held += waiting
         own = (place // span) % count
         inside = (place % span) * rows
         merged = jnp.zeros_like(total)
@@ -355,27 +359,29 @@
     near = jnp.concatenate([out_weight, core_weight], axis=1)
     first = tied(jnp.concatenate([gated, beside], axis=0))[0]
     near_first = product(first, near)
+    across[0], *far = tied(across[0], *far)
     second = [tied(jnp.concatenate([above[0], across[0]], axis=0))[0]]
-    near_second = [product(second[0], near)]
-    above[1], far[1], _, _ = tied(above[1], far[1], near_first, near_second[0])
-    across.append(xor_permute(above[1], "seq", side))
     far_all = jnp.concatenate(far + [xor_permute(piece, "seq", core) for piece in far], axis=1)
-    second.append(tied(jnp.concatenate([above[1], across[1]], axis=0))[0])
-    near_second.append(product(second[1], near))
 
     def first_sums(partial):
         total = added_up(partial, placed_permute(partial, False, 0, 1))
         return total[:rows], placed_permute(total[rows:], True, side, 0)
 
-    def second_sums(close, distant):
-        other = xor_permute(jnp.where(here, distant, close), "chan", 1)
-        total = added_up(jnp.where(here, close, distant), other)
+    def shared(rows_all):
+        close, distant = product(rows_all, near), product(rows_all, far_all)
+        return jnp.where(here, distant, close), jnp.where(here, close, distant)
+
+    def second_sums(sent, kept):
+        total = added_up(kept, xor_permute(sent, "chan", 1))
         back = [xor_permute(total[:part], "seq", top), xor_permute(total[part:], "seq", top | side)]
         hop = placed_permute(jnp.concatenate(back, axis=1), True, 0, 1)
         return back, jnp.split(hop, 2, axis=1)
 
-    far_second = [product(rows_all, far_all) for rows_all in second]
-    sums = [second_sums(*pair) for pair in zip(near_second, far_second)]
+    early = shared(second[0])
+    above[1], *_ = tied(above[1], near_first, *early)
+    across.append(xor_permute(above[1], "seq", side))
+    second.append(tied(jnp.concatenate([above[1], across[1]], axis=0))[0])
+    sums = [second_sums(*early), second_sums(*shared(second[1]))]
     near_sums = first_sums(near_first)
     far_sums = first_sums(product(first, far_all))
     blocks = {}
@@ -441,10 +447,10 @@
     bits = range(count.bit_length() - 1)
     merges = [(bit,) for bit in bits]
     before = {(2,): far[:1]} if fast else None
-    entering, held = entering_states(end, rates, rows, merges, before)
+    after = far[1:] if fast else ()
+    entering, held = entering_states(end, rates, rows, merges, before, after)
     if fast:
-        entering, *waiting = tied(entering, *far[1:])
-        far = held + [xor_permute(piece, "seq", low) for piece in waiting]
+        far = held[:1] + [xor_permute(held[1], "seq", low)]
     if fast:
         entering, core_weight = tied(entering, core_weight)
     gated = gated_rows(streams, halo, taps, mixed, skip_gain[None, :], rates, weights, entering)

time: 329 us -> 315 us (0.957)
  waiting for transfers between devices: 196 us -> 169 us
  starting transfers between devices: 42.3 us -> 56.5 us
    ppermute x21, waiting for transfers between devices: 183 us -> 145 us  [xor_permute(): lax.ppermute(value, axis, [(source, source ^ mask) for source in range(co...]
    ppermute x21, starting transfers between devices: 24.3 us -> 38.8 us  [xor_permute(): lax.ppermute(value, axis, [(source, source ^ mask) for source in range(co...]
    ppermute x6, waiting for transfers between devices: 13 us -> 23.4 us  [placed_permute(): return lax.ppermute(value, ('seq', 'chan'), pairs)]
    unnamed x38 -> x32, local copies, waits for them, and re-layouts: 16.9 us -> 16 us
  transfers between devices with their start and end apart: 28 -> 28, of which waited for: 15 -> 16; matrix products, arithmetic and copies ran while one was open for 15% -> 15% of each run, Pallas kernels for 3% -> 8%
where the time goes in v4:
time: 315 us; the launch traced here: 314 us
  waiting for transfers between devices  169 us (54%)
  starting transfers between devices  56.5 us (18%)
  Pallas kernels  30.9 us (10%)
  local copies, waits for them, and re-layouts  29.1 us (9%)
  matrix products  18.4 us (6%)
  other arithmetic  9.22 us (3%)
    ppermute x21, waiting for transfers between devices, xor_permute(): lax.ppermute(value, axis, [(source, source ^ mask) for source in range(co...  145 us
    ppermute x21, starting transfers between devices, xor_permute(): lax.ppermute(value, axis, [(source, source ^ mask) for source in range(co...  38.8 us
    ppermute x6, waiting for transfers between devices, placed_permute(): return lax.ppermute(value, ('seq', 'chan'), pairs)  23.4 us
    dot_general x6, matrix products, product(): return jnp.dot(rows, weight, preferred_element_type=F32).astype(BF16)  18.4 us
    unnamed x32, local copies, waits for them, and re-layouts  16 us
    ppermute x6, starting transfers between devices, placed_permute(): return lax.ppermute(value, ('seq', 'chan'), pairs)  15.7 us
    pallas_call x1, Pallas kernels, gated_rows(): pl.pallas_call(gated_kernel, grid=(width // GROUP,), in_specs=[pl.BlockSp...  13.4 us
    pallas_call x1, Pallas kernels, mixed_and_states(): pl.pallas_call(states_kernel, grid=(width // GROUP,), in_specs=[stream(1)...  10.8 us
  transfers between devices with their start and end apart: 28, of which 16 were waited for; matrix products, arithmetic and copies ran while one was open for 15% of the time, Pallas kernels for 8%

profile of v4, /device:TPU:0, one launch (start us, length us, event | category | flops | bytes accessed | tf_op | source)
XLA Modules:
  0.0 313.9 jit_solution(16553568601995079424)
XLA Ops:
  5.4 3.1 collective-permute-start.3
  10.6 2.8 copy-done
  13.4 10.8 %mixed_and_states.1 = (bf16[256,4096]{1,0:T(8,128)(2,1)S(1)}, f32[16,32,128]{2,1,0:T(8,128)S(1)}) custom-call(bf16[3,256,4096]{2,1,0:T(8,128)(2,1)S(1)} %bitcast.60, bf16[3,256,4096]{2,1,0:T(8,128)(2,1)S(1)} %bitcast.61, f32[3,8,4096]{2,1,0:T(8,128)S(1)} %pad_convert_fusion.halo_ref, f32[9,4096]{1,0:T(8,128)S(1)} %reshape.13.taps_ref, ...), custom_call_target="tpu_custom_call" | custom-call | flops 1048576 | bytes 256 | tf_op jit(solution)/shard_map/mixed_and_states/pallas_call | solution.py:132
  30.3 7.1 %collective-permute-done.2 = f32[16,32,128]{2,1,0:T(8,128)} collective-permute-done((f32[16,32,128]{2,1,0:T(8,128)S(1)}, f32[16,32,128]{2,1,0:T(8,128)}, u32[]{:S(2)}, u32[]{:S(2)}) %collective-permute-start.2) | collective-permute-done | bytes 262176 | tf_op jit(solution)/shard_map/ppermute | solution.py:20
  39.0 4.0 %slice.121 = bf16[4096,384]{1,0:T(8,128)(2,1)} slice(bf16[4096,512]{1,0:T(8,128)(2,1)} %param.16), slice={[0:4096], [128:512]} | slice | bytes 6291456 | tf_op jit(solution)/shard_map/slice | solution.py:326
  43.0 3.3 %collective-permute-done.4 = f32[16,32,128]{2,1,0:T(8,128)S(1)} collective-permute-done((f32[16,32,128]{2,1,0:T(8,128)S(1)}, f32[16,32,128]{2,1,0:T(8,128)S(1)}, u32[]{:S(2)}, u32[]{:S(2)}) %collective-permute-start.4) | collective-permute-done | bytes 262176 | tf_op jit(solution)/shard_map/ppermute | solution.py:20
  49.6 10.2 %collective-permute-done.5 = f32[16,32,128]{2,1,0:T(8,128)S(1)} collective-permute-done((f32[16,32,128]{2,1,0:T(8,128)S(1)}, f32[16,32,128]{2,1,0:T(8,128)S(1)}, u32[]{:S(2)}, u32[]{:S(2)}) %collective-permute-start.5) | collective-permute-done | bytes 262176 | tf_op jit(solution)/shard_map/ppermute | solution.py:20
  61.1 2.8 copy-done.1
  65.5 13.4 %gated_rows.1 = bf16[256,4096]{1,0:T(8,128)(2,1)S(1)} custom-call(bf16[3,256,4096]{2,1,0:T(8,128)(2,1)S(1)} %bitcast.62, f32[3,8,4096]{2,1,0:T(8,128)S(1)} %pad_convert_fusion.halo_ref, f32[9,4096]{1,0:T(8,128)S(1)} %reshape.13.taps_ref, bf16[256,4096]{1,0:T(8,128)(2,1)S(1)} %copy-done.5, f32[1,4096]{1,0:T(1,128)S(1)} %bitcast.66, ...), custom_call_target="tpu_custom_call" | custom-call | flops 1048576 | bytes 256 | tf_op jit(solution)/shard_map/gated_rows/pallas_call | solution.py:162
  82.1 2.9 constant_dynamic-update-slice_fusion.1
  85.0 3.0 collective-permute-start.16
  88.0 57.8 %collective-permute-done.9 = bf16[128,4096]{1,0:T(8,128)(2,1)} collective-permute-done((bf16[128,4096]{1,0:T(8,128)(2,1)}, bf16[128,4096]{1,0:T(8,128)(2,1)}, u32[]{:S(2)}, u32[]{:S(2)}) %collective-permute-start.9) | collective-permute-done | bytes 1048608 | tf_op jit(solution)/shard_map/ppermute | solution.py:20
  146.4 3.1 constant_dynamic-update-slice_fusion
  151.6 7.9 %collective-permute-done.11 = bf16[4096,384]{1,0:T(8,128)(2,1)} collective-permute-done((bf16[4096,384]{1,0:T(8,128)(2,1)}, bf16[4096,384]{1,0:T(8,128)(2,1)}, u32[]{:S(2)}, u32[]{:S(2)}) %collective-permute-start.11) | collective-permute-done | bytes 3145760 | tf_op jit(solution)/shard_map/ppermute | solution.py:20
  159.5 7.0 %collective-permute-done.10 = bf16[128,4096]{1,0:T(8,128)(2,1)S(1)} collective-permute-done((bf16[128,4096]{1,0:T(8,128)(2,1)}, bf16[128,4096]{1,0:T(8,128)(2,1)S(1)}, u32[]{:S(2)}, u32[]{:S(2)}) %collective-permute-start.10) | collective-permute-done | bytes 1048608 | tf_op jit(solution)/shard_map/ppermute | solution.py:20
  166.5 4.5 %convolution_convert_fusion.1 = bf16[512,1024]{1,0:T(8,128)(2,1)S(1)} fusion(bf16[512,4096]{1,0:T(8,128)(2,1)S(1)} %pad_maximum_fusion, bf16[4096,1024]{1,0:T(8,128)(2,1)S(1)} %constant_dynamic-update-slice_fusion), kind=kOutput, calls=%fused_computation.6 | convolution fusion | flops 4295491584 | bytes 13631488 | tf_op jit(solution)/shard_map/dot_general | solution.py:330
  174.8 2.8 constant_dynamic-update-slice_fusion.4
  186.2 12.7 %collective-permute-done.8 = bf16[512,1024]{1,0:T(8,128)(2,1)S(1)} collective-permute-done((bf16[512,1024]{1,0:T(8,128)(2,1)S(1)}, bf16[512,1024]{1,0:T(8,128)(2,1)S(1)}, u32[]{:S(2)}, u32[]{:S(2)}) %collective-permute-start.8) | collective-permute-done | bytes 1048608 | tf_op jit(solution)/shard_map/ppermute | solution.py:344
  201.5 8.2 %collective-permute-done.14 = bf16[256,1024]{1,0:T(8,128)(2,1)S(1)} collective-permute-done((bf16[256,1024]{1,0:T(8,128)(2,1)S(1)}, bf16[256,1024]{1,0:T(8,128)(2,1)S(1)}, u32[]{:S(2)}, u32[]{:S(2)}) %collective-permute-start.14) | collective-permute-done | bytes 524320 | tf_op jit(solution)/shard_map/ppermute | solution.py:20
  210.4 4.5 %convolution_convert_fusion = bf16[512,1024]{1,0:T(8,128)(2,1)S(1)} fusion(bf16[512,4096]{1,0:T(8,128)(2,1)S(1)} %pad_maximum_fusion, bf16[4096,1024]{1,0:T(8,128)(2,1)S(1)} %constant_dynamic-update-slice_fusion.2), kind=kOutput, calls=%fused_computation.5 | convolution fusion | flops 4295491584 | bytes 13631488 | tf_op jit(solution)/shard_map/dot_general | solution.py:330
  216.4 5.6 %collective-permute-start.15 = (bf16[128,1024]{1,0:T(8,128)(2,1)S(1)}, bf16[128,1024]{1,0:T(8,128)(2,1)S(1)}, u32[]{:S(2)}, u32[]{:S(2)}) collective-permute-start(bf16[128,1024]{1,0:T(8,128)(2,1)S(1)} %get-tuple-element.43), channel_id=1, source_target_pairs={{0,16},{2,18},{4,20},{6,22},{8,24},{10,26},{12,28},{14,30},{16,0},... | collective-permute-start | bytes 786440 | tf_op jit(solution)/shard_map/ppermute | solution.py:20
  223.3 13.5 %collective-permute-done.17 = bf16[128,4096]{1,0:T(8,128)(2,1)S(1)} collective-permute-done((bf16[128,4096]{1,0:T(8,128)(2,1)S(1)}, bf16[128,4096]{1,0:T(8,128)(2,1)S(1)}, u32[]{:S(2)}, u32[]{:S(2)}) %collective-permute-start.17) | collective-permute-done | bytes 1048608 | tf_op jit(solution)/shard_map/ppermute | solution.py:20
  243.8 3.7 %collective-permute-start.24 = (bf16[128,2048]{1,0:T(8,128)(2,1)S(1)}, bf16[128,2048]{1,0:T(8,128)(2,1)S(1)}, u32[]{:S(2)}, u32[]{:S(2)}) collective-permute-start(bf16[128,2048]{1,0:T(8,128)(2,1)S(1)} %pad_maximum_fusion.3), channel_id=1, source_target_pairs={{0,1},{2,3},{4,5},{6,7},{8,9},{10,11},{12,13},{14,15},{17,16},{19,... | collective-permute-start | bytes 1572872 | tf_op jit(solution)/shard_map/ppermute | solution.py:344
  247.5 6.8 %collective-permute-done.18 = bf16[256,1024]{1,0:T(8,128)(2,1)S(1)} collective-permute-done((bf16[256,1024]{1,0:T(8,128)(2,1)S(1)}, bf16[256,1024]{1,0:T(8,128)(2,1)S(1)}, u32[]{:S(2)}, u32[]{:S(2)}) %collective-permute-start.18) | collective-permute-done | bytes 524320 | tf_op jit(solution)/shard_map/ppermute | solution.py:20
  254.6 11.0 %collective-permute-start.19 = (bf16[128,1024]{1,0:T(8,128)(2,1)S(1)}, bf16[128,1024]{1,0:T(8,128)(2,1)S(1)}, u32[]{:S(2)}, u32[]{:S(2)}) collective-permute-start(bf16[128,1024]{1,0:T(8,128)(2,1)S(1)} %get-tuple-element.45), channel_id=1, source_target_pairs={{0,16},{2,18},{4,20},{6,22},{8,24},{10,26},{12,28},{14,30},{16,0},... | collective-permute-start | bytes 786440 | tf_op jit(solution)/shard_map/ppermute | solution.py:20
  266.1 3.4 %collective-permute-start.26 = (bf16[256,1024]{1,0:T(8,128)(2,1)S(1)}, bf16[256,1024]{1,0:T(8,128)(2,1)S(1)}, u32[]{:S(2)}, u32[]{:S(2)}) collective-permute-start(bf16[256,1024]{1,0:T(8,128)(2,1)S(1)} %slice.179), channel_id=1, source_target_pairs={{0,4},{2,6},{4,0},{6,2},{8,12},{10,14},{12,8},{14,10},{17,21},{19,... | collective-permute-start | bytes 1572872 | tf_op jit(solution)/shard_map/ppermute | solution.py:344
  269.6 9.2 %collective-permute-done.19 = bf16[128,1024]{1,0:T(8,128)(2,1)S(1)} collective-permute-done((bf16[128,1024]{1,0:T(8,128)(2,1)S(1)}, bf16[128,1024]{1,0:T(8,128)(2,1)S(1)}, u32[]{:S(2)}, u32[]{:S(2)}) %collective-permute-start.19) | collective-permute-done | bytes 262176 | tf_op jit(solution)/shard_map/ppermute | solution.py:20
  278.8 5.4 %collective-permute-done.22 = bf16[128,1024]{1,0:T(8,128)(2,1)S(1)} collective-permute-done((bf16[128,1024]{1,0:T(8,128)(2,1)S(1)}, bf16[128,1024]{1,0:T(8,128)(2,1)S(1)}, u32[]{:S(2)}, u32[]{:S(2)}) %collective-permute-start.22) | collective-permute-done | bytes 262176 | tf_op jit(solution)/shard_map/ppermute | solution.py:20
  284.2 3.4 %collective-permute-start.25 = (bf16[128,2048]{1,0:T(8,128)(2,1)S(1)}, bf16[128,2048]{1,0:T(8,128)(2,1)S(1)}, u32[]{:S(2)}, u32[]{:S(2)}) collective-permute-start(bf16[128,2048]{1,0:T(8,128)(2,1)S(1)} %pad_maximum_fusion.4), channel_id=1, source_target_pairs={{0,1},{2,3},{4,5},{6,7},{8,9},{10,11},{12,13},{14,15},{17,16},{19,... | collective-permute-start | bytes 1572872 | tf_op jit(solution)/shard_map/ppermute | solution.py:344
  288.0 10.6 %collective-permute-done.25 = bf16[128,2048]{1,0:T(8,128)(2,1)S(1)} collective-permute-done((bf16[128,2048]{1,0:T(8,128)(2,1)S(1)}, bf16[128,2048]{1,0:T(8,128)(2,1)S(1)}, u32[]{:S(2)}, u32[]{:S(2)}) %collective-permute-start.25) | collective-permute-done | bytes 524320 | tf_op jit(solution)/shard_map/ppermute | solution.py:344
  299.1 5.9 %output_rows.1 = (bf16[256,4096]{1,0:T(8,128)(2,1)}, bf16[528,256]{1,0:T(8,128)(2,1)S(1)}) custom-call(s32[8]{0:T(128)S(1)} %iota_xor_fusion.order_ref, bf16[8,256,512]{2,1,0:T(8,128)(2,1)S(1)} %fusion.1.added_ref, bf16[256,4096]{1,0:T(8,128)(2,1)S(1)} %copy-done.3, f32[1,4096]{1,0:T(1,128)S(1)} %bitcast.67, bf16[512,4096]{1,0:T(8,128)(2,1)S(1)} %copy-done.2), custom_call_target="tpu_custom_call" | custom-call | flops 1073741824 | bytes 10485760 | tf_op jit(solution)/shard_map/output_rows/pallas_call | solution.py:253
  307.5 5.6 %collective-permute-done.27.second_ref = bf16[528,256]{1,0:T(8,128)(2,1)S(1)} collective-permute-done((bf16[528,256]{1,0:T(8,128)(2,1)S(1)}, bf16[528,256]{1,0:T(8,128)(2,1)S(1)}, u32[]{:S(2)}, u32[]{:S(2)}) %collective-permute-start.27) | collective-permute-done | bytes 270368 | tf_op jit(solution)/shard_map/ppermute | solution.py:20
  (106 shorter events, 56.5 us)
Async XLA Ops:
  0.6 60.4 %collective-permute-start.6 = (bf16[4096,512]{1,0:T(8,128)(2,1)}, bf16[4096,512]{1,0:T(8,128)(2,1)}, u32[]{:S(2)}, u32[]{:S(2)}) collective-permute-start(bf16[4096,512]{1,0:T(8,128)(2,1)} %param.16), channel_id=1, source_target_pairs={{0,2},{2,0},{4,6},{6,4},{8,10},{10,8},{12,14},{14,12},{16,18},{18,... | collective-permute-start | bytes 12582920 | tf_op jit(solution)/shard_map/ppermute | solution.py:20
  2.1 8.4 %collective-permute-start = (bf16[2,3,4096]{2,0,1:T(2,128)(2,1)S(1)}, bf16[2,3,4096]{2,0,1:T(2,128)(2,1)S(1)}, u32[]{:S(2)}, u32[]{:S(2)}) collective-permute-start(bf16[2,3,4096]{2,0,1:T(2,128)(2,1)S(1)} %slice.119), channel_id=1, source_target_pairs={{0,2},{2,4},{4,6},{6,8},{8,10},{10,12},{12,14},{14,16},{16,18},{18... | collective-permute-start | bytes 147464 | tf_op jit(solution)/shard_map/ppermute | solution.py:26
  5.4 33.0 %collective-permute-start.3 = (bf16[4096,128]{1,0:T(8,128)(2,1)S(1)}, bf16[4096,128]{1,0:T(8,128)(2,1)S(1)}, u32[]{:S(2)}, u32[]{:S(2)}) collective-permute-start(bf16[4096,128]{1,0:T(8,128)(2,1)S(1)} %slice.120), channel_id=1, source_target_pairs={{0,8},{2,10},{4,12},{6,14},{8,0},{10,2},{12,4},{14,6},{16,24},{18,... | collective-permute-start | bytes 3145736 | tf_op jit(solution)/shard_map/ppermute | solution.py:20
  25.5 2.1 collective-permute-start.1
  28.6 8.8 %collective-permute-start.2 = (f32[16,32,128]{2,1,0:T(8,128)S(1)}, f32[16,32,128]{2,1,0:T(8,128)}, u32[]{:S(2)}, u32[]{:S(2)}) collective-permute-start(f32[16,32,128]{2,1,0:T(8,128)S(1)} %multiply_add_fusion.2), channel_id=1, source_target_pairs={{0,4},{2,6},{4,0},{6,2},{8,12},{10,14},{12,8},{14,10},{16,20},{18,... | collective-permute-start | bytes 786440 | tf_op jit(solution)/shard_map/ppermute | solution.py:20
  38.5 7.8 %collective-permute-start.4 = (f32[16,32,128]{2,1,0:T(8,128)S(1)}, f32[16,32,128]{2,1,0:T(8,128)S(1)}, u32[]{:S(2)}, u32[]{:S(2)}) collective-permute-start(f32[16,32,128]{2,1,0:T(8,128)S(1)} %multiply_add_fusion.1), channel_id=1, source_target_pairs={{0,8},{2,10},{4,12},{6,14},{8,0},{10,2},{12,4},{14,6},{16,24},{18,... | collective-permute-start | bytes 786440 | tf_op jit(solution)/shard_map/ppermute | solution.py:20
  43.0 18.1 %copy-start.6 = (f32[4096]{0:T(1024)S(1)}, f32[4096]{0:T(1024)}, u32[]{:S(2)}) copy-start(f32[4096]{0:T(1024)} %param.15) | copy-start | bytes 49156
  46.4 13.4 %collective-permute-start.5 = (f32[16,32,128]{2,1,0:T(8,128)S(1)}, f32[16,32,128]{2,1,0:T(8,128)S(1)}, u32[]{:S(2)}, u32[]{:S(2)}) collective-permute-start(f32[16,32,128]{2,1,0:T(8,128)S(1)} %multiply_add_fusion), channel_id=1, source_target_pairs={{0,16},{2,18},{4,20},{6,22},{8,24},{10,26},{12,28},{14,30},{16,0},... | collective-permute-start | bytes 786440 | tf_op jit(solution)/shard_map/ppermute | solution.py:20
  49.1 110.4 %collective-permute-start.11 = (bf16[4096,384]{1,0:T(8,128)(2,1)}, bf16[4096,384]{1,0:T(8,128)(2,1)}, u32[]{:S(2)}, u32[]{:S(2)}) collective-permute-start(bf16[4096,384]{1,0:T(8,128)(2,1)} %slice.121), channel_id=1, source_target_pairs={{0,8},{2,10},{4,12},{6,14},{8,0},{10,2},{12,4},{14,6},{16,24},{18,... | collective-permute-start | bytes 9437192 | tf_op jit(solution)/shard_map/ppermute | solution.py:20
  78.9 70.6 %collective-permute-start.7 = (bf16[256,4096]{1,0:T(8,128)(2,1)S(1)}, bf16[256,4096]{1,0:T(8,128)(2,1)}, u32[]{:S(2)}, u32[]{:S(2)}) collective-permute-start(bf16[256,4096]{1,0:T(8,128)(2,1)S(1)} %gated_rows.1), channel_id=1, source_target_pairs={{0,4},{2,6},{4,0},{6,2},{8,12},{10,14},{12,8},{14,10},{16,20},{18,... | collective-permute-start | bytes 6291464 | tf_op jit(solution)/shard_map/ppermute | solution.py:20
  82.1 63.8 %collective-permute-start.9 = (bf16[128,4096]{1,0:T(8,128)(2,1)}, bf16[128,4096]{1,0:T(8,128)(2,1)}, u32[]{:S(2)}, u32[]{:S(2)}) collective-permute-start(bf16[128,4096]{1,0:T(8,128)(2,1)} %get-tuple-element.32), channel_id=1, source_target_pairs={{0,16},{2,18},{4,20},{6,22},{8,24},{10,26},{12,28},{14,30},{16,0},... | collective-permute-start | bytes 3145736 | tf_op jit(solution)/shard_map/ppermute | solution.py:20
  85.0 125.0 %collective-permute-start.16 = (bf16[128,4096]{1,0:T(8,128)(2,1)S(1)}, bf16[128,4096]{1,0:T(8,128)(2,1)S(1)}, u32[]{:S(2)}, u32[]{:S(2)}) collective-permute-start(bf16[128,4096]{1,0:T(8,128)(2,1)S(1)} %copy-done.11), channel_id=1, source_target_pairs={{0,16},{2,18},{4,20},{6,22},{8,24},{10,26},{12,28},{14,30},{16,0},... | collective-permute-start | bytes 3145736 | tf_op jit(solution)/shard_map/ppermute | solution.py:20
  145.8 20.7 %collective-permute-start.10 = (bf16[128,4096]{1,0:T(8,128)(2,1)}, bf16[128,4096]{1,0:T(8,128)(2,1)S(1)}, u32[]{:S(2)}, u32[]{:S(2)}) collective-permute-start(bf16[128,4096]{1,0:T(8,128)(2,1)} %collective-permute-done.9), channel_id=1, source_target_pairs={{0,4},{2,6},{4,0},{6,2},{8,12},{10,14},{12,8},{14,10},{16,20},{18,... | collective-permute-start | bytes 3145736 | tf_op jit(solution)/shard_map/ppermute | solution.py:20
  151.6 20.9 %copy-start.10 = (bf16[4096,128]{1,0:T(8,128)(2,1)S(1)}, bf16[4096,128]{1,0:T(8,128)(2,1)}, u32[]{:S(2)}) copy-start(bf16[4096,128]{1,0:T(8,128)(2,1)} %copy-done.9) | copy-start | bytes 3145732
  166.5 13.8 %collective-permute-start.13 = (bf16[4096,384]{1,0:T(8,128)(2,1)}, bf16[4096,384]{1,0:T(8,128)(2,1)S(1)}, u32[]{:S(2)}, u32[]{:S(2)}) collective-permute-start(bf16[4096,384]{1,0:T(8,128)(2,1)} %collective-permute-done.11), channel_id=1, source_target_pairs={{0,2},{2,0},{4,6},{6,4},{8,10},{10,8},{12,14},{14,12},{16,18},{18,... | collective-permute-start | bytes 9437192 | tf_op jit(solution)/shard_map/ppermute | solution.py:20
  171.0 27.8 %collective-permute-start.8 = (bf16[512,1024]{1,0:T(8,128)(2,1)S(1)}, bf16[512,1024]{1,0:T(8,128)(2,1)S(1)}, u32[]{:S(2)}, u32[]{:S(2)}) collective-permute-start(bf16[512,1024]{1,0:T(8,128)(2,1)S(1)} %convolution_convert_fusion.1), channel_id=1, source_target_pairs={{1,0},{3,2},{5,4},{7,6},{9,8},{11,10},{13,12},{15,14},{16,17},{18,... | collective-permute-start | bytes 3145736 | tf_op jit(solution)/shard_map/ppermute | solution.py:344
  172.5 7.5 %collective-permute-start.12 = (bf16[4096,128]{1,0:T(8,128)(2,1)S(1)}, bf16[4096,128]{1,0:T(8,128)(2,1)S(1)}, u32[]{:S(2)}, u32[]{:S(2)}) collective-permute-start(bf16[4096,128]{1,0:T(8,128)(2,1)S(1)} %copy-done.10), channel_id=1, source_target_pairs={{0,2},{2,0},{4,6},{6,4},{8,10},{10,8},{12,14},{14,12},{16,18},{18,... | collective-permute-start | bytes 3145736 | tf_op jit(solution)/shard_map/ppermute | solution.py:20
  183.7 26.1 %collective-permute-start.14 = (bf16[256,1024]{1,0:T(8,128)(2,1)S(1)}, bf16[256,1024]{1,0:T(8,128)(2,1)S(1)}, u32[]{:S(2)}, u32[]{:S(2)}) collective-permute-start(bf16[256,1024]{1,0:T(8,128)(2,1)S(1)} %get-tuple-element.54), channel_id=1, source_target_pairs={{0,1},{1,0},{2,3},{3,2},{4,5},{5,4},{6,7},{7,6},{8,9},{9,8},{10,11... | collective-permute-start | bytes 1572872 | tf_op jit(solution)/shard_map/ppermute | solution.py:20
  199.3 88.5 %collective-permute-start.20 = (bf16[256,1024]{1,0:T(8,128)(2,1)S(1)}, bf16[256,1024]{1,0:T(8,128)(2,1)S(1)}, u32[]{:S(2)}, u32[]{:S(2)}) collective-permute-start(bf16[256,1024]{1,0:T(8,128)(2,1)S(1)} %slice.164), channel_id=1, source_target_pairs={{0,4},{2,6},{4,0},{6,2},{8,12},{10,14},{12,8},{14,10},{17,21},{19,... | collective-permute-start | bytes 1572872 | tf_op jit(solution)/shard_map/ppermute | solution.py:344
  210.0 26.8 %collective-permute-start.17 = (bf16[128,4096]{1,0:T(8,128)(2,1)S(1)}, bf16[128,4096]{1,0:T(8,128)(2,1)S(1)}, u32[]{:S(2)}, u32[]{:S(2)}) collective-permute-start(bf16[128,4096]{1,0:T(8,128)(2,1)S(1)} %collective-permute-done.16), channel_id=1, source_target_pairs={{0,4},{2,6},{4,0},{6,2},{8,12},{10,14},{12,8},{14,10},{16,20},{18,... | collective-permute-start | bytes 3145736 | tf_op jit(solution)/shard_map/ppermute | solution.py:20
  214.9 50.8 %collective-permute-start.23 = (bf16[512,1024]{1,0:T(8,128)(2,1)S(1)}, bf16[512,1024]{1,0:T(8,128)(2,1)S(1)}, u32[]{:S(2)}, u32[]{:S(2)}) collective-permute-start(bf16[512,1024]{1,0:T(8,128)(2,1)S(1)} %convolution_convert_fusion), channel_id=1, source_target_pairs={{1,0},{3,2},{5,4},{7,6},{9,8},{11,10},{13,12},{15,14},{16,17},{18,... | collective-permute-start | bytes 3145736 | tf_op jit(solution)/shard_map/ppermute | solution.py:344
  216.4 25.5 %collective-permute-start.15 = (bf16[128,1024]{1,0:T(8,128)(2,1)S(1)}, bf16[128,1024]{1,0:T(8,128)(2,1)S(1)}, u32[]{:S(2)}, u32[]{:S(2)}) collective-permute-start(bf16[128,1024]{1,0:T(8,128)(2,1)S(1)} %get-tuple-element.43), channel_id=1, source_target_pairs={{0,16},{2,18},{4,20},{6,22},{8,24},{10,26},{12,28},{14,30},{16,0},... | collective-permute-start | bytes 786440 | tf_op jit(solution)/shard_map/ppermute | solution.py:20
  222.1 21.7 %collective-permute-start.21 = (bf16[128,1024]{1,0:T(8,128)(2,1)S(1)}, bf16[128,1024]{1,0:T(8,128)(2,1)S(1)}, u32[]{:S(2)}, u32[]{:S(2)}) collective-permute-start(bf16[128,1024]{1,0:T(8,128)(2,1)S(1)} %get-tuple-element.42), channel_id=1, source_target_pairs={{0,20},{2,22},{4,16},{6,18},{8,28},{10,30},{12,24},{14,26},{16,4},... | collective-permute-start | bytes 786440 | tf_op jit(solution)/shard_map/ppermute | solution.py:20
  241.8 12.5 %collective-permute-start.18 = (bf16[256,1024]{1,0:T(8,128)(2,1)S(1)}, bf16[256,1024]{1,0:T(8,128)(2,1)S(1)}, u32[]{:S(2)}, u32[]{:S(2)}) collective-permute-start(bf16[256,1024]{1,0:T(8,128)(2,1)S(1)} %get-tuple-element.56), channel_id=1, source_target_pairs={{0,1},{1,0},{2,3},{3,2},{4,5},{5,4},{6,7},{7,6},{8,9},{9,8},{10,11... | collective-permute-start | bytes 1572872 | tf_op jit(solution)/shard_map/ppermute | solution.py:20
  243.8 25.8 %collective-permute-start.24 = (bf16[128,2048]{1,0:T(8,128)(2,1)S(1)}, bf16[128,2048]{1,0:T(8,128)(2,1)S(1)}, u32[]{:S(2)}, u32[]{:S(2)}) collective-permute-start(bf16[128,2048]{1,0:T(8,128)(2,1)S(1)} %pad_maximum_fusion.3), channel_id=1, source_target_pairs={{0,1},{2,3},{4,5},{6,7},{8,9},{10,11},{12,13},{14,15},{17,16},{19,... | collective-permute-start | bytes 1572872 | tf_op jit(solution)/shard_map/ppermute | solution.py:344
  254.6 24.2 %collective-permute-start.19 = (bf16[128,1024]{1,0:T(8,128)(2,1)S(1)}, bf16[128,1024]{1,0:T(8,128)(2,1)S(1)}, u32[]{:S(2)}, u32[]{:S(2)}) collective-permute-start(bf16[128,1024]{1,0:T(8,128)(2,1)S(1)} %get-tuple-element.45), channel_id=1, source_target_pairs={{0,16},{2,18},{4,20},{6,22},{8,24},{10,26},{12,28},{14,30},{16,0},... | collective-permute-start | bytes 786440 | tf_op jit(solution)/shard_map/ppermute | solution.py:20
  265.6 18.5 %collective-permute-start.22 = (bf16[128,1024]{1,0:T(8,128)(2,1)S(1)}, bf16[128,1024]{1,0:T(8,128)(2,1)S(1)}, u32[]{:S(2)}, u32[]{:S(2)}) collective-permute-start(bf16[128,1024]{1,0:T(8,128)(2,1)S(1)} %get-tuple-element.44), channel_id=1, source_target_pairs={{0,20},{2,22},{4,16},{6,18},{8,28},{10,30},{12,24},{14,26},{16,4},... | collective-permute-start | bytes 786440 | tf_op jit(solution)/shard_map/ppermute | solution.py:20
  266.1 32.8 %collective-permute-start.26 = (bf16[256,1024]{1,0:T(8,128)(2,1)S(1)}, bf16[256,1024]{1,0:T(8,128)(2,1)S(1)}, u32[]{:S(2)}, u32[]{:S(2)}) collective-permute-start(bf16[256,1024]{1,0:T(8,128)(2,1)S(1)} %slice.179), channel_id=1, source_target_pairs={{0,4},{2,6},{4,0},{6,2},{8,12},{10,14},{12,8},{14,10},{17,21},{19,... | collective-permute-start | bytes 1572872 | tf_op jit(solution)/shard_map/ppermute | solution.py:344
  284.2 14.5 %collective-permute-start.25 = (bf16[128,2048]{1,0:T(8,128)(2,1)S(1)}, bf16[128,2048]{1,0:T(8,128)(2,1)S(1)}, u32[]{:S(2)}, u32[]{:S(2)}) collective-permute-start(bf16[128,2048]{1,0:T(8,128)(2,1)S(1)} %pad_maximum_fusion.4), channel_id=1, source_target_pairs={{0,1},{2,3},{4,5},{6,7},{8,9},{10,11},{12,13},{14,15},{17,16},{19,... | collective-permute-start | bytes 1572872 | tf_op jit(solution)/shard_map/ppermute | solution.py:344
  287.8 11.3 %copy-start.2 = (bf16[512,4096]{1,0:T(8,128)(2,1)S(1)}, bf16[512,4096]{1,0:T(8,128)(2,1)}, u32[]{:S(2)}) copy-start(bf16[512,4096]{1,0:T(8,128)(2,1)} %table_ref.1) | copy-start | bytes 12582916
  299.1 14.0 %copy-start.8 = (s32[256]{0:T(256)S(1)}, s32[256]{0:T(256)}, u32[]{:S(2)}) copy-start(s32[256]{0:T(256)} %param.19) | copy-start | bytes 3076
  305.1 8.0 %collective-permute-start.27 = (bf16[528,256]{1,0:T(8,128)(2,1)S(1)}, bf16[528,256]{1,0:T(8,128)(2,1)S(1)}, u32[]{:S(2)}, u32[]{:S(2)}) collective-permute-start(bf16[528,256]{1,0:T(8,128)(2,1)S(1)} %get-tuple-element.29.first_ref), channel_id=1, source_target_pairs={{0,1},{1,0},{2,3},{3,2},{4,5},{5,4},{6,7},{7,6},{8,9},{9,8},{10,11... | collective-permute-start | bytes 811016 | tf_op jit(solution)/shard_map/ppermute | solution.py:20
  (9 other events, 49.1 us)

commit v5 on v4

--- a/solution.py
+++ b/solution.py
@@ -363,16 +363,18 @@
     second = [tied(jnp.concatenate([above[0], across[0]], axis=0))[0]]
     far_all = jnp.concatenate(far + [xor_permute(piece, "seq", core) for piece in far], axis=1)
 
-    def first_sums(partial):
-        total = added_up(partial, placed_permute(partial, False, 0, 1))
+    def first_sums(partial, *after):
+        other, *_ = tied(placed_permute(partial, False, 0, 1), *after)
+        total = added_up(partial, other)
         return total[:rows], placed_permute(total[rows:], True, side, 0)
 
     def shared(rows_all):
         close, distant = product(rows_all, near), product(rows_all, far_all)
         return jnp.where(here, distant, close), jnp.where(here, close, distant)
 
-    def second_sums(sent, kept):
-        total = added_up(kept, xor_permute(sent, "chan", 1))
+    def second_sums(sent, kept, *after):
+        other, *_ = tied(xor_permute(sent, "chan", 1), *after)
+        total = added_up(kept, other)
         back = [xor_permute(total[:part], "seq", top), xor_permute(total[part:], "seq", top | side)]
         hop = placed_permute(jnp.concatenate(back, axis=1), True, 0, 1)
         return back, jnp.split(hop, 2, axis=1)
@@ -381,9 +383,11 @@
     above[1], *_ = tied(above[1], near_first, *early)
     across.append(xor_permute(above[1], "seq", side))
     second.append(tied(jnp.concatenate([above[1], across[1]], axis=0))[0])
-    sums = [second_sums(*early), second_sums(*shared(second[1]))]
-    near_sums = first_sums(near_first)
-    far_sums = first_sums(product(first, far_all))
+    late = shared(second[1])
+    sums = [second_sums(*early, across[1]), second_sums(*late)]
+    near_sums = first_sums(near_first, across[1])
+    far_first, _ = tied(product(first, far_all), late[0])
+    far_sums = first_sums(far_first)
     blocks = {}
     for half, mask in itertools.product(range(2), (0, side)):
         span = slice(half * block, (half + 1) * block)

time: 315 us -> 298 us (0.946)
  starting transfers between devices: 56.5 us -> 45.5 us
  waiting for transfers between devices: 169 us -> 163 us
    ppermute x21, starting transfers between devices: 38.8 us -> 26.5 us  [xor_permute(): lax.ppermute(value, axis, [(source, source ^ mask) for source in range(co...]
    ppermute x6, waiting for transfers between devices: 23.4 us -> 11.8 us  [placed_permute(): return lax.ppermute(value, ('seq', 'chan'), pairs)]
    ppermute x21, waiting for transfers between devices: 145 us -> 151 us  [xor_permute(): lax.ppermute(value, axis, [(source, source ^ mask) for source in range(co...]
  transfers between devices with their start and end apart: 28 -> 28, of which waited for: 16 -> 16; matrix products, arithmetic and copies ran while one was open for 15% -> 16% of each run, Pallas kernels for 8% -> 8%
where the time goes in v5:
time: 298 us; the launch traced here: 297 us
  waiting for transfers between devices  163 us (55%)
  starting transfers between devices  45.5 us (15%)
  Pallas kernels  31 us (10%)
  local copies, waits for them, and re-layouts  29.1 us (10%)
  matrix products  18.6 us (6%)
  other arithmetic  9.16 us (3%)
    ppermute x21, waiting for transfers between devices, xor_permute(): lax.ppermute(value, axis, [(source, source ^ mask) for source in range(co...  151 us
    ppermute x21, starting transfers between devices, xor_permute(): lax.ppermute(value, axis, [(source, source ^ mask) for source in range(co...  26.5 us
    dot_general x6, matrix products, product(): return jnp.dot(rows, weight, preferred_element_type=F32).astype(BF16)  18.6 us
    ppermute x6, starting transfers between devices, placed_permute(): return lax.ppermute(value, ('seq', 'chan'), pairs)  17 us
    unnamed x32, local copies, waits for them, and re-layouts  16 us
    pallas_call x1, Pallas kernels, gated_rows(): pl.pallas_call(gated_kernel, grid=(width // GROUP,), in_specs=[pl.BlockSp...  13.4 us
    ppermute x6, waiting for transfers between devices, placed_permute(): return lax.ppermute(value, ('seq', 'chan'), pairs)  11.8 us
    pallas_call x1, Pallas kernels, mixed_and_states(): pl.pallas_call(states_kernel, grid=(width // GROUP,), in_specs=[stream(1)...  10.8 us
  transfers between devices with their start and end apart: 28, of which 16 were waited for; matrix products, arithmetic and copies ran while one was open for 16% of the time, Pallas kernels for 8%

profile of v5, /device:TPU:0, one launch (start us, length us, event | category | flops | bytes accessed | tf_op | source)
XLA Modules:
  0.0 297.4 jit_solution(3001071256046758499)
XLA Ops:
  5.4 3.1 %collective-permute-start.3 = (bf16[4096,128]{1,0:T(8,128)(2,1)S(1)}, bf16[4096,128]{1,0:T(8,128)(2,1)S(1)}, u32[]{:S(2)}, u32[]{:S(2)}) collective-permute-start(bf16[4096,128]{1,0:T(8,128)(2,1)S(1)} %slice.120), channel_id=1, source_target_pairs={{0,8},{2,10},{4,12},{6,14},{8,0},{10,2},{12,4},{14,6},{16,24},{18,... | collective-permute-start | bytes 3145736 | tf_op jit(solution)/shard_map/ppermute | solution.py:20
  10.6 2.8 copy-done
  13.4 10.8 %mixed_and_states.1 = (bf16[256,4096]{1,0:T(8,128)(2,1)S(1)}, f32[16,32,128]{2,1,0:T(8,128)S(1)}) custom-call(bf16[3,256,4096]{2,1,0:T(8,128)(2,1)S(1)} %bitcast.60, bf16[3,256,4096]{2,1,0:T(8,128)(2,1)S(1)} %bitcast.61, f32[3,8,4096]{2,1,0:T(8,128)S(1)} %pad_convert_fusion.halo_ref, f32[9,4096]{1,0:T(8,128)S(1)} %reshape.13.taps_ref, ...), custom_call_target="tpu_custom_call" | custom-call | flops 1048576 | bytes 256 | tf_op jit(solution)/shard_map/mixed_and_states/pallas_call | solution.py:132
  30.3 7.1 %collective-permute-done.2 = f32[16,32,128]{2,1,0:T(8,128)} collective-permute-done((f32[16,32,128]{2,1,0:T(8,128)S(1)}, f32[16,32,128]{2,1,0:T(8,128)}, u32[]{:S(2)}, u32[]{:S(2)}) %collective-permute-start.2) | collective-permute-done | bytes 262176 | tf_op jit(solution)/shard_map/ppermute | solution.py:20
  39.0 4.0 %slice.121 = bf16[4096,384]{1,0:T(8,128)(2,1)} slice(bf16[4096,512]{1,0:T(8,128)(2,1)} %param.16), slice={[0:4096], [128:512]} | slice | bytes 6291456 | tf_op jit(solution)/shard_map/slice | solution.py:326
  43.0 3.3 %collective-permute-done.4 = f32[16,32,128]{2,1,0:T(8,128)S(1)} collective-permute-done((f32[16,32,128]{2,1,0:T(8,128)S(1)}, f32[16,32,128]{2,1,0:T(8,128)S(1)}, u32[]{:S(2)}, u32[]{:S(2)}) %collective-permute-start.4) | collective-permute-done | bytes 262176 | tf_op jit(solution)/shard_map/ppermute | solution.py:20
  49.6 10.2 %collective-permute-done.5 = f32[16,32,128]{2,1,0:T(8,128)S(1)} collective-permute-done((f32[16,32,128]{2,1,0:T(8,128)S(1)}, f32[16,32,128]{2,1,0:T(8,128)S(1)}, u32[]{:S(2)}, u32[]{:S(2)}) %collective-permute-start.5) | collective-permute-done | bytes 262176 | tf_op jit(solution)/shard_map/ppermute | solution.py:20
  65.5 13.4 %gated_rows.1 = bf16[256,4096]{1,0:T(8,128)(2,1)S(1)} custom-call(bf16[3,256,4096]{2,1,0:T(8,128)(2,1)S(1)} %bitcast.62, f32[3,8,4096]{2,1,0:T(8,128)S(1)} %pad_convert_fusion.halo_ref, f32[9,4096]{1,0:T(8,128)S(1)} %reshape.13.taps_ref, bf16[256,4096]{1,0:T(8,128)(2,1)S(1)} %copy-done.5, f32[1,4096]{1,0:T(1,128)S(1)} %bitcast.66, ...), custom_call_target="tpu_custom_call" | custom-call | flops 1048576 | bytes 256 | tf_op jit(solution)/shard_map/gated_rows/pallas_call | solution.py:162
  82.1 2.9 constant_dynamic-update-slice_fusion.1
  85.0 3.0 %collective-permute-start.9 = (bf16[128,4096]{1,0:T(8,128)(2,1)S(1)}, bf16[128,4096]{1,0:T(8,128)(2,1)S(1)}, u32[]{:S(2)}, u32[]{:S(2)}) collective-permute-start(bf16[128,4096]{1,0:T(8,128)(2,1)S(1)} %copy-done.11), channel_id=1, source_target_pairs={{0,16},{2,18},{4,20},{6,22},{8,24},{10,26},{12,28},{14,30},{16,0},... | collective-permute-start | bytes 3145736 | tf_op jit(solution)/shard_map/ppermute | solution.py:20
  88.0 57.8 %collective-permute-done.10 = bf16[128,4096]{1,0:T(8,128)(2,1)} collective-permute-done((bf16[128,4096]{1,0:T(8,128)(2,1)}, bf16[128,4096]{1,0:T(8,128)(2,1)}, u32[]{:S(2)}, u32[]{:S(2)}) %collective-permute-start.10) | collective-permute-done | bytes 1048608 | tf_op jit(solution)/shard_map/ppermute | solution.py:20
  146.4 3.1 %constant_dynamic-update-slice_fusion = bf16[4096,1024]{1,0:T(8,128)(2,1)S(1)} fusion(bf16[4096,1024]{1,0:T(8,128)(2,1)S(1)} %constant_dynamic-update-slice_fusion.1, bf16[4096,512]{1,0:T(8,128)(2,1)} %collective-permute-done.6), kind=kLoop, calls=%fused_computation.47 | loop fusion | bytes 8388608 | tf_op jit(solution)/shard_map/concatenate | solution.py:359
  151.6 7.9 %collective-permute-done.12 = bf16[4096,384]{1,0:T(8,128)(2,1)} collective-permute-done((bf16[4096,384]{1,0:T(8,128)(2,1)}, bf16[4096,384]{1,0:T(8,128)(2,1)}, u32[]{:S(2)}, u32[]{:S(2)}) %collective-permute-start.12) | collective-permute-done | bytes 3145760 | tf_op jit(solution)/shard_map/ppermute | solution.py:20
  159.5 7.0 %collective-permute-done.11 = bf16[128,4096]{1,0:T(8,128)(2,1)S(1)} collective-permute-done((bf16[128,4096]{1,0:T(8,128)(2,1)}, bf16[128,4096]{1,0:T(8,128)(2,1)S(1)}, u32[]{:S(2)}, u32[]{:S(2)}) %collective-permute-start.11) | collective-permute-done | bytes 1048608 | tf_op jit(solution)/shard_map/ppermute | solution.py:20
  166.5 4.5 %convolution_convert_fusion.1 = bf16[512,1024]{1,0:T(8,128)(2,1)S(1)} fusion(bf16[512,4096]{1,0:T(8,128)(2,1)S(1)} %pad_maximum_fusion, bf16[4096,1024]{1,0:T(8,128)(2,1)S(1)} %constant_dynamic-update-slice_fusion), kind=kOutput, calls=%fused_computation.6 | convolution fusion | flops 4295491584 | bytes 13631488 | tf_op jit(solution)/shard_map/dot_general | solution.py:330
  174.8 2.8 constant_dynamic-update-slice_fusion.4
  186.4 4.5 %convolution_convert_fusion = bf16[512,1024]{1,0:T(8,128)(2,1)S(1)} fusion(bf16[512,4096]{1,0:T(8,128)(2,1)S(1)} %pad_maximum_fusion, bf16[4096,1024]{1,0:T(8,128)(2,1)S(1)} %constant_dynamic-update-slice_fusion.2), kind=kOutput, calls=%fused_computation.5 | convolution fusion | flops 4295491584 | bytes 13631488 | tf_op jit(solution)/shard_map/dot_general | solution.py:330
  190.9 18.8 %collective-permute-done.16 = bf16[256,1024]{1,0:T(8,128)(2,1)S(1)} collective-permute-done((bf16[256,1024]{1,0:T(8,128)(2,1)S(1)}, bf16[256,1024]{1,0:T(8,128)(2,1)S(1)}, u32[]{:S(2)}, u32[]{:S(2)}) %collective-permute-start.16) | collective-permute-done | bytes 524320 | tf_op jit(solution)/shard_map/ppermute | solution.py:20
  211.5 3.3 %collective-permute-start.17 = (bf16[128,1024]{1,0:T(8,128)(2,1)S(1)}, bf16[128,1024]{1,0:T(8,128)(2,1)S(1)}, u32[]{:S(2)}, u32[]{:S(2)}) collective-permute-start(bf16[128,1024]{1,0:T(8,128)(2,1)S(1)} %get-tuple-element.49), channel_id=1, source_target_pairs={{0,16},{2,18},{4,20},{6,22},{8,24},{10,26},{12,28},{14,30},{16,0},... | collective-permute-start | bytes 786440 | tf_op jit(solution)/shard_map/ppermute | solution.py:20
  223.4 3.5 %collective-permute-start.20 = (bf16[256,1024]{1,0:T(8,128)(2,1)S(1)}, bf16[256,1024]{1,0:T(8,128)(2,1)S(1)}, u32[]{:S(2)}, u32[]{:S(2)}) collective-permute-start(bf16[256,1024]{1,0:T(8,128)(2,1)S(1)} %slice.164), channel_id=1, source_target_pairs={{0,4},{2,6},{4,0},{6,2},{8,12},{10,14},{12,8},{14,10},{17,21},{19,... | collective-permute-start | bytes 1572872 | tf_op jit(solution)/shard_map/ppermute | solution.py:344
  226.9 4.9 %collective-permute-done.17 = bf16[128,1024]{1,0:T(8,128)(2,1)S(1)} collective-permute-done((bf16[128,1024]{1,0:T(8,128)(2,1)S(1)}, bf16[128,1024]{1,0:T(8,128)(2,1)S(1)}, u32[]{:S(2)}, u32[]{:S(2)}) %collective-permute-start.17) | collective-permute-done | bytes 262176 | tf_op jit(solution)/shard_map/ppermute | solution.py:20
  231.8 5.6 %collective-permute-done.21 = bf16[128,1024]{1,0:T(8,128)(2,1)S(1)} collective-permute-done((bf16[128,1024]{1,0:T(8,128)(2,1)S(1)}, bf16[128,1024]{1,0:T(8,128)(2,1)S(1)}, u32[]{:S(2)}, u32[]{:S(2)}) %collective-permute-start.21) | collective-permute-done | bytes 262176 | tf_op jit(solution)/shard_map/ppermute | solution.py:20
  237.4 3.2 %collective-permute-start.24 = (bf16[128,2048]{1,0:T(8,128)(2,1)S(1)}, bf16[128,2048]{1,0:T(8,128)(2,1)S(1)}, u32[]{:S(2)}, u32[]{:S(2)}) collective-permute-start(bf16[128,2048]{1,0:T(8,128)(2,1)S(1)} %pad_maximum_fusion.3), channel_id=1, source_target_pairs={{0,1},{2,3},{4,5},{6,7},{8,9},{10,11},{12,13},{14,15},{17,16},{19,... | collective-permute-start | bytes 1572872 | tf_op jit(solution)/shard_map/ppermute | solution.py:344
  241.0 3.2 %collective-permute-start.22 = (bf16[128,1024]{1,0:T(8,128)(2,1)S(1)}, bf16[128,1024]{1,0:T(8,128)(2,1)S(1)}, u32[]{:S(2)}, u32[]{:S(2)}) collective-permute-start(bf16[128,1024]{1,0:T(8,128)(2,1)S(1)} %get-tuple-element.50), channel_id=1, source_target_pairs={{0,20},{2,22},{4,16},{6,18},{8,28},{10,30},{12,24},{14,26},{16,4},... | collective-permute-start | bytes 786440 | tf_op jit(solution)/shard_map/ppermute | solution.py:20
  244.3 12.4 %collective-permute-done.19 = bf16[128,1024]{1,0:T(8,128)(2,1)S(1)} collective-permute-done((bf16[128,1024]{1,0:T(8,128)(2,1)S(1)}, bf16[128,1024]{1,0:T(8,128)(2,1)S(1)}, u32[]{:S(2)}, u32[]{:S(2)}) %collective-permute-start.19) | collective-permute-done | bytes 262176 | tf_op jit(solution)/shard_map/ppermute | solution.py:20
  256.6 5.9 %collective-permute-done.22 = bf16[128,1024]{1,0:T(8,128)(2,1)S(1)} collective-permute-done((bf16[128,1024]{1,0:T(8,128)(2,1)S(1)}, bf16[128,1024]{1,0:T(8,128)(2,1)S(1)}, u32[]{:S(2)}, u32[]{:S(2)}) %collective-permute-start.22) | collective-permute-done | bytes 262176 | tf_op jit(solution)/shard_map/ppermute | solution.py:20
  262.5 3.9 %collective-permute-start.25 = (bf16[128,2048]{1,0:T(8,128)(2,1)S(1)}, bf16[128,2048]{1,0:T(8,128)(2,1)S(1)}, u32[]{:S(2)}, u32[]{:S(2)}) collective-permute-start(bf16[128,2048]{1,0:T(8,128)(2,1)S(1)} %pad_maximum_fusion.4), channel_id=1, source_target_pairs={{0,1},{2,3},{4,5},{6,7},{8,9},{10,11},{12,13},{14,15},{17,16},{19,... | collective-permute-start | bytes 1572872 | tf_op jit(solution)/shard_map/ppermute | solution.py:344
  267.4 3.7 %collective-permute-start.26 = (bf16[256,1024]{1,0:T(8,128)(2,1)S(1)}, bf16[256,1024]{1,0:T(8,128)(2,1)S(1)}, u32[]{:S(2)}, u32[]{:S(2)}) collective-permute-start(bf16[256,1024]{1,0:T(8,128)(2,1)S(1)} %slice.179), channel_id=1, source_target_pairs={{0,4},{2,6},{4,0},{6,2},{8,12},{10,14},{12,8},{14,10},{17,21},{19,... | collective-permute-start | bytes 1572872 | tf_op jit(solution)/shard_map/ppermute | solution.py:344
  271.1 6.6 %collective-permute-done.25 = bf16[128,2048]{1,0:T(8,128)(2,1)S(1)} collective-permute-done((bf16[128,2048]{1,0:T(8,128)(2,1)S(1)}, bf16[128,2048]{1,0:T(8,128)(2,1)S(1)}, u32[]{:S(2)}, u32[]{:S(2)}) %collective-permute-start.25) | collective-permute-done | bytes 524320 | tf_op jit(solution)/shard_map/ppermute | solution.py:344
  278.0 5.2 %collective-permute-done.26 = bf16[256,1024]{1,0:T(8,128)(2,1)S(1)} collective-permute-done((bf16[256,1024]{1,0:T(8,128)(2,1)S(1)}, bf16[256,1024]{1,0:T(8,128)(2,1)S(1)}, u32[]{:S(2)}, u32[]{:S(2)}) %collective-permute-start.26) | collective-permute-done | bytes 524320 | tf_op jit(solution)/shard_map/ppermute | solution.py:344
  283.4 5.9 %output_rows.1 = (bf16[256,4096]{1,0:T(8,128)(2,1)}, bf16[528,256]{1,0:T(8,128)(2,1)S(1)}) custom-call(s32[8]{0:T(128)S(1)} %iota_xor_fusion.order_ref, bf16[8,256,512]{2,1,0:T(8,128)(2,1)S(1)} %fusion.1.added_ref, bf16[256,4096]{1,0:T(8,128)(2,1)S(1)} %copy-done.3, f32[1,4096]{1,0:T(1,128)S(1)} %bitcast.67, bf16[512,4096]{1,0:T(8,128)(2,1)S(1)} %copy-done.2), custom_call_target="tpu_custom_call" | custom-call | flops 1073741824 | bytes 10485760 | tf_op jit(solution)/shard_map/output_rows/pallas_call | solution.py:253
  289.3 7.2 %collective-permute-done.27.second_ref = bf16[528,256]{1,0:T(8,128)(2,1)S(1)} collective-permute-done((bf16[528,256]{1,0:T(8,128)(2,1)S(1)}, bf16[528,256]{1,0:T(8,128)(2,1)S(1)}, u32[]{:S(2)}, u32[]{:S(2)}) %collective-permute-start.27) | collective-permute-done | bytes 270368 | tf_op jit(solution)/shard_map/ppermute | solution.py:20
  (106 shorter events, 54.6 us)
Async XLA Ops:
  0.6 60.4 %collective-permute-start.6 = (bf16[4096,512]{1,0:T(8,128)(2,1)}, bf16[4096,512]{1,0:T(8,128)(2,1)}, u32[]{:S(2)}, u32[]{:S(2)}) collective-permute-start(bf16[4096,512]{1,0:T(8,128)(2,1)} %param.16), channel_id=1, source_target_pairs={{0,2},{2,0},{4,6},{6,4},{8,10},{10,8},{12,14},{14,12},{16,18},{18,... | collective-permute-start | bytes 12582920 | tf_op jit(solution)/shard_map/ppermute | solution.py:20
  2.1 8.4 %collective-permute-start = (bf16[2,3,4096]{2,0,1:T(2,128)(2,1)S(1)}, bf16[2,3,4096]{2,0,1:T(2,128)(2,1)S(1)}, u32[]{:S(2)}, u32[]{:S(2)}) collective-permute-start(bf16[2,3,4096]{2,0,1:T(2,128)(2,1)S(1)} %slice.119), channel_id=1, source_target_pairs={{0,2},{2,4},{4,6},{6,8},{8,10},{10,12},{12,14},{14,16},{16,18},{18... | collective-permute-start | bytes 147464 | tf_op jit(solution)/shard_map/ppermute | solution.py:26
  5.4 33.0 %collective-permute-start.3 = (bf16[4096,128]{1,0:T(8,128)(2,1)S(1)}, bf16[4096,128]{1,0:T(8,128)(2,1)S(1)}, u32[]{:S(2)}, u32[]{:S(2)}) collective-permute-start(bf16[4096,128]{1,0:T(8,128)(2,1)S(1)} %slice.120), channel_id=1, source_target_pairs={{0,8},{2,10},{4,12},{6,14},{8,0},{10,2},{12,4},{14,6},{16,24},{18,... | collective-permute-start | bytes 3145736 | tf_op jit(solution)/shard_map/ppermute | solution.py:20
  25.5 2.1 collective-permute-start.1
  28.6 8.8 %collective-permute-start.2 = (f32[16,32,128]{2,1,0:T(8,128)S(1)}, f32[16,32,128]{2,1,0:T(8,128)}, u32[]{:S(2)}, u32[]{:S(2)}) collective-permute-start(f32[16,32,128]{2,1,0:T(8,128)S(1)} %multiply_add_fusion.2), channel_id=1, source_target_pairs={{0,4},{2,6},{4,0},{6,2},{8,12},{10,14},{12,8},{14,10},{16,20},{18,... | collective-permute-start | bytes 786440 | tf_op jit(solution)/shard_map/ppermute | solution.py:20
  38.5 7.8 %collective-permute-start.4 = (f32[16,32,128]{2,1,0:T(8,128)S(1)}, f32[16,32,128]{2,1,0:T(8,128)S(1)}, u32[]{:S(2)}, u32[]{:S(2)}) collective-permute-start(f32[16,32,128]{2,1,0:T(8,128)S(1)} %multiply_add_fusion.1), channel_id=1, source_target_pairs={{0,8},{2,10},{4,12},{6,14},{8,0},{10,2},{12,4},{14,6},{16,24},{18,... | collective-permute-start | bytes 786440 | tf_op jit(solution)/shard_map/ppermute | solution.py:20
  43.0 18.1 %copy-start.6 = (f32[4096]{0:T(1024)S(1)}, f32[4096]{0:T(1024)}, u32[]{:S(2)}) copy-start(f32[4096]{0:T(1024)} %param.15) | copy-start | bytes 49156
  46.4 13.4 %collective-permute-start.5 = (f32[16,32,128]{2,1,0:T(8,128)S(1)}, f32[16,32,128]{2,1,0:T(8,128)S(1)}, u32[]{:S(2)}, u32[]{:S(2)}) collective-permute-start(f32[16,32,128]{2,1,0:T(8,128)S(1)} %multiply_add_fusion), channel_id=1, source_target_pairs={{0,16},{2,18},{4,20},{6,22},{8,24},{10,26},{12,28},{14,30},{16,0},... | collective-permute-start | bytes 786440 | tf_op jit(solution)/shard_map/ppermute | solution.py:20
  49.1 110.4 %collective-permute-start.12 = (bf16[4096,384]{1,0:T(8,128)(2,1)}, bf16[4096,384]{1,0:T(8,128)(2,1)}, u32[]{:S(2)}, u32[]{:S(2)}) collective-permute-start(bf16[4096,384]{1,0:T(8,128)(2,1)} %slice.121), channel_id=1, source_target_pairs={{0,8},{2,10},{4,12},{6,14},{8,0},{10,2},{12,4},{14,6},{16,24},{18,... | collective-permute-start | bytes 9437192 | tf_op jit(solution)/shard_map/ppermute | solution.py:20
  78.9 70.6 %collective-permute-start.7 = (bf16[256,4096]{1,0:T(8,128)(2,1)S(1)}, bf16[256,4096]{1,0:T(8,128)(2,1)}, u32[]{:S(2)}, u32[]{:S(2)}) collective-permute-start(bf16[256,4096]{1,0:T(8,128)(2,1)S(1)} %gated_rows.1), channel_id=1, source_target_pairs={{0,4},{2,6},{4,0},{6,2},{8,12},{10,14},{12,8},{14,10},{16,20},{18,... | collective-permute-start | bytes 6291464 | tf_op jit(solution)/shard_map/ppermute | solution.py:20
  82.1 63.8 %collective-permute-start.10 = (bf16[128,4096]{1,0:T(8,128)(2,1)}, bf16[128,4096]{1,0:T(8,128)(2,1)}, u32[]{:S(2)}, u32[]{:S(2)}) collective-permute-start(bf16[128,4096]{1,0:T(8,128)(2,1)} %get-tuple-element.36), channel_id=1, source_target_pairs={{0,16},{2,18},{4,20},{6,22},{8,24},{10,26},{12,28},{14,30},{16,0},... | collective-permute-start | bytes 3145736 | tf_op jit(solution)/shard_map/ppermute | solution.py:20
  85.0 101.1 %collective-permute-start.9 = (bf16[128,4096]{1,0:T(8,128)(2,1)S(1)}, bf16[128,4096]{1,0:T(8,128)(2,1)S(1)}, u32[]{:S(2)}, u32[]{:S(2)}) collective-permute-start(bf16[128,4096]{1,0:T(8,128)(2,1)S(1)} %copy-done.11), channel_id=1, source_target_pairs={{0,16},{2,18},{4,20},{6,22},{8,24},{10,26},{12,28},{14,30},{16,0},... | collective-permute-start | bytes 3145736 | tf_op jit(solution)/shard_map/ppermute | solution.py:20
  145.8 20.7 %collective-permute-start.11 = (bf16[128,4096]{1,0:T(8,128)(2,1)}, bf16[128,4096]{1,0:T(8,128)(2,1)S(1)}, u32[]{:S(2)}, u32[]{:S(2)}) collective-permute-start(bf16[128,4096]{1,0:T(8,128)(2,1)} %collective-permute-done.10), channel_id=1, source_target_pairs={{0,4},{2,6},{4,0},{6,2},{8,12},{10,14},{12,8},{14,10},{16,20},{18,... | collective-permute-start | bytes 3145736 | tf_op jit(solution)/shard_map/ppermute | solution.py:20
  151.6 20.9 %copy-start.10 = (bf16[4096,128]{1,0:T(8,128)(2,1)S(1)}, bf16[4096,128]{1,0:T(8,128)(2,1)}, u32[]{:S(2)}) copy-start(bf16[4096,128]{1,0:T(8,128)(2,1)} %copy-done.9) | copy-start | bytes 3145732
  166.5 11.5 %collective-permute-start.14 = (bf16[4096,384]{1,0:T(8,128)(2,1)}, bf16[4096,384]{1,0:T(8,128)(2,1)S(1)}, u32[]{:S(2)}, u32[]{:S(2)}) collective-permute-start(bf16[4096,384]{1,0:T(8,128)(2,1)} %collective-permute-done.12), channel_id=1, source_target_pairs={{0,2},{2,0},{4,6},{6,4},{8,10},{10,8},{12,14},{14,12},{16,18},{18,... | collective-permute-start | bytes 9437192 | tf_op jit(solution)/shard_map/ppermute | solution.py:20
  171.0 52.0 %collective-permute-start.8 = (bf16[512,1024]{1,0:T(8,128)(2,1)S(1)}, bf16[512,1024]{1,0:T(8,128)(2,1)S(1)}, u32[]{:S(2)}, u32[]{:S(2)}) collective-permute-start(bf16[512,1024]{1,0:T(8,128)(2,1)S(1)} %convolution_convert_fusion.1), channel_id=1, source_target_pairs={{1,0},{3,2},{5,4},{7,6},{9,8},{11,10},{13,12},{15,14},{16,17},{18,... | collective-permute-start | bytes 3145736 | tf_op jit(solution)/shard_map/ppermute | solution.py:344
  172.5 5.1 %collective-permute-start.13 = (bf16[4096,128]{1,0:T(8,128)(2,1)S(1)}, bf16[4096,128]{1,0:T(8,128)(2,1)S(1)}, u32[]{:S(2)}, u32[]{:S(2)}) collective-permute-start(bf16[4096,128]{1,0:T(8,128)(2,1)S(1)} %copy-done.10), channel_id=1, source_target_pairs={{0,2},{2,0},{4,6},{6,4},{8,10},{10,8},{12,14},{14,12},{16,18},{18,... | collective-permute-start | bytes 3145736 | tf_op jit(solution)/shard_map/ppermute | solution.py:20
  183.7 26.1 %collective-permute-start.16 = (bf16[256,1024]{1,0:T(8,128)(2,1)S(1)}, bf16[256,1024]{1,0:T(8,128)(2,1)S(1)}, u32[]{:S(2)}, u32[]{:S(2)}) collective-permute-start(bf16[256,1024]{1,0:T(8,128)(2,1)S(1)} %get-tuple-element.39), channel_id=1, source_target_pairs={{0,1},{1,0},{2,3},{3,2},{4,5},{5,4},{6,7},{7,6},{8,9},{9,8},{10,11... | collective-permute-start | bytes 1572872 | tf_op jit(solution)/shard_map/ppermute | solution.py:20
  186.2 25.1 %collective-permute-start.15 = (bf16[128,4096]{1,0:T(8,128)(2,1)S(1)}, bf16[128,4096]{1,0:T(8,128)(2,1)S(1)}, u32[]{:S(2)}, u32[]{:S(2)}) collective-permute-start(bf16[128,4096]{1,0:T(8,128)(2,1)S(1)} %collective-permute-done.9), channel_id=1, source_target_pairs={{0,4},{2,6},{4,0},{6,2},{8,12},{10,14},{12,8},{14,10},{16,20},{18,... | collective-permute-start | bytes 3145736 | tf_op jit(solution)/shard_map/ppermute | solution.py:20
  211.5 20.3 %collective-permute-start.17 = (bf16[128,1024]{1,0:T(8,128)(2,1)S(1)}, bf16[128,1024]{1,0:T(8,128)(2,1)S(1)}, u32[]{:S(2)}, u32[]{:S(2)}) collective-permute-start(bf16[128,1024]{1,0:T(8,128)(2,1)S(1)} %get-tuple-element.49), channel_id=1, source_target_pairs={{0,16},{2,18},{4,20},{6,22},{8,24},{10,26},{12,28},{14,30},{16,0},... | collective-permute-start | bytes 786440 | tf_op jit(solution)/shard_map/ppermute | solution.py:20
  214.8 22.6 %collective-permute-start.21 = (bf16[128,1024]{1,0:T(8,128)(2,1)S(1)}, bf16[128,1024]{1,0:T(8,128)(2,1)S(1)}, u32[]{:S(2)}, u32[]{:S(2)}) collective-permute-start(bf16[128,1024]{1,0:T(8,128)(2,1)S(1)} %get-tuple-element.48), channel_id=1, source_target_pairs={{0,20},{2,22},{4,16},{6,18},{8,28},{10,30},{12,24},{14,26},{16,4},... | collective-permute-start | bytes 786440 | tf_op jit(solution)/shard_map/ppermute | solution.py:20
  220.0 20.6 %collective-permute-start.18 = (bf16[256,1024]{1,0:T(8,128)(2,1)S(1)}, bf16[256,1024]{1,0:T(8,128)(2,1)S(1)}, u32[]{:S(2)}, u32[]{:S(2)}) collective-permute-start(bf16[256,1024]{1,0:T(8,128)(2,1)S(1)} %get-tuple-element.60), channel_id=1, source_target_pairs={{0,1},{1,0},{2,3},{3,2},{4,5},{5,4},{6,7},{7,6},{8,9},{9,8},{10,11... | collective-permute-start | bytes 1572872 | tf_op jit(solution)/shard_map/ppermute | solution.py:20
  221.7 45.2 %collective-permute-start.23 = (bf16[512,1024]{1,0:T(8,128)(2,1)S(1)}, bf16[512,1024]{1,0:T(8,128)(2,1)S(1)}, u32[]{:S(2)}, u32[]{:S(2)}) collective-permute-start(bf16[512,1024]{1,0:T(8,128)(2,1)S(1)} %convolution_convert_fusion), channel_id=1, source_target_pairs={{1,0},{3,2},{5,4},{7,6},{9,8},{11,10},{13,12},{15,14},{16,17},{18,... | collective-permute-start | bytes 3145736 | tf_op jit(solution)/shard_map/ppermute | solution.py:344
  223.4 43.2 %collective-permute-start.20 = (bf16[256,1024]{1,0:T(8,128)(2,1)S(1)}, bf16[256,1024]{1,0:T(8,128)(2,1)S(1)}, u32[]{:S(2)}, u32[]{:S(2)}) collective-permute-start(bf16[256,1024]{1,0:T(8,128)(2,1)S(1)} %slice.164), channel_id=1, source_target_pairs={{0,4},{2,6},{4,0},{6,2},{8,12},{10,14},{12,8},{14,10},{17,21},{19,... | collective-permute-start | bytes 1572872 | tf_op jit(solution)/shard_map/ppermute | solution.py:344
  237.4 29.3 %collective-permute-start.24 = (bf16[128,2048]{1,0:T(8,128)(2,1)S(1)}, bf16[128,2048]{1,0:T(8,128)(2,1)S(1)}, u32[]{:S(2)}, u32[]{:S(2)}) collective-permute-start(bf16[128,2048]{1,0:T(8,128)(2,1)S(1)} %pad_maximum_fusion.3), channel_id=1, source_target_pairs={{0,1},{2,3},{4,5},{6,7},{8,9},{10,11},{12,13},{14,15},{17,16},{19,... | collective-permute-start | bytes 1572872 | tf_op jit(solution)/shard_map/ppermute | solution.py:344
  240.9 15.7 %collective-permute-start.19 = (bf16[128,1024]{1,0:T(8,128)(2,1)S(1)}, bf16[128,1024]{1,0:T(8,128)(2,1)S(1)}, u32[]{:S(2)}, u32[]{:S(2)}) collective-permute-start(bf16[128,1024]{1,0:T(8,128)(2,1)S(1)} %get-tuple-element.51), channel_id=1, source_target_pairs={{0,16},{2,18},{4,20},{6,22},{8,24},{10,26},{12,28},{14,30},{16,0},... | collective-permute-start | bytes 786440 | tf_op jit(solution)/shard_map/ppermute | solution.py:20
  241.0 21.5 %collective-permute-start.22 = (bf16[128,1024]{1,0:T(8,128)(2,1)S(1)}, bf16[128,1024]{1,0:T(8,128)(2,1)S(1)}, u32[]{:S(2)}, u32[]{:S(2)}) collective-permute-start(bf16[128,1024]{1,0:T(8,128)(2,1)S(1)} %get-tuple-element.50), channel_id=1, source_target_pairs={{0,20},{2,22},{4,16},{6,18},{8,28},{10,30},{12,24},{14,26},{16,4},... | collective-permute-start | bytes 786440 | tf_op jit(solution)/shard_map/ppermute | solution.py:20
  262.5 15.2 %collective-permute-start.25 = (bf16[128,2048]{1,0:T(8,128)(2,1)S(1)}, bf16[128,2048]{1,0:T(8,128)(2,1)S(1)}, u32[]{:S(2)}, u32[]{:S(2)}) collective-permute-start(bf16[128,2048]{1,0:T(8,128)(2,1)S(1)} %pad_maximum_fusion.4), channel_id=1, source_target_pairs={{0,1},{2,3},{4,5},{6,7},{8,9},{10,11},{12,13},{14,15},{17,16},{19,... | collective-permute-start | bytes 1572872 | tf_op jit(solution)/shard_map/ppermute | solution.py:344
  266.9 16.4 %copy-start.3 = (bf16[256,4096]{1,0:T(8,128)(2,1)S(1)}, bf16[256,4096]{1,0:T(8,128)(2,1)}, u32[]{:S(2)}) copy-start(bf16[256,4096]{1,0:T(8,128)(2,1)} %residual_ref.1) | copy-start | bytes 6291460
  267.3 16.0 %copy-start.2 = (bf16[512,4096]{1,0:T(8,128)(2,1)S(1)}, bf16[512,4096]{1,0:T(8,128)(2,1)}, u32[]{:S(2)}) copy-start(bf16[512,4096]{1,0:T(8,128)(2,1)} %table_ref.1) | copy-start | bytes 12582916
  267.4 15.7 %collective-permute-start.26 = (bf16[256,1024]{1,0:T(8,128)(2,1)S(1)}, bf16[256,1024]{1,0:T(8,128)(2,1)S(1)}, u32[]{:S(2)}, u32[]{:S(2)}) collective-permute-start(bf16[256,1024]{1,0:T(8,128)(2,1)S(1)} %slice.179), channel_id=1, source_target_pairs={{0,4},{2,6},{4,0},{6,2},{8,12},{10,14},{12,8},{14,10},{17,21},{19,... | collective-permute-start | bytes 1572872 | tf_op jit(solution)/shard_map/ppermute | solution.py:344
  289.3 7.2 %collective-permute-start.27 = (bf16[528,256]{1,0:T(8,128)(2,1)S(1)}, bf16[528,256]{1,0:T(8,128)(2,1)S(1)}, u32[]{:S(2)}, u32[]{:S(2)}) collective-permute-start(bf16[528,256]{1,0:T(8,128)(2,1)S(1)} %get-tuple-element.35.first_ref), channel_id=1, source_target_pairs={{0,1},{1,0},{2,3},{3,2},{4,5},{5,4},{6,7},{7,6},{8,9},{9,8},{10,11... | collective-permute-start | bytes 811016 | tf_op jit(solution)/shard_map/ppermute | solution.py:20
  (9 other events, 55.7 us)

commit v6 on v5

--- a/solution.py
+++ b/solution.py
@@ -384,7 +384,7 @@
     across.append(xor_permute(above[1], "seq", side))
     second.append(tied(jnp.concatenate([above[1], across[1]], axis=0))[0])
     late = shared(second[1])
-    sums = [second_sums(*early, across[1]), second_sums(*late)]
+    sums = [second_sums(*early, late[0]), second_sums(*late)]
     near_sums = first_sums(near_first, across[1])
     far_first, _ = tied(product(first, far_all), late[0])
     far_sums = first_sums(far_first)

time: 298 us -> 304 us (1.020)
  waiting for transfers between devices: 163 us -> 169 us
    ppermute x21, waiting for transfers between devices: 151 us -> 157 us  [xor_permute(): lax.ppermute(value, axis, [(source, source ^ mask) for source in range(co...]
  transfers between devices with their start and end apart: 28 -> 28, of which waited for: 16 -> 15; matrix products, arithmetic and copies ran while one was open for 16% -> 16% of each run, Pallas kernels for 8% -> 8%
where the time goes in v6:
time: 304 us; the launch traced here: 303 us
  waiting for transfers between devices  169 us (56%)
  starting transfers between devices  44.8 us (15%)
  Pallas kernels  30.9 us (10%)
  local copies, waits for them, and re-layouts  29.1 us (10%)
  matrix products  18.6 us (6%)
  other arithmetic  9.16 us (3%)
    ppermute x21, waiting for transfers between devices, xor_permute(): lax.ppermute(value, axis, [(source, source ^ mask) for source in range(co...  157 us
    ppermute x21, starting transfers between devices, xor_permute(): lax.ppermute(value, axis, [(source, source ^ mask) for source in range(co...  27.2 us
    dot_general x6, matrix products, product(): return jnp.dot(rows, weight, preferred_element_type=F32).astype(BF16)  18.6 us
    unnamed x32, local copies, waits for them, and re-layouts  16 us
    ppermute x6, starting transfers between devices, placed_permute(): return lax.ppermute(value, ('seq', 'chan'), pairs)  15.6 us
    pallas_call x1, Pallas kernels, gated_rows(): pl.pallas_call(gated_kernel, grid=(width // GROUP,), in_specs=[pl.BlockSp...  13.4 us
    ppermute x6, waiting for transfers between devices, placed_permute(): return lax.ppermute(value, ('seq', 'chan'), pairs)  12 us
    pallas_call x1, Pallas kernels, mixed_and_states(): pl.pallas_call(states_kernel, grid=(width // GROUP,), in_specs=[stream(1)...  10.8 us
  transfers between devices with their start and end apart: 28, of which 15 were waited for; matrix products, arithmetic and copies ran while one was open for 16% of the time, Pallas kernels for 8%

profile of v6, /device:TPU:0, one launch (start us, length us, event | category | flops | bytes accessed | tf_op | source)
XLA Modules:
  0.0 302.8 jit_solution(14431124420953913490)
XLA Ops:
  5.4 3.1 %collective-permute-start.3 = (bf16[4096,128]{1,0:T(8,128)(2,1)S(1)}, bf16[4096,128]{1,0:T(8,128)(2,1)S(1)}, u32[]{:S(2)}, u32[]{:S(2)}) collective-permute-start(bf16[4096,128]{1,0:T(8,128)(2,1)S(1)} %slice.120), channel_id=1, source_target_pairs={{0,8},{2,10},{4,12},{6,14},{8,0},{10,2},{12,4},{14,6},{16,24},{18,... | collective-permute-start | bytes 3145736 | tf_op jit(solution)/shard_map/ppermute | solution.py:20
  10.6 2.8 copy-done
  13.4 10.8 %mixed_and_states.1 = (bf16[256,4096]{1,0:T(8,128)(2,1)S(1)}, f32[16,32,128]{2,1,0:T(8,128)S(1)}) custom-call(bf16[3,256,4096]{2,1,0:T(8,128)(2,1)S(1)} %bitcast.60, bf16[3,256,4096]{2,1,0:T(8,128)(2,1)S(1)} %bitcast.61, f32[3,8,4096]{2,1,0:T(8,128)S(1)} %pad_convert_fusion.halo_ref, f32[9,4096]{1,0:T(8,128)S(1)} %reshape.13.taps_ref, ...), custom_call_target="tpu_custom_call" | custom-call | flops 1048576 | bytes 256 | tf_op jit(solution)/shard_map/mixed_and_states/pallas_call | solution.py:132
  30.3 7.1 %collective-permute-done.2 = f32[16,32,128]{2,1,0:T(8,128)} collective-permute-done((f32[16,32,128]{2,1,0:T(8,128)S(1)}, f32[16,32,128]{2,1,0:T(8,128)}, u32[]{:S(2)}, u32[]{:S(2)}) %collective-permute-start.2) | collective-permute-done | bytes 262176 | tf_op jit(solution)/shard_map/ppermute | solution.py:20
  39.0 4.0 %slice.121 = bf16[4096,384]{1,0:T(8,128)(2,1)} slice(bf16[4096,512]{1,0:T(8,128)(2,1)} %param.16), slice={[0:4096], [128:512]} | slice | bytes 6291456 | tf_op jit(solution)/shard_map/slice | solution.py:326
  43.0 3.3 %collective-permute-done.4 = f32[16,32,128]{2,1,0:T(8,128)S(1)} collective-permute-done((f32[16,32,128]{2,1,0:T(8,128)S(1)}, f32[16,32,128]{2,1,0:T(8,128)S(1)}, u32[]{:S(2)}, u32[]{:S(2)}) %collective-permute-start.4) | collective-permute-done | bytes 262176 | tf_op jit(solution)/shard_map/ppermute | solution.py:20
  49.6 10.2 %collective-permute-done.5 = f32[16,32,128]{2,1,0:T(8,128)S(1)} collective-permute-done((f32[16,32,128]{2,1,0:T(8,128)S(1)}, f32[16,32,128]{2,1,0:T(8,128)S(1)}, u32[]{:S(2)}, u32[]{:S(2)}) %collective-permute-start.5) | collective-permute-done | bytes 262176 | tf_op jit(solution)/shard_map/ppermute | solution.py:20
  61.1 2.8 copy-done.1
  65.5 13.4 %gated_rows.1 = bf16[256,4096]{1,0:T(8,128)(2,1)S(1)} custom-call(bf16[3,256,4096]{2,1,0:T(8,128)(2,1)S(1)} %bitcast.62, f32[3,8,4096]{2,1,0:T(8,128)S(1)} %pad_convert_fusion.halo_ref, f32[9,4096]{1,0:T(8,128)S(1)} %reshape.13.taps_ref, bf16[256,4096]{1,0:T(8,128)(2,1)S(1)} %copy-done.5, f32[1,4096]{1,0:T(1,128)S(1)} %bitcast.66, ...), custom_call_target="tpu_custom_call" | custom-call | flops 1048576 | bytes 256 | tf_op jit(solution)/shard_map/gated_rows/pallas_call | solution.py:162
  82.1 2.9 constant_dynamic-update-slice_fusion.1
  85.0 3.0 collective-permute-start.9
  88.0 57.8 %collective-permute-done.10 = bf16[128,4096]{1,0:T(8,128)(2,1)} collective-permute-done((bf16[128,4096]{1,0:T(8,128)(2,1)}, bf16[128,4096]{1,0:T(8,128)(2,1)}, u32[]{:S(2)}, u32[]{:S(2)}) %collective-permute-start.10) | collective-permute-done | bytes 1048608 | tf_op jit(solution)/shard_map/ppermute | solution.py:20
  146.4 3.1 %constant_dynamic-update-slice_fusion = bf16[4096,1024]{1,0:T(8,128)(2,1)S(1)} fusion(bf16[4096,1024]{1,0:T(8,128)(2,1)S(1)} %constant_dynamic-update-slice_fusion.1, bf16[4096,512]{1,0:T(8,128)(2,1)} %collective-permute-done.6), kind=kLoop, calls=%fused_computation.47 | loop fusion | bytes 8388608 | tf_op jit(solution)/shard_map/concatenate | solution.py:359
  151.6 7.9 %collective-permute-done.12 = bf16[4096,384]{1,0:T(8,128)(2,1)} collective-permute-done((bf16[4096,384]{1,0:T(8,128)(2,1)}, bf16[4096,384]{1,0:T(8,128)(2,1)}, u32[]{:S(2)}, u32[]{:S(2)}) %collective-permute-start.12) | collective-permute-done | bytes 3145760 | tf_op jit(solution)/shard_map/ppermute | solution.py:20
  159.5 7.0 %collective-permute-done.11 = bf16[128,4096]{1,0:T(8,128)(2,1)S(1)} collective-permute-done((bf16[128,4096]{1,0:T(8,128)(2,1)}, bf16[128,4096]{1,0:T(8,128)(2,1)S(1)}, u32[]{:S(2)}, u32[]{:S(2)}) %collective-permute-start.11) | collective-permute-done | bytes 1048608 | tf_op jit(solution)/shard_map/ppermute | solution.py:20
  166.5 4.5 %convolution_convert_fusion.1 = bf16[512,1024]{1,0:T(8,128)(2,1)S(1)} fusion(bf16[512,4096]{1,0:T(8,128)(2,1)S(1)} %pad_maximum_fusion, bf16[4096,1024]{1,0:T(8,128)(2,1)S(1)} %constant_dynamic-update-slice_fusion), kind=kOutput, calls=%fused_computation.6 | convolution fusion | flops 4295491584 | bytes 13631488 | tf_op jit(solution)/shard_map/dot_general | solution.py:330
  174.8 2.8 constant_dynamic-update-slice_fusion.4
  186.4 4.5 %convolution_convert_fusion = bf16[512,1024]{1,0:T(8,128)(2,1)S(1)} fusion(bf16[512,4096]{1,0:T(8,128)(2,1)S(1)} %pad_maximum_fusion, bf16[4096,1024]{1,0:T(8,128)(2,1)S(1)} %constant_dynamic-update-slice_fusion.2), kind=kOutput, calls=%fused_computation.5 | convolution fusion | flops 4295491584 | bytes 13631488 | tf_op jit(solution)/shard_map/dot_general | solution.py:330
  190.9 20.3 %collective-permute-done.15 = bf16[128,4096]{1,0:T(8,128)(2,1)S(1)} collective-permute-done((bf16[128,4096]{1,0:T(8,128)(2,1)S(1)}, bf16[128,4096]{1,0:T(8,128)(2,1)S(1)}, u32[]{:S(2)}, u32[]{:S(2)}) %collective-permute-start.15) | collective-permute-done | bytes 1048608 | tf_op jit(solution)/shard_map/ppermute | solution.py:20
  217.1 4.6 %collective-permute-start.17 = (bf16[128,1024]{1,0:T(8,128)(2,1)S(1)}, bf16[128,1024]{1,0:T(8,128)(2,1)S(1)}, u32[]{:S(2)}, u32[]{:S(2)}) collective-permute-start(bf16[128,1024]{1,0:T(8,128)(2,1)S(1)} %get-tuple-element.49), channel_id=1, source_target_pairs={{0,16},{2,18},{4,20},{6,22},{8,24},{10,26},{12,28},{14,30},{16,0},... | collective-permute-start | bytes 786440 | tf_op jit(solution)/shard_map/ppermute | solution.py:20
  223.5 3.4 %collective-permute-start.20 = (bf16[256,1024]{1,0:T(8,128)(2,1)S(1)}, bf16[256,1024]{1,0:T(8,128)(2,1)S(1)}, u32[]{:S(2)}, u32[]{:S(2)}) collective-permute-start(bf16[256,1024]{1,0:T(8,128)(2,1)S(1)} %slice.164), channel_id=1, source_target_pairs={{0,4},{2,6},{4,0},{6,2},{8,12},{10,14},{12,8},{14,10},{17,21},{19,... | collective-permute-start | bytes 1572872 | tf_op jit(solution)/shard_map/ppermute | solution.py:344
  226.9 10.6 %collective-permute-done.17 = bf16[128,1024]{1,0:T(8,128)(2,1)S(1)} collective-permute-done((bf16[128,1024]{1,0:T(8,128)(2,1)S(1)}, bf16[128,1024]{1,0:T(8,128)(2,1)S(1)}, u32[]{:S(2)}, u32[]{:S(2)}) %collective-permute-start.17) | collective-permute-done | bytes 262176 | tf_op jit(solution)/shard_map/ppermute | solution.py:20
  237.5 6.1 %collective-permute-done.21 = bf16[128,1024]{1,0:T(8,128)(2,1)S(1)} collective-permute-done((bf16[128,1024]{1,0:T(8,128)(2,1)S(1)}, bf16[128,1024]{1,0:T(8,128)(2,1)S(1)}, u32[]{:S(2)}, u32[]{:S(2)}) %collective-permute-start.21) | collective-permute-done | bytes 262176 | tf_op jit(solution)/shard_map/ppermute | solution.py:20
  246.7 3.9 %collective-permute-start.22 = (bf16[128,1024]{1,0:T(8,128)(2,1)S(1)}, bf16[128,1024]{1,0:T(8,128)(2,1)S(1)}, u32[]{:S(2)}, u32[]{:S(2)}) collective-permute-start(bf16[128,1024]{1,0:T(8,128)(2,1)S(1)} %get-tuple-element.50), channel_id=1, source_target_pairs={{0,20},{2,22},{4,16},{6,18},{8,28},{10,30},{12,24},{14,26},{16,4},... | collective-permute-start | bytes 786440 | tf_op jit(solution)/shard_map/ppermute | solution.py:20
  250.6 11.4 %collective-permute-done.19 = bf16[128,1024]{1,0:T(8,128)(2,1)S(1)} collective-permute-done((bf16[128,1024]{1,0:T(8,128)(2,1)S(1)}, bf16[128,1024]{1,0:T(8,128)(2,1)S(1)}, u32[]{:S(2)}, u32[]{:S(2)}) %collective-permute-start.19) | collective-permute-done | bytes 262176 | tf_op jit(solution)/shard_map/ppermute | solution.py:20
  262.0 6.5 %collective-permute-done.22 = bf16[128,1024]{1,0:T(8,128)(2,1)S(1)} collective-permute-done((bf16[128,1024]{1,0:T(8,128)(2,1)S(1)}, bf16[128,1024]{1,0:T(8,128)(2,1)S(1)}, u32[]{:S(2)}, u32[]{:S(2)}) %collective-permute-start.22) | collective-permute-done | bytes 262176 | tf_op jit(solution)/shard_map/ppermute | solution.py:20
  268.6 3.3 %collective-permute-start.25 = (bf16[128,2048]{1,0:T(8,128)(2,1)S(1)}, bf16[128,2048]{1,0:T(8,128)(2,1)S(1)}, u32[]{:S(2)}, u32[]{:S(2)}) collective-permute-start(bf16[128,2048]{1,0:T(8,128)(2,1)S(1)} %pad_maximum_fusion.4), channel_id=1, source_target_pairs={{0,1},{2,3},{4,5},{6,7},{8,9},{10,11},{12,13},{14,15},{17,16},{19,... | collective-permute-start | bytes 1572872 | tf_op jit(solution)/shard_map/ppermute | solution.py:344
  272.8 3.5 %collective-permute-start.26 = (bf16[256,1024]{1,0:T(8,128)(2,1)S(1)}, bf16[256,1024]{1,0:T(8,128)(2,1)S(1)}, u32[]{:S(2)}, u32[]{:S(2)}) collective-permute-start(bf16[256,1024]{1,0:T(8,128)(2,1)S(1)} %slice.179), channel_id=1, source_target_pairs={{0,4},{2,6},{4,0},{6,2},{8,12},{10,14},{12,8},{14,10},{17,21},{19,... | collective-permute-start | bytes 1572872 | tf_op jit(solution)/shard_map/ppermute | solution.py:344
  276.4 6.8 %collective-permute-done.25 = bf16[128,2048]{1,0:T(8,128)(2,1)S(1)} collective-permute-done((bf16[128,2048]{1,0:T(8,128)(2,1)S(1)}, bf16[128,2048]{1,0:T(8,128)(2,1)S(1)}, u32[]{:S(2)}, u32[]{:S(2)}) %collective-permute-start.25) | collective-permute-done | bytes 524320 | tf_op jit(solution)/shard_map/ppermute | solution.py:344
  283.4 5.2 %collective-permute-done.26 = bf16[256,1024]{1,0:T(8,128)(2,1)S(1)} collective-permute-done((bf16[256,1024]{1,0:T(8,128)(2,1)S(1)}, bf16[256,1024]{1,0:T(8,128)(2,1)S(1)}, u32[]{:S(2)}, u32[]{:S(2)}) %collective-permute-start.26) | collective-permute-done | bytes 524320 | tf_op jit(solution)/shard_map/ppermute | solution.py:344
  288.8 5.9 %output_rows.1 = (bf16[256,4096]{1,0:T(8,128)(2,1)}, bf16[528,256]{1,0:T(8,128)(2,1)S(1)}) custom-call(s32[8]{0:T(128)S(1)} %iota_xor_fusion.order_ref, bf16[8,256,512]{2,1,0:T(8,128)(2,1)S(1)} %fusion.1.added_ref, bf16[256,4096]{1,0:T(8,128)(2,1)S(1)} %copy-done.3, f32[1,4096]{1,0:T(1,128)S(1)} %bitcast.67, bf16[512,4096]{1,0:T(8,128)(2,1)S(1)} %copy-done.2), custom_call_target="tpu_custom_call" | custom-call | flops 1073741824 | bytes 10485760 | tf_op jit(solution)/shard_map/output_rows/pallas_call | solution.py:253
  294.7 7.2 %collective-permute-done.27.second_ref = bf16[528,256]{1,0:T(8,128)(2,1)S(1)} collective-permute-done((bf16[528,256]{1,0:T(8,128)(2,1)S(1)}, bf16[528,256]{1,0:T(8,128)(2,1)S(1)}, u32[]{:S(2)}, u32[]{:S(2)}) %collective-permute-start.27) | collective-permute-done | bytes 270368 | tf_op jit(solution)/shard_map/ppermute | solution.py:20
  (106 shorter events, 51.7 us)
Async XLA Ops:
  0.6 60.4 %collective-permute-start.6 = (bf16[4096,512]{1,0:T(8,128)(2,1)}, bf16[4096,512]{1,0:T(8,128)(2,1)}, u32[]{:S(2)}, u32[]{:S(2)}) collective-permute-start(bf16[4096,512]{1,0:T(8,128)(2,1)} %param.16), channel_id=1, source_target_pairs={{0,2},{2,0},{4,6},{6,4},{8,10},{10,8},{12,14},{14,12},{16,18},{18,... | collective-permute-start | bytes 12582920 | tf_op jit(solution)/shard_map/ppermute | solution.py:20
  2.1 8.4 %collective-permute-start = (bf16[2,3,4096]{2,0,1:T(2,128)(2,1)S(1)}, bf16[2,3,4096]{2,0,1:T(2,128)(2,1)S(1)}, u32[]{:S(2)}, u32[]{:S(2)}) collective-permute-start(bf16[2,3,4096]{2,0,1:T(2,128)(2,1)S(1)} %slice.119), channel_id=1, source_target_pairs={{0,2},{2,4},{4,6},{6,8},{8,10},{10,12},{12,14},{14,16},{16,18},{18... | collective-permute-start | bytes 147464 | tf_op jit(solution)/shard_map/ppermute | solution.py:26
  5.4 33.0 %collective-permute-start.3 = (bf16[4096,128]{1,0:T(8,128)(2,1)S(1)}, bf16[4096,128]{1,0:T(8,128)(2,1)S(1)}, u32[]{:S(2)}, u32[]{:S(2)}) collective-permute-start(bf16[4096,128]{1,0:T(8,128)(2,1)S(1)} %slice.120), channel_id=1, source_target_pairs={{0,8},{2,10},{4,12},{6,14},{8,0},{10,2},{12,4},{14,6},{16,24},{18,... | collective-permute-start | bytes 3145736 | tf_op jit(solution)/shard_map/ppermute | solution.py:20
  25.5 2.1 collective-permute-start.1
  28.6 8.8 %collective-permute-start.2 = (f32[16,32,128]{2,1,0:T(8,128)S(1)}, f32[16,32,128]{2,1,0:T(8,128)}, u32[]{:S(2)}, u32[]{:S(2)}) collective-permute-start(f32[16,32,128]{2,1,0:T(8,128)S(1)} %multiply_add_fusion.2), channel_id=1, source_target_pairs={{0,4},{2,6},{4,0},{6,2},{8,12},{10,14},{12,8},{14,10},{16,20},{18,... | collective-permute-start | bytes 786440 | tf_op jit(solution)/shard_map/ppermute | solution.py:20
  38.5 7.8 %collective-permute-start.4 = (f32[16,32,128]{2,1,0:T(8,128)S(1)}, f32[16,32,128]{2,1,0:T(8,128)S(1)}, u32[]{:S(2)}, u32[]{:S(2)}) collective-permute-start(f32[16,32,128]{2,1,0:T(8,128)S(1)} %multiply_add_fusion.1), channel_id=1, source_target_pairs={{0,8},{2,10},{4,12},{6,14},{8,0},{10,2},{12,4},{14,6},{16,24},{18,... | collective-permute-start | bytes 786440 | tf_op jit(solution)/shard_map/ppermute | solution.py:20
  43.0 18.1 %copy-start.6 = (f32[4096]{0:T(1024)S(1)}, f32[4096]{0:T(1024)}, u32[]{:S(2)}) copy-start(f32[4096]{0:T(1024)} %param.15) | copy-start | bytes 49156
  46.4 13.4 %collective-permute-start.5 = (f32[16,32,128]{2,1,0:T(8,128)S(1)}, f32[16,32,128]{2,1,0:T(8,128)S(1)}, u32[]{:S(2)}, u32[]{:S(2)}) collective-permute-start(f32[16,32,128]{2,1,0:T(8,128)S(1)} %multiply_add_fusion), channel_id=1, source_target_pairs={{0,16},{2,18},{4,20},{6,22},{8,24},{10,26},{12,28},{14,30},{16,0},... | collective-permute-start | bytes 786440 | tf_op jit(solution)/shard_map/ppermute | solution.py:20
  49.1 110.4 %collective-permute-start.12 = (bf16[4096,384]{1,0:T(8,128)(2,1)}, bf16[4096,384]{1,0:T(8,128)(2,1)}, u32[]{:S(2)}, u32[]{:S(2)}) collective-permute-start(bf16[4096,384]{1,0:T(8,128)(2,1)} %slice.121), channel_id=1, source_target_pairs={{0,8},{2,10},{4,12},{6,14},{8,0},{10,2},{12,4},{14,6},{16,24},{18,... | collective-permute-start | bytes 9437192 | tf_op jit(solution)/shard_map/ppermute | solution.py:20
  78.9 70.6 %collective-permute-start.7 = (bf16[256,4096]{1,0:T(8,128)(2,1)S(1)}, bf16[256,4096]{1,0:T(8,128)(2,1)}, u32[]{:S(2)}, u32[]{:S(2)}) collective-permute-start(bf16[256,4096]{1,0:T(8,128)(2,1)S(1)} %gated_rows.1), channel_id=1, source_target_pairs={{0,4},{2,6},{4,0},{6,2},{8,12},{10,14},{12,8},{14,10},{16,20},{18,... | collective-permute-start | bytes 6291464 | tf_op jit(solution)/shard_map/ppermute | solution.py:20
  82.1 63.8 %collective-permute-start.10 = (bf16[128,4096]{1,0:T(8,128)(2,1)}, bf16[128,4096]{1,0:T(8,128)(2,1)}, u32[]{:S(2)}, u32[]{:S(2)}) collective-permute-start(bf16[128,4096]{1,0:T(8,128)(2,1)} %get-tuple-element.36), channel_id=1, source_target_pairs={{0,16},{2,18},{4,20},{6,22},{8,24},{10,26},{12,28},{14,30},{16,0},... | collective-permute-start | bytes 3145736 | tf_op jit(solution)/shard_map/ppermute | solution.py:20
  85.0 101.1 %collective-permute-start.9 = (bf16[128,4096]{1,0:T(8,128)(2,1)S(1)}, bf16[128,4096]{1,0:T(8,128)(2,1)S(1)}, u32[]{:S(2)}, u32[]{:S(2)}) collective-permute-start(bf16[128,4096]{1,0:T(8,128)(2,1)S(1)} %copy-done.11), channel_id=1, source_target_pairs={{0,16},{2,18},{4,20},{6,22},{8,24},{10,26},{12,28},{14,30},{16,0},... | collective-permute-start | bytes 3145736 | tf_op jit(solution)/shard_map/ppermute | solution.py:20
  145.8 20.7 %collective-permute-start.11 = (bf16[128,4096]{1,0:T(8,128)(2,1)}, bf16[128,4096]{1,0:T(8,128)(2,1)S(1)}, u32[]{:S(2)}, u32[]{:S(2)}) collective-permute-start(bf16[128,4096]{1,0:T(8,128)(2,1)} %collective-permute-done.10), channel_id=1, source_target_pairs={{0,4},{2,6},{4,0},{6,2},{8,12},{10,14},{12,8},{14,10},{16,20},{18,... | collective-permute-start | bytes 3145736 | tf_op jit(solution)/shard_map/ppermute | solution.py:20
  151.6 20.9 %copy-start.10 = (bf16[4096,128]{1,0:T(8,128)(2,1)S(1)}, bf16[4096,128]{1,0:T(8,128)(2,1)}, u32[]{:S(2)}) copy-start(bf16[4096,128]{1,0:T(8,128)(2,1)} %copy-done.9) | copy-start | bytes 3145732
  166.5 11.5 %collective-permute-start.14 = (bf16[4096,384]{1,0:T(8,128)(2,1)}, bf16[4096,384]{1,0:T(8,128)(2,1)S(1)}, u32[]{:S(2)}, u32[]{:S(2)}) collective-permute-start(bf16[4096,384]{1,0:T(8,128)(2,1)} %collective-permute-done.12), channel_id=1, source_target_pairs={{0,2},{2,0},{4,6},{6,4},{8,10},{10,8},{12,14},{14,12},{16,18},{18,... | collective-permute-start | bytes 9437192 | tf_op jit(solution)/shard_map/ppermute | solution.py:20
  171.0 52.0 %collective-permute-start.8 = (bf16[512,1024]{1,0:T(8,128)(2,1)S(1)}, bf16[512,1024]{1,0:T(8,128)(2,1)S(1)}, u32[]{:S(2)}, u32[]{:S(2)}) collective-permute-start(bf16[512,1024]{1,0:T(8,128)(2,1)S(1)} %convolution_convert_fusion.1), channel_id=1, source_target_pairs={{1,0},{3,2},{5,4},{7,6},{9,8},{11,10},{13,12},{15,14},{16,17},{18,... | collective-permute-start | bytes 3145736 | tf_op jit(solution)/shard_map/ppermute | solution.py:344
  172.5 5.1 %collective-permute-start.13 = (bf16[4096,128]{1,0:T(8,128)(2,1)S(1)}, bf16[4096,128]{1,0:T(8,128)(2,1)S(1)}, u32[]{:S(2)}, u32[]{:S(2)}) collective-permute-start(bf16[4096,128]{1,0:T(8,128)(2,1)S(1)} %copy-done.10), channel_id=1, source_target_pairs={{0,2},{2,0},{4,6},{6,4},{8,10},{10,8},{12,14},{14,12},{16,18},{18,... | collective-permute-start | bytes 3145736 | tf_op jit(solution)/shard_map/ppermute | solution.py:20
  183.7 33.2 %collective-permute-start.16 = (bf16[256,1024]{1,0:T(8,128)(2,1)S(1)}, bf16[256,1024]{1,0:T(8,128)(2,1)S(1)}, u32[]{:S(2)}, u32[]{:S(2)}) collective-permute-start(bf16[256,1024]{1,0:T(8,128)(2,1)S(1)} %get-tuple-element.39), channel_id=1, source_target_pairs={{0,1},{1,0},{2,3},{3,2},{4,5},{5,4},{6,7},{7,6},{8,9},{9,8},{10,11... | collective-permute-start | bytes 1572872 | tf_op jit(solution)/shard_map/ppermute | solution.py:20
  186.2 25.1 %collective-permute-start.15 = (bf16[128,4096]{1,0:T(8,128)(2,1)S(1)}, bf16[128,4096]{1,0:T(8,128)(2,1)S(1)}, u32[]{:S(2)}, u32[]{:S(2)}) collective-permute-start(bf16[128,4096]{1,0:T(8,128)(2,1)S(1)} %collective-permute-done.9), channel_id=1, source_target_pairs={{0,4},{2,6},{4,0},{6,2},{8,12},{10,14},{12,8},{14,10},{16,20},{18,... | collective-permute-start | bytes 3145736 | tf_op jit(solution)/shard_map/ppermute | solution.py:20
  216.4 29.9 %collective-permute-start.18 = (bf16[256,1024]{1,0:T(8,128)(2,1)S(1)}, bf16[256,1024]{1,0:T(8,128)(2,1)S(1)}, u32[]{:S(2)}, u32[]{:S(2)}) collective-permute-start(bf16[256,1024]{1,0:T(8,128)(2,1)S(1)} %get-tuple-element.60), channel_id=1, source_target_pairs={{0,1},{1,0},{2,3},{3,2},{4,5},{5,4},{6,7},{7,6},{8,9},{9,8},{10,11... | collective-permute-start | bytes 1572872 | tf_op jit(solution)/shard_map/ppermute | solution.py:20
  217.1 20.4 %collective-permute-start.17 = (bf16[128,1024]{1,0:T(8,128)(2,1)S(1)}, bf16[128,1024]{1,0:T(8,128)(2,1)S(1)}, u32[]{:S(2)}, u32[]{:S(2)}) collective-permute-start(bf16[128,1024]{1,0:T(8,128)(2,1)S(1)} %get-tuple-element.49), channel_id=1, source_target_pairs={{0,16},{2,18},{4,20},{6,22},{8,24},{10,26},{12,28},{14,30},{16,0},... | collective-permute-start | bytes 786440 | tf_op jit(solution)/shard_map/ppermute | solution.py:20
  221.7 21.9 %collective-permute-start.21 = (bf16[128,1024]{1,0:T(8,128)(2,1)S(1)}, bf16[128,1024]{1,0:T(8,128)(2,1)S(1)}, u32[]{:S(2)}, u32[]{:S(2)}) collective-permute-start(bf16[128,1024]{1,0:T(8,128)(2,1)S(1)} %get-tuple-element.48), channel_id=1, source_target_pairs={{0,20},{2,22},{4,16},{6,18},{8,28},{10,30},{12,24},{14,26},{16,4},... | collective-permute-start | bytes 786440 | tf_op jit(solution)/shard_map/ppermute | solution.py:20
  221.7 50.6 %collective-permute-start.23 = (bf16[512,1024]{1,0:T(8,128)(2,1)S(1)}, bf16[512,1024]{1,0:T(8,128)(2,1)S(1)}, u32[]{:S(2)}, u32[]{:S(2)}) collective-permute-start(bf16[512,1024]{1,0:T(8,128)(2,1)S(1)} %convolution_convert_fusion), channel_id=1, source_target_pairs={{1,0},{3,2},{5,4},{7,6},{9,8},{11,10},{13,12},{15,14},{16,17},{18,... | collective-permute-start | bytes 3145736 | tf_op jit(solution)/shard_map/ppermute | solution.py:344
  223.5 48.7 %collective-permute-start.20 = (bf16[256,1024]{1,0:T(8,128)(2,1)S(1)}, bf16[256,1024]{1,0:T(8,128)(2,1)S(1)}, u32[]{:S(2)}, u32[]{:S(2)}) collective-permute-start(bf16[256,1024]{1,0:T(8,128)(2,1)S(1)} %slice.164), channel_id=1, source_target_pairs={{0,4},{2,6},{4,0},{6,2},{8,12},{10,14},{12,8},{14,10},{17,21},{19,... | collective-permute-start | bytes 1572872 | tf_op jit(solution)/shard_map/ppermute | solution.py:344
  243.7 28.5 %collective-permute-start.24 = (bf16[128,2048]{1,0:T(8,128)(2,1)S(1)}, bf16[128,2048]{1,0:T(8,128)(2,1)S(1)}, u32[]{:S(2)}, u32[]{:S(2)}) collective-permute-start(bf16[128,2048]{1,0:T(8,128)(2,1)S(1)} %pad_maximum_fusion.3), channel_id=1, source_target_pairs={{0,1},{2,3},{4,5},{6,7},{8,9},{10,11},{12,13},{14,15},{17,16},{19,... | collective-permute-start | bytes 1572872 | tf_op jit(solution)/shard_map/ppermute | solution.py:344
  246.6 15.4 %collective-permute-start.19 = (bf16[128,1024]{1,0:T(8,128)(2,1)S(1)}, bf16[128,1024]{1,0:T(8,128)(2,1)S(1)}, u32[]{:S(2)}, u32[]{:S(2)}) collective-permute-start(bf16[128,1024]{1,0:T(8,128)(2,1)S(1)} %get-tuple-element.51), channel_id=1, source_target_pairs={{0,16},{2,18},{4,20},{6,22},{8,24},{10,26},{12,28},{14,30},{16,0},... | collective-permute-start | bytes 786440 | tf_op jit(solution)/shard_map/ppermute | solution.py:20
  246.7 21.8 %collective-permute-start.22 = (bf16[128,1024]{1,0:T(8,128)(2,1)S(1)}, bf16[128,1024]{1,0:T(8,128)(2,1)S(1)}, u32[]{:S(2)}, u32[]{:S(2)}) collective-permute-start(bf16[128,1024]{1,0:T(8,128)(2,1)S(1)} %get-tuple-element.50), channel_id=1, source_target_pairs={{0,20},{2,22},{4,16},{6,18},{8,28},{10,30},{12,24},{14,26},{16,4},... | collective-permute-start | bytes 786440 | tf_op jit(solution)/shard_map/ppermute | solution.py:20
  268.6 14.6 %collective-permute-start.25 = (bf16[128,2048]{1,0:T(8,128)(2,1)S(1)}, bf16[128,2048]{1,0:T(8,128)(2,1)S(1)}, u32[]{:S(2)}, u32[]{:S(2)}) collective-permute-start(bf16[128,2048]{1,0:T(8,128)(2,1)S(1)} %pad_maximum_fusion.4), channel_id=1, source_target_pairs={{0,1},{2,3},{4,5},{6,7},{8,9},{10,11},{12,13},{14,15},{17,16},{19,... | collective-permute-start | bytes 1572872 | tf_op jit(solution)/shard_map/ppermute | solution.py:344
  272.4 16.4 %copy-start.3 = (bf16[256,4096]{1,0:T(8,128)(2,1)S(1)}, bf16[256,4096]{1,0:T(8,128)(2,1)}, u32[]{:S(2)}) copy-start(bf16[256,4096]{1,0:T(8,128)(2,1)} %residual_ref.1) | copy-start | bytes 6291460
  272.8 16.0 %copy-start.2 = (bf16[512,4096]{1,0:T(8,128)(2,1)S(1)}, bf16[512,4096]{1,0:T(8,128)(2,1)}, u32[]{:S(2)}) copy-start(bf16[512,4096]{1,0:T(8,128)(2,1)} %table_ref.1) | copy-start | bytes 12582916
  272.8 15.7 %collective-permute-start.26 = (bf16[256,1024]{1,0:T(8,128)(2,1)S(1)}, bf16[256,1024]{1,0:T(8,128)(2,1)S(1)}, u32[]{:S(2)}, u32[]{:S(2)}) collective-permute-start(bf16[256,1024]{1,0:T(8,128)(2,1)S(1)} %slice.179), channel_id=1, source_target_pairs={{0,4},{2,6},{4,0},{6,2},{8,12},{10,14},{12,8},{14,10},{17,21},{19,... | collective-permute-start | bytes 1572872 | tf_op jit(solution)/shard_map/ppermute | solution.py:344
  294.7 7.2 %collective-permute-start.27 = (bf16[528,256]{1,0:T(8,128)(2,1)S(1)}, bf16[528,256]{1,0:T(8,128)(2,1)S(1)}, u32[]{:S(2)}, u32[]{:S(2)}) collective-permute-start(bf16[528,256]{1,0:T(8,128)(2,1)S(1)} %get-tuple-element.35.first_ref), channel_id=1, source_target_pairs={{0,1},{1,0},{2,3},{3,2},{4,5},{5,4},{6,7},{7,6},{8,9},{9,8},{10,11... | collective-permute-start | bytes 811016 | tf_op jit(solution)/shard_map/ppermute | solution.py:20
  (9 other events, 55.7 us)

commit v7 on v5

--- a/solution.py
+++ b/solution.py
@@ -385,6 +385,7 @@
     second.append(tied(jnp.concatenate([above[1], across[1]], axis=0))[0])
     late = shared(second[1])
     sums = [second_sums(*early, across[1]), second_sums(*late)]
+    near_first, _ = tied(near_first, early[0])
     near_sums = first_sums(near_first, across[1])
     far_first, _ = tied(product(first, far_all), late[0])
     far_sums = first_sums(far_first)

time: 298 us -> 295 us (0.990)
  no operation moved by 1% of the time
where the time goes in v7:
time: 295 us; the launch traced here: 294 us
  waiting for transfers between devices  161 us (55%)
  starting transfers between devices  43.4 us (15%)
  Pallas kernels  31 us (11%)
  local copies, waits for them, and re-layouts  29.3 us (10%)
  matrix products  18.6 us (6%)
  other arithmetic  9.16 us (3%)
    ppermute x21, waiting for transfers between devices, xor_permute(): lax.ppermute(value, axis, [(source, source ^ mask) for source in range(co...  150 us
    ppermute x21, starting transfers between devices, xor_permute(): lax.ppermute(value, axis, [(source, source ^ mask) for source in range(co...  25.5 us
    dot_general x6, matrix products, product(): return jnp.dot(rows, weight, preferred_element_type=F32).astype(BF16)  18.6 us
    unnamed x32, local copies, waits for them, and re-layouts  16 us
    ppermute x6, starting transfers between devices, placed_permute(): return lax.ppermute(value, ('seq', 'chan'), pairs)  15.9 us
    pallas_call x1, Pallas kernels, gated_rows(): pl.pallas_call(gated_kernel, grid=(width // GROUP,), in_specs=[pl.BlockSp...  13.4 us
    ppermute x6, waiting for transfers between devices, placed_permute(): return lax.ppermute(value, ('seq', 'chan'), pairs)  11.8 us
    pallas_call x1, Pallas kernels, mixed_and_states(): pl.pallas_call(states_kernel, grid=(width // GROUP,), in_specs=[stream(1)...  10.8 us
  transfers between devices with their start and end apart: 28, of which 16 were waited for; matrix products, arithmetic and copies ran while one was open for 16% of the time, Pallas kernels for 8%

profile of v7, /device:TPU:0, one launch (start us, length us, event | category | flops | bytes accessed | tf_op | source)
XLA Modules:
  0.0 294.1 jit_solution(7992208794056986243)
XLA Ops:
  5.4 3.1 %collective-permute-start.3 = (bf16[4096,128]{1,0:T(8,128)(2,1)S(1)}, bf16[4096,128]{1,0:T(8,128)(2,1)S(1)}, u32[]{:S(2)}, u32[]{:S(2)}) collective-permute-start(bf16[4096,128]{1,0:T(8,128)(2,1)S(1)} %slice.120), channel_id=1, source_target_pairs={{0,8},{2,10},{4,12},{6,14},{8,0},{10,2},{12,4},{14,6},{16,24},{18,... | collective-permute-start | bytes 3145736 | tf_op jit(solution)/shard_map/ppermute | solution.py:20
  10.6 2.8 copy-done
  13.4 10.8 %mixed_and_states.1 = (bf16[256,4096]{1,0:T(8,128)(2,1)S(1)}, f32[16,32,128]{2,1,0:T(8,128)S(1)}) custom-call(bf16[3,256,4096]{2,1,0:T(8,128)(2,1)S(1)} %bitcast.60, bf16[3,256,4096]{2,1,0:T(8,128)(2,1)S(1)} %bitcast.61, f32[3,8,4096]{2,1,0:T(8,128)S(1)} %pad_convert_fusion.halo_ref, f32[9,4096]{1,0:T(8,128)S(1)} %reshape.13.taps_ref, ...), custom_call_target="tpu_custom_call" | custom-call | flops 1048576 | bytes 256 | tf_op jit(solution)/shard_map/mixed_and_states/pallas_call | solution.py:132
  30.3 7.1 %collective-permute-done.2 = f32[16,32,128]{2,1,0:T(8,128)} collective-permute-done((f32[16,32,128]{2,1,0:T(8,128)S(1)}, f32[16,32,128]{2,1,0:T(8,128)}, u32[]{:S(2)}, u32[]{:S(2)}) %collective-permute-start.2) | collective-permute-done | bytes 262176 | tf_op jit(solution)/shard_map/ppermute | solution.py:20
  39.0 4.0 %slice.121 = bf16[4096,384]{1,0:T(8,128)(2,1)} slice(bf16[4096,512]{1,0:T(8,128)(2,1)} %param.16), slice={[0:4096], [128:512]} | slice | bytes 6291456 | tf_op jit(solution)/shard_map/slice | solution.py:326
  43.0 3.3 %collective-permute-done.4 = f32[16,32,128]{2,1,0:T(8,128)S(1)} collective-permute-done((f32[16,32,128]{2,1,0:T(8,128)S(1)}, f32[16,32,128]{2,1,0:T(8,128)S(1)}, u32[]{:S(2)}, u32[]{:S(2)}) %collective-permute-start.4) | collective-permute-done | bytes 262176 | tf_op jit(solution)/shard_map/ppermute | solution.py:20
  49.6 10.2 %collective-permute-done.5 = f32[16,32,128]{2,1,0:T(8,128)S(1)} collective-permute-done((f32[16,32,128]{2,1,0:T(8,128)S(1)}, f32[16,32,128]{2,1,0:T(8,128)S(1)}, u32[]{:S(2)}, u32[]{:S(2)}) %collective-permute-start.5) | collective-permute-done | bytes 262176 | tf_op jit(solution)/shard_map/ppermute | solution.py:20
  65.5 13.4 %gated_rows.1 = bf16[256,4096]{1,0:T(8,128)(2,1)S(1)} custom-call(bf16[3,256,4096]{2,1,0:T(8,128)(2,1)S(1)} %bitcast.62, f32[3,8,4096]{2,1,0:T(8,128)S(1)} %pad_convert_fusion.halo_ref, f32[9,4096]{1,0:T(8,128)S(1)} %reshape.13.taps_ref, bf16[256,4096]{1,0:T(8,128)(2,1)S(1)} %copy-done.5, f32[1,4096]{1,0:T(1,128)S(1)} %bitcast.66, ...), custom_call_target="tpu_custom_call" | custom-call | flops 1048576 | bytes 256 | tf_op jit(solution)/shard_map/gated_rows/pallas_call | solution.py:162
  82.1 2.9 constant_dynamic-update-slice_fusion.1
  85.0 3.0 %collective-permute-start.14 = (bf16[128,4096]{1,0:T(8,128)(2,1)S(1)}, bf16[128,4096]{1,0:T(8,128)(2,1)S(1)}, u32[]{:S(2)}, u32[]{:S(2)}) collective-permute-start(bf16[128,4096]{1,0:T(8,128)(2,1)S(1)} %copy-done.11), channel_id=1, source_target_pairs={{0,16},{2,18},{4,20},{6,22},{8,24},{10,26},{12,28},{14,30},{16,0},... | collective-permute-start | bytes 3145736 | tf_op jit(solution)/shard_map/ppermute | solution.py:20
  88.0 57.8 %collective-permute-done.8 = bf16[128,4096]{1,0:T(8,128)(2,1)} collective-permute-done((bf16[128,4096]{1,0:T(8,128)(2,1)}, bf16[128,4096]{1,0:T(8,128)(2,1)}, u32[]{:S(2)}, u32[]{:S(2)}) %collective-permute-start.8) | collective-permute-done | bytes 1048608 | tf_op jit(solution)/shard_map/ppermute | solution.py:20
  146.4 3.3 %constant_dynamic-update-slice_fusion = bf16[4096,1024]{1,0:T(8,128)(2,1)S(1)} fusion(bf16[4096,1024]{1,0:T(8,128)(2,1)S(1)} %constant_dynamic-update-slice_fusion.1, bf16[4096,512]{1,0:T(8,128)(2,1)} %collective-permute-done.6), kind=kLoop, calls=%fused_computation.47 | loop fusion | bytes 8388608 | tf_op jit(solution)/shard_map/concatenate | solution.py:359
  151.8 7.7 %collective-permute-done.10 = bf16[4096,384]{1,0:T(8,128)(2,1)} collective-permute-done((bf16[4096,384]{1,0:T(8,128)(2,1)}, bf16[4096,384]{1,0:T(8,128)(2,1)}, u32[]{:S(2)}, u32[]{:S(2)}) %collective-permute-start.10) | collective-permute-done | bytes 3145760 | tf_op jit(solution)/shard_map/ppermute | solution.py:20
  159.5 7.0 %collective-permute-done.9 = bf16[128,4096]{1,0:T(8,128)(2,1)S(1)} collective-permute-done((bf16[128,4096]{1,0:T(8,128)(2,1)}, bf16[128,4096]{1,0:T(8,128)(2,1)S(1)}, u32[]{:S(2)}, u32[]{:S(2)}) %collective-permute-start.9) | collective-permute-done | bytes 1048608 | tf_op jit(solution)/shard_map/ppermute | solution.py:20
  166.5 4.5 %convolution_convert_fusion.1 = bf16[512,1024]{1,0:T(8,128)(2,1)S(1)} fusion(bf16[512,4096]{1,0:T(8,128)(2,1)S(1)} %pad_maximum_fusion, bf16[4096,1024]{1,0:T(8,128)(2,1)S(1)} %constant_dynamic-update-slice_fusion), kind=kOutput, calls=%fused_computation.6 | convolution fusion | flops 4295491584 | bytes 13631488 | tf_op jit(solution)/shard_map/dot_general | solution.py:330
  173.4 2.8 constant_dynamic-update-slice_fusion.4
  184.1 4.7 %convolution_convert_fusion = bf16[512,1024]{1,0:T(8,128)(2,1)S(1)} fusion(bf16[512,4096]{1,0:T(8,128)(2,1)S(1)} %pad_maximum_fusion, bf16[4096,1024]{1,0:T(8,128)(2,1)S(1)} %constant_dynamic-update-slice_fusion.2), kind=kOutput, calls=%fused_computation.5 | convolution fusion | flops 4295491584 | bytes 13631488 | tf_op jit(solution)/shard_map/dot_general | solution.py:330
  190.1 7.0 %collective-permute-done.16 = bf16[256,1024]{1,0:T(8,128)(2,1)S(1)} collective-permute-done((bf16[256,1024]{1,0:T(8,128)(2,1)S(1)}, bf16[256,1024]{1,0:T(8,128)(2,1)S(1)}, u32[]{:S(2)}, u32[]{:S(2)}) %collective-permute-start.16) | collective-permute-done | bytes 524320 | tf_op jit(solution)/shard_map/ppermute | solution.py:20
  197.0 11.5 %collective-permute-done.15 = bf16[128,4096]{1,0:T(8,128)(2,1)S(1)} collective-permute-done((bf16[128,4096]{1,0:T(8,128)(2,1)S(1)}, bf16[128,4096]{1,0:T(8,128)(2,1)S(1)}, u32[]{:S(2)}, u32[]{:S(2)}) %collective-permute-start.15) | collective-permute-done | bytes 1048608 | tf_op jit(solution)/shard_map/ppermute | solution.py:20
  208.8 3.4 %collective-permute-start.17 = (bf16[128,1024]{1,0:T(8,128)(2,1)S(1)}, bf16[128,1024]{1,0:T(8,128)(2,1)S(1)}, u32[]{:S(2)}, u32[]{:S(2)}) collective-permute-start(bf16[128,1024]{1,0:T(8,128)(2,1)S(1)} %get-tuple-element.51), channel_id=1, source_target_pairs={{0,16},{2,18},{4,20},{6,22},{8,24},{10,26},{12,28},{14,30},{16,0},... | collective-permute-start | bytes 786440 | tf_op jit(solution)/shard_map/ppermute | solution.py:20
  219.6 3.4 %collective-permute-start.20 = (bf16[256,1024]{1,0:T(8,128)(2,1)S(1)}, bf16[256,1024]{1,0:T(8,128)(2,1)S(1)}, u32[]{:S(2)}, u32[]{:S(2)}) collective-permute-start(bf16[256,1024]{1,0:T(8,128)(2,1)S(1)} %slice.164), channel_id=1, source_target_pairs={{0,4},{2,6},{4,0},{6,2},{8,12},{10,14},{12,8},{14,10},{17,21},{19,... | collective-permute-start | bytes 1572872 | tf_op jit(solution)/shard_map/ppermute | solution.py:344
  223.0 5.8 %collective-permute-done.17 = bf16[128,1024]{1,0:T(8,128)(2,1)S(1)} collective-permute-done((bf16[128,1024]{1,0:T(8,128)(2,1)S(1)}, bf16[128,1024]{1,0:T(8,128)(2,1)S(1)}, u32[]{:S(2)}, u32[]{:S(2)}) %collective-permute-start.17) | collective-permute-done | bytes 262176 | tf_op jit(solution)/shard_map/ppermute | solution.py:20
  228.8 5.4 %collective-permute-done.21 = bf16[128,1024]{1,0:T(8,128)(2,1)S(1)} collective-permute-done((bf16[128,1024]{1,0:T(8,128)(2,1)S(1)}, bf16[128,1024]{1,0:T(8,128)(2,1)S(1)}, u32[]{:S(2)}, u32[]{:S(2)}) %collective-permute-start.21) | collective-permute-done | bytes 262176 | tf_op jit(solution)/shard_map/ppermute | solution.py:20
  237.0 4.0 %collective-permute-start.22 = (bf16[128,1024]{1,0:T(8,128)(2,1)S(1)}, bf16[128,1024]{1,0:T(8,128)(2,1)S(1)}, u32[]{:S(2)}, u32[]{:S(2)}) collective-permute-start(bf16[128,1024]{1,0:T(8,128)(2,1)S(1)} %get-tuple-element.52), channel_id=1, source_target_pairs={{0,20},{2,22},{4,16},{6,18},{8,28},{10,30},{12,24},{14,26},{16,4},... | collective-permute-start | bytes 786440 | tf_op jit(solution)/shard_map/ppermute | solution.py:20
  241.1 12.2 %collective-permute-done.19 = bf16[128,1024]{1,0:T(8,128)(2,1)S(1)} collective-permute-done((bf16[128,1024]{1,0:T(8,128)(2,1)S(1)}, bf16[128,1024]{1,0:T(8,128)(2,1)S(1)}, u32[]{:S(2)}, u32[]{:S(2)}) %collective-permute-start.19) | collective-permute-done | bytes 262176 | tf_op jit(solution)/shard_map/ppermute | solution.py:20
  253.4 5.9 %collective-permute-done.22 = bf16[128,1024]{1,0:T(8,128)(2,1)S(1)} collective-permute-done((bf16[128,1024]{1,0:T(8,128)(2,1)S(1)}, bf16[128,1024]{1,0:T(8,128)(2,1)S(1)}, u32[]{:S(2)}, u32[]{:S(2)}) %collective-permute-start.22) | collective-permute-done | bytes 262176 | tf_op jit(solution)/shard_map/ppermute | solution.py:20
  259.3 3.9 %collective-permute-start.25 = (bf16[128,2048]{1,0:T(8,128)(2,1)S(1)}, bf16[128,2048]{1,0:T(8,128)(2,1)S(1)}, u32[]{:S(2)}, u32[]{:S(2)}) collective-permute-start(bf16[128,2048]{1,0:T(8,128)(2,1)S(1)} %pad_maximum_fusion.4), channel_id=1, source_target_pairs={{0,1},{2,3},{4,5},{6,7},{8,9},{10,11},{12,13},{14,15},{17,16},{19,... | collective-permute-start | bytes 1572872 | tf_op jit(solution)/shard_map/ppermute | solution.py:344
  264.1 3.7 %collective-permute-start.26 = (bf16[256,1024]{1,0:T(8,128)(2,1)S(1)}, bf16[256,1024]{1,0:T(8,128)(2,1)S(1)}, u32[]{:S(2)}, u32[]{:S(2)}) collective-permute-start(bf16[256,1024]{1,0:T(8,128)(2,1)S(1)} %slice.179), channel_id=1, source_target_pairs={{0,4},{2,6},{4,0},{6,2},{8,12},{10,14},{12,8},{14,10},{17,21},{19,... | collective-permute-start | bytes 1572872 | tf_op jit(solution)/shard_map/ppermute | solution.py:344
  267.9 6.6 %collective-permute-done.25 = bf16[128,2048]{1,0:T(8,128)(2,1)S(1)} collective-permute-done((bf16[128,2048]{1,0:T(8,128)(2,1)S(1)}, bf16[128,2048]{1,0:T(8,128)(2,1)S(1)}, u32[]{:S(2)}, u32[]{:S(2)}) %collective-permute-start.25) | collective-permute-done | bytes 524320 | tf_op jit(solution)/shard_map/ppermute | solution.py:344
  274.7 5.2 %collective-permute-done.26 = bf16[256,1024]{1,0:T(8,128)(2,1)S(1)} collective-permute-done((bf16[256,1024]{1,0:T(8,128)(2,1)S(1)}, bf16[256,1024]{1,0:T(8,128)(2,1)S(1)}, u32[]{:S(2)}, u32[]{:S(2)}) %collective-permute-start.26) | collective-permute-done | bytes 524320 | tf_op jit(solution)/shard_map/ppermute | solution.py:344
  280.1 5.9 %output_rows.1 = (bf16[256,4096]{1,0:T(8,128)(2,1)}, bf16[528,256]{1,0:T(8,128)(2,1)S(1)}) custom-call(s32[8]{0:T(128)S(1)} %iota_xor_fusion.order_ref, bf16[8,256,512]{2,1,0:T(8,128)(2,1)S(1)} %fusion.1.added_ref, bf16[256,4096]{1,0:T(8,128)(2,1)S(1)} %copy-done.3, f32[1,4096]{1,0:T(1,128)S(1)} %bitcast.67, bf16[512,4096]{1,0:T(8,128)(2,1)S(1)} %copy-done.2), custom_call_target="tpu_custom_call" | custom-call | flops 1073741824 | bytes 10485760 | tf_op jit(solution)/shard_map/output_rows/pallas_call | solution.py:253
  286.0 7.2 %collective-permute-done.27.second_ref = bf16[528,256]{1,0:T(8,128)(2,1)S(1)} collective-permute-done((bf16[528,256]{1,0:T(8,128)(2,1)S(1)}, bf16[528,256]{1,0:T(8,128)(2,1)S(1)}, u32[]{:S(2)}, u32[]{:S(2)}) %collective-permute-start.27) | collective-permute-done | bytes 270368 | tf_op jit(solution)/shard_map/ppermute | solution.py:20
  (106 shorter events, 53.0 us)
Async XLA Ops:
  0.6 60.4 %collective-permute-start.6 = (bf16[4096,512]{1,0:T(8,128)(2,1)}, bf16[4096,512]{1,0:T(8,128)(2,1)}, u32[]{:S(2)}, u32[]{:S(2)}) collective-permute-start(bf16[4096,512]{1,0:T(8,128)(2,1)} %param.16), channel_id=1, source_target_pairs={{0,2},{2,0},{4,6},{6,4},{8,10},{10,8},{12,14},{14,12},{16,18},{18,... | collective-permute-start | bytes 12582920 | tf_op jit(solution)/shard_map/ppermute | solution.py:20
  2.1 8.4 %collective-permute-start = (bf16[2,3,4096]{2,0,1:T(2,128)(2,1)S(1)}, bf16[2,3,4096]{2,0,1:T(2,128)(2,1)S(1)}, u32[]{:S(2)}, u32[]{:S(2)}) collective-permute-start(bf16[2,3,4096]{2,0,1:T(2,128)(2,1)S(1)} %slice.119), channel_id=1, source_target_pairs={{0,2},{2,4},{4,6},{6,8},{8,10},{10,12},{12,14},{14,16},{16,18},{18... | collective-permute-start | bytes 147464 | tf_op jit(solution)/shard_map/ppermute | solution.py:26
  5.4 33.0 %collective-permute-start.3 = (bf16[4096,128]{1,0:T(8,128)(2,1)S(1)}, bf16[4096,128]{1,0:T(8,128)(2,1)S(1)}, u32[]{:S(2)}, u32[]{:S(2)}) collective-permute-start(bf16[4096,128]{1,0:T(8,128)(2,1)S(1)} %slice.120), channel_id=1, source_target_pairs={{0,8},{2,10},{4,12},{6,14},{8,0},{10,2},{12,4},{14,6},{16,24},{18,... | collective-permute-start | bytes 3145736 | tf_op jit(solution)/shard_map/ppermute | solution.py:20
  25.5 2.1 collective-permute-start.1
  28.6 8.8 %collective-permute-start.2 = (f32[16,32,128]{2,1,0:T(8,128)S(1)}, f32[16,32,128]{2,1,0:T(8,128)}, u32[]{:S(2)}, u32[]{:S(2)}) collective-permute-start(f32[16,32,128]{2,1,0:T(8,128)S(1)} %multiply_add_fusion.2), channel_id=1, source_target_pairs={{0,4},{2,6},{4,0},{6,2},{8,12},{10,14},{12,8},{14,10},{16,20},{18,... | collective-permute-start | bytes 786440 | tf_op jit(solution)/shard_map/ppermute | solution.py:20
  38.5 7.8 %collective-permute-start.4 = (f32[16,32,128]{2,1,0:T(8,128)S(1)}, f32[16,32,128]{2,1,0:T(8,128)S(1)}, u32[]{:S(2)}, u32[]{:S(2)}) collective-permute-start(f32[16,32,128]{2,1,0:T(8,128)S(1)} %multiply_add_fusion.1), channel_id=1, source_target_pairs={{0,8},{2,10},{4,12},{6,14},{8,0},{10,2},{12,4},{14,6},{16,24},{18,... | collective-permute-start | bytes 786440 | tf_op jit(solution)/shard_map/ppermute | solution.py:20
  43.0 18.1 %copy-start.6 = (f32[4096]{0:T(1024)S(1)}, f32[4096]{0:T(1024)}, u32[]{:S(2)}) copy-start(f32[4096]{0:T(1024)} %param.15) | copy-start | bytes 49156
  46.4 13.4 %collective-permute-start.5 = (f32[16,32,128]{2,1,0:T(8,128)S(1)}, f32[16,32,128]{2,1,0:T(8,128)S(1)}, u32[]{:S(2)}, u32[]{:S(2)}) collective-permute-start(f32[16,32,128]{2,1,0:T(8,128)S(1)} %multiply_add_fusion), channel_id=1, source_target_pairs={{0,16},{2,18},{4,20},{6,22},{8,24},{10,26},{12,28},{14,30},{16,0},... | collective-permute-start | bytes 786440 | tf_op jit(solution)/shard_map/ppermute | solution.py:20
  49.1 110.4 %collective-permute-start.10 = (bf16[4096,384]{1,0:T(8,128)(2,1)}, bf16[4096,384]{1,0:T(8,128)(2,1)}, u32[]{:S(2)}, u32[]{:S(2)}) collective-permute-start(bf16[4096,384]{1,0:T(8,128)(2,1)} %slice.121), channel_id=1, source_target_pairs={{0,8},{2,10},{4,12},{6,14},{8,0},{10,2},{12,4},{14,6},{16,24},{18,... | collective-permute-start | bytes 9437192 | tf_op jit(solution)/shard_map/ppermute | solution.py:20
  78.9 70.8 %collective-permute-start.7 = (bf16[256,4096]{1,0:T(8,128)(2,1)S(1)}, bf16[256,4096]{1,0:T(8,128)(2,1)}, u32[]{:S(2)}, u32[]{:S(2)}) collective-permute-start(bf16[256,4096]{1,0:T(8,128)(2,1)S(1)} %gated_rows.1), channel_id=1, source_target_pairs={{0,4},{2,6},{4,0},{6,2},{8,12},{10,14},{12,8},{14,10},{16,20},{18,... | collective-permute-start | bytes 6291464 | tf_op jit(solution)/shard_map/ppermute | solution.py:20
  82.1 63.8 %collective-permute-start.8 = (bf16[128,4096]{1,0:T(8,128)(2,1)}, bf16[128,4096]{1,0:T(8,128)(2,1)}, u32[]{:S(2)}, u32[]{:S(2)}) collective-permute-start(bf16[128,4096]{1,0:T(8,128)(2,1)} %get-tuple-element.39), channel_id=1, source_target_pairs={{0,16},{2,18},{4,20},{6,22},{8,24},{10,26},{12,28},{14,30},{16,0},... | collective-permute-start | bytes 3145736 | tf_op jit(solution)/shard_map/ppermute | solution.py:20
  85.0 98.7 %collective-permute-start.14 = (bf16[128,4096]{1,0:T(8,128)(2,1)S(1)}, bf16[128,4096]{1,0:T(8,128)(2,1)S(1)}, u32[]{:S(2)}, u32[]{:S(2)}) collective-permute-start(bf16[128,4096]{1,0:T(8,128)(2,1)S(1)} %copy-done.11), channel_id=1, source_target_pairs={{0,16},{2,18},{4,20},{6,22},{8,24},{10,26},{12,28},{14,30},{16,0},... | collective-permute-start | bytes 3145736 | tf_op jit(solution)/shard_map/ppermute | solution.py:20
  145.8 20.7 %collective-permute-start.9 = (bf16[128,4096]{1,0:T(8,128)(2,1)}, bf16[128,4096]{1,0:T(8,128)(2,1)S(1)}, u32[]{:S(2)}, u32[]{:S(2)}) collective-permute-start(bf16[128,4096]{1,0:T(8,128)(2,1)} %collective-permute-done.8), channel_id=1, source_target_pairs={{0,4},{2,6},{4,0},{6,2},{8,12},{10,14},{12,8},{14,10},{16,20},{18,... | collective-permute-start | bytes 3145736 | tf_op jit(solution)/shard_map/ppermute | solution.py:20
  151.8 19.3 %copy-start.10 = (bf16[4096,128]{1,0:T(8,128)(2,1)S(1)}, bf16[4096,128]{1,0:T(8,128)(2,1)}, u32[]{:S(2)}) copy-start(bf16[4096,128]{1,0:T(8,128)(2,1)} %copy-done.9) | copy-start | bytes 3145732
  166.5 10.0 %collective-permute-start.12 = (bf16[4096,384]{1,0:T(8,128)(2,1)}, bf16[4096,384]{1,0:T(8,128)(2,1)S(1)}, u32[]{:S(2)}, u32[]{:S(2)}) collective-permute-start(bf16[4096,384]{1,0:T(8,128)(2,1)} %collective-permute-done.10), channel_id=1, source_target_pairs={{0,2},{2,0},{4,6},{6,4},{8,10},{10,8},{12,14},{14,12},{16,18},{18,... | collective-permute-start | bytes 9437192 | tf_op jit(solution)/shard_map/ppermute | solution.py:20
  171.1 5.1 %collective-permute-start.11 = (bf16[4096,128]{1,0:T(8,128)(2,1)S(1)}, bf16[4096,128]{1,0:T(8,128)(2,1)S(1)}, u32[]{:S(2)}, u32[]{:S(2)}) collective-permute-start(bf16[4096,128]{1,0:T(8,128)(2,1)S(1)} %copy-done.10), channel_id=1, source_target_pairs={{0,2},{2,0},{4,6},{6,4},{8,10},{10,8},{12,14},{14,12},{16,18},{18,... | collective-permute-start | bytes 3145736 | tf_op jit(solution)/shard_map/ppermute | solution.py:20
  182.2 14.9 %collective-permute-start.16 = (bf16[256,1024]{1,0:T(8,128)(2,1)S(1)}, bf16[256,1024]{1,0:T(8,128)(2,1)S(1)}, u32[]{:S(2)}, u32[]{:S(2)}) collective-permute-start(bf16[256,1024]{1,0:T(8,128)(2,1)S(1)} %get-tuple-element.41), channel_id=1, source_target_pairs={{0,1},{1,0},{2,3},{3,2},{4,5},{5,4},{6,7},{7,6},{8,9},{9,8},{10,11... | collective-permute-start | bytes 1572872 | tf_op jit(solution)/shard_map/ppermute | solution.py:20
  183.8 24.8 %collective-permute-start.15 = (bf16[128,4096]{1,0:T(8,128)(2,1)S(1)}, bf16[128,4096]{1,0:T(8,128)(2,1)S(1)}, u32[]{:S(2)}, u32[]{:S(2)}) collective-permute-start(bf16[128,4096]{1,0:T(8,128)(2,1)S(1)} %collective-permute-done.14), channel_id=1, source_target_pairs={{0,4},{2,6},{4,0},{6,2},{8,12},{10,14},{12,8},{14,10},{16,20},{18,... | collective-permute-start | bytes 3145736 | tf_op jit(solution)/shard_map/ppermute | solution.py:20
  188.8 30.3 %collective-permute-start.13 = (bf16[512,1024]{1,0:T(8,128)(2,1)S(1)}, bf16[512,1024]{1,0:T(8,128)(2,1)S(1)}, u32[]{:S(2)}, u32[]{:S(2)}) collective-permute-start(bf16[512,1024]{1,0:T(8,128)(2,1)S(1)} %convolution_convert_fusion.1), channel_id=1, source_target_pairs={{1,0},{3,2},{5,4},{7,6},{9,8},{11,10},{13,12},{15,14},{16,17},{18,... | collective-permute-start | bytes 3145736 | tf_op jit(solution)/shard_map/ppermute | solution.py:344
  208.8 20.0 %collective-permute-start.17 = (bf16[128,1024]{1,0:T(8,128)(2,1)S(1)}, bf16[128,1024]{1,0:T(8,128)(2,1)S(1)}, u32[]{:S(2)}, u32[]{:S(2)}) collective-permute-start(bf16[128,1024]{1,0:T(8,128)(2,1)S(1)} %get-tuple-element.51), channel_id=1, source_target_pairs={{0,16},{2,18},{4,20},{6,22},{8,24},{10,26},{12,28},{14,30},{16,0},... | collective-permute-start | bytes 786440 | tf_op jit(solution)/shard_map/ppermute | solution.py:20
  212.3 22.0 %collective-permute-start.21 = (bf16[128,1024]{1,0:T(8,128)(2,1)S(1)}, bf16[128,1024]{1,0:T(8,128)(2,1)S(1)}, u32[]{:S(2)}, u32[]{:S(2)}) collective-permute-start(bf16[128,1024]{1,0:T(8,128)(2,1)S(1)} %get-tuple-element.50), channel_id=1, source_target_pairs={{0,20},{2,22},{4,16},{6,18},{8,28},{10,30},{12,24},{14,26},{16,4},... | collective-permute-start | bytes 786440 | tf_op jit(solution)/shard_map/ppermute | solution.py:20
  217.2 19.4 %collective-permute-start.18 = (bf16[256,1024]{1,0:T(8,128)(2,1)S(1)}, bf16[256,1024]{1,0:T(8,128)(2,1)S(1)}, u32[]{:S(2)}, u32[]{:S(2)}) collective-permute-start(bf16[256,1024]{1,0:T(8,128)(2,1)S(1)} %get-tuple-element.62), channel_id=1, source_target_pairs={{0,1},{1,0},{2,3},{3,2},{4,5},{5,4},{6,7},{7,6},{8,9},{9,8},{10,11... | collective-permute-start | bytes 1572872 | tf_op jit(solution)/shard_map/ppermute | solution.py:20
  217.8 45.8 %collective-permute-start.23 = (bf16[512,1024]{1,0:T(8,128)(2,1)S(1)}, bf16[512,1024]{1,0:T(8,128)(2,1)S(1)}, u32[]{:S(2)}, u32[]{:S(2)}) collective-permute-start(bf16[512,1024]{1,0:T(8,128)(2,1)S(1)} %convolution_convert_fusion), channel_id=1, source_target_pairs={{1,0},{3,2},{5,4},{7,6},{9,8},{11,10},{13,12},{15,14},{16,17},{18,... | collective-permute-start | bytes 3145736 | tf_op jit(solution)/shard_map/ppermute | solution.py:344
  219.6 43.9 %collective-permute-start.20 = (bf16[256,1024]{1,0:T(8,128)(2,1)S(1)}, bf16[256,1024]{1,0:T(8,128)(2,1)S(1)}, u32[]{:S(2)}, u32[]{:S(2)}) collective-permute-start(bf16[256,1024]{1,0:T(8,128)(2,1)S(1)} %slice.164), channel_id=1, source_target_pairs={{0,4},{2,6},{4,0},{6,2},{8,12},{10,14},{12,8},{14,10},{17,21},{19,... | collective-permute-start | bytes 1572872 | tf_op jit(solution)/shard_map/ppermute | solution.py:344
  234.3 29.2 %collective-permute-start.24 = (bf16[128,2048]{1,0:T(8,128)(2,1)S(1)}, bf16[128,2048]{1,0:T(8,128)(2,1)S(1)}, u32[]{:S(2)}, u32[]{:S(2)}) collective-permute-start(bf16[128,2048]{1,0:T(8,128)(2,1)S(1)} %pad_maximum_fusion.3), channel_id=1, source_target_pairs={{0,1},{2,3},{4,5},{6,7},{8,9},{10,11},{12,13},{14,15},{17,16},{19,... | collective-permute-start | bytes 1572872 | tf_op jit(solution)/shard_map/ppermute | solution.py:344
  237.0 16.4 %collective-permute-start.19 = (bf16[128,1024]{1,0:T(8,128)(2,1)S(1)}, bf16[128,1024]{1,0:T(8,128)(2,1)S(1)}, u32[]{:S(2)}, u32[]{:S(2)}) collective-permute-start(bf16[128,1024]{1,0:T(8,128)(2,1)S(1)} %get-tuple-element.53), channel_id=1, source_target_pairs={{0,16},{2,18},{4,20},{6,22},{8,24},{10,26},{12,28},{14,30},{16,0},... | collective-permute-start | bytes 786440 | tf_op jit(solution)/shard_map/ppermute | solution.py:20
  237.0 22.2 %collective-permute-start.22 = (bf16[128,1024]{1,0:T(8,128)(2,1)S(1)}, bf16[128,1024]{1,0:T(8,128)(2,1)S(1)}, u32[]{:S(2)}, u32[]{:S(2)}) collective-permute-start(bf16[128,1024]{1,0:T(8,128)(2,1)S(1)} %get-tuple-element.52), channel_id=1, source_target_pairs={{0,20},{2,22},{4,16},{6,18},{8,28},{10,30},{12,24},{14,26},{16,4},... | collective-permute-start | bytes 786440 | tf_op jit(solution)/shard_map/ppermute | solution.py:20
  259.3 15.2 %collective-permute-start.25 = (bf16[128,2048]{1,0:T(8,128)(2,1)S(1)}, bf16[128,2048]{1,0:T(8,128)(2,1)S(1)}, u32[]{:S(2)}, u32[]{:S(2)}) collective-permute-start(bf16[128,2048]{1,0:T(8,128)(2,1)S(1)} %pad_maximum_fusion.4), channel_id=1, source_target_pairs={{0,1},{2,3},{4,5},{6,7},{8,9},{10,11},{12,13},{14,15},{17,16},{19,... | collective-permute-start | bytes 1572872 | tf_op jit(solution)/shard_map/ppermute | solution.py:344
  263.7 16.4 %copy-start.3 = (bf16[256,4096]{1,0:T(8,128)(2,1)S(1)}, bf16[256,4096]{1,0:T(8,128)(2,1)}, u32[]{:S(2)}) copy-start(bf16[256,4096]{1,0:T(8,128)(2,1)} %residual_ref.1) | copy-start | bytes 6291460
  264.1 16.0 %copy-start.2 = (bf16[512,4096]{1,0:T(8,128)(2,1)S(1)}, bf16[512,4096]{1,0:T(8,128)(2,1)}, u32[]{:S(2)}) copy-start(bf16[512,4096]{1,0:T(8,128)(2,1)} %table_ref.1) | copy-start | bytes 12582916
  264.1 15.7 %collective-permute-start.26 = (bf16[256,1024]{1,0:T(8,128)(2,1)S(1)}, bf16[256,1024]{1,0:T(8,128)(2,1)S(1)}, u32[]{:S(2)}, u32[]{:S(2)}) collective-permute-start(bf16[256,1024]{1,0:T(8,128)(2,1)S(1)} %slice.179), channel_id=1, source_target_pairs={{0,4},{2,6},{4,0},{6,2},{8,12},{10,14},{12,8},{14,10},{17,21},{19,... | collective-permute-start | bytes 1572872 | tf_op jit(solution)/shard_map/ppermute | solution.py:344
  286.0 7.2 %collective-permute-start.27 = (bf16[528,256]{1,0:T(8,128)(2,1)S(1)}, bf16[528,256]{1,0:T(8,128)(2,1)S(1)}, u32[]{:S(2)}, u32[]{:S(2)}) collective-permute-start(bf16[528,256]{1,0:T(8,128)(2,1)S(1)} %get-tuple-element.37.first_ref), channel_id=1, source_target_pairs={{0,1},{1,0},{2,3},{3,2},{4,5},{5,4},{6,7},{7,6},{8,9},{9,8},{10,11... | collective-permute-start | bytes 811016 | tf_op jit(solution)/shard_map/ppermute | solution.py:20
  (9 other events, 55.7 us)

commit v8 on v5

--- a/solution.py
+++ b/solution.py
@@ -358,7 +358,6 @@
     across = [xor_permute(above[0], "seq", side)]
     near = jnp.concatenate([out_weight, core_weight], axis=1)
     first = tied(jnp.concatenate([gated, beside], axis=0))[0]
-    near_first = product(first, near)
     across[0], *far = tied(across[0], *far)
     second = [tied(jnp.concatenate([above[0], across[0]], axis=0))[0]]
     far_all = jnp.concatenate(far + [xor_permute(piece, "seq", core) for piece in far], axis=1)
@@ -380,11 +379,12 @@
         return back, jnp.split(hop, 2, axis=1)
 
     early = shared(second[0])
-    above[1], *_ = tied(above[1], near_first, *early)
+    above[1], *_ = tied(above[1], *early)
     across.append(xor_permute(above[1], "seq", side))
     second.append(tied(jnp.concatenate([above[1], across[1]], axis=0))[0])
     late = shared(second[1])
     sums = [second_sums(*early, across[1]), second_sums(*late)]
+    near_first = product(tied(first, early[0])[0], near)
     near_sums = first_sums(near_first, across[1])
     far_first, _ = tied(product(first, far_all), late[0])
     far_sums = first_sums(far_first)

time: 298 us -> 327 us (1.097)
  waiting for transfers between devices: 163 us -> 185 us
  matrix products: 18.6 us -> 24.3 us
  local copies, waits for them, and re-layouts: 29.1 us -> 33.6 us
  starting transfers between devices: 45.5 us -> 42 us
    ppermute x21, waiting for transfers between devices: 151 us -> 173 us  [xor_permute(): lax.ppermute(value, axis, [(source, source ^ mask) for source in range(co...]
    dot_general x6, matrix products: 18.6 us -> 24.3 us  [product(): return jnp.dot(rows, weight, preferred_element_type=F32).astype(BF16)]
    unnamed x32 -> x36, local copies, waits for them, and re-layouts: 16 us -> 19.7 us
  transfers between devices with their start and end apart: 28 -> 28, of which waited for: 16 -> 15; matrix products, arithmetic and copies ran while one was open for 16% -> 18% of each run, Pallas kernels for 8% -> 7%
where the time goes in v8:
time: 327 us; the launch traced here: 326 us
  waiting for transfers between devices  185 us (57%)
  starting transfers between devices  42 us (13%)
  local copies, waits for them, and re-layouts  33.6 us (10%)
  Pallas kernels  31 us (9%)
  matrix products  24.3 us (7%)
  other arithmetic  9.58 us (3%)
    ppermute x21, waiting for transfers between devices, xor_permute(): lax.ppermute(value, axis, [(source, source ^ mask) for source in range(co...  173 us
    ppermute x21, starting transfers between devices, xor_permute(): lax.ppermute(value, axis, [(source, source ^ mask) for source in range(co...  24.5 us
    dot_general x6, matrix products, product(): return jnp.dot(rows, weight, preferred_element_type=F32).astype(BF16)  24.3 us
    unnamed x36, local copies, waits for them, and re-layouts  19.7 us
    ppermute x6, starting transfers between devices, placed_permute(): return lax.ppermute(value, ('seq', 'chan'), pairs)  15.6 us
    pallas_call x1, Pallas kernels, gated_rows(): pl.pallas_call(gated_kernel, grid=(width // GROUP,), in_specs=[pl.BlockSp...  13.4 us
    ppermute x6, waiting for transfers between devices, placed_permute(): return lax.ppermute(value, ('seq', 'chan'), pairs)  11.2 us
    pallas_call x1, Pallas kernels, mixed_and_states(): pl.pallas_call(states_kernel, grid=(width // GROUP,), in_specs=[stream(1)...  10.8 us
  transfers between devices with their start and end apart: 28, of which 15 were waited for; matrix products, arithmetic and copies ran while one was open for 18% of the time, Pallas kernels for 7%

profile of v8, /device:TPU:0, one launch (start us, length us, event | category | flops | bytes accessed | tf_op | source)
XLA Modules:
  0.0 326.3 jit_solution(2507170508827122284)
XLA Ops:
  5.4 3.1 collective-permute-start.3
  10.6 2.8 copy-done
  13.4 10.8 %mixed_and_states.1 = (bf16[256,4096]{1,0:T(8,128)(2,1)S(1)}, f32[16,32,128]{2,1,0:T(8,128)S(1)}) custom-call(bf16[3,256,4096]{2,1,0:T(8,128)(2,1)S(1)} %bitcast.60, bf16[3,256,4096]{2,1,0:T(8,128)(2,1)S(1)} %bitcast.61, f32[3,8,4096]{2,1,0:T(8,128)S(1)} %pad_convert_fusion.halo_ref, f32[9,4096]{1,0:T(8,128)S(1)} %reshape.13.taps_ref, ...), custom_call_target="tpu_custom_call" | custom-call | flops 1048576 | bytes 256 | tf_op jit(solution)/shard_map/mixed_and_states/pallas_call | solution.py:132
  30.3 7.1 %collective-permute-done.2 = f32[16,32,128]{2,1,0:T(8,128)} collective-permute-done((f32[16,32,128]{2,1,0:T(8,128)S(1)}, f32[16,32,128]{2,1,0:T(8,128)}, u32[]{:S(2)}, u32[]{:S(2)}) %collective-permute-start.2) | collective-permute-done | bytes 262176 | tf_op jit(solution)/shard_map/ppermute | solution.py:20
  39.0 3.9 %slice.121 = bf16[4096,384]{1,0:T(8,128)(2,1)} slice(bf16[4096,512]{1,0:T(8,128)(2,1)} %param.16), slice={[0:4096], [128:512]} | slice | bytes 6291456 | tf_op jit(solution)/shard_map/slice | solution.py:326
  42.8 3.5 %collective-permute-done.4 = f32[16,32,128]{2,1,0:T(8,128)S(1)} collective-permute-done((f32[16,32,128]{2,1,0:T(8,128)S(1)}, f32[16,32,128]{2,1,0:T(8,128)S(1)}, u32[]{:S(2)}, u32[]{:S(2)}) %collective-permute-start.4) | collective-permute-done | bytes 262176 | tf_op jit(solution)/shard_map/ppermute | solution.py:20
  46.4 2.7 collective-permute-start.5
  49.6 10.2 %collective-permute-done.5 = f32[16,32,128]{2,1,0:T(8,128)S(1)} collective-permute-done((f32[16,32,128]{2,1,0:T(8,128)S(1)}, f32[16,32,128]{2,1,0:T(8,128)S(1)}, u32[]{:S(2)}, u32[]{:S(2)}) %collective-permute-start.5) | collective-permute-done | bytes 262176 | tf_op jit(solution)/shard_map/ppermute | solution.py:20
  61.1 2.8 copy-done.1
  65.5 13.4 %gated_rows.1 = bf16[256,4096]{1,0:T(8,128)(2,1)S(1)} custom-call(bf16[3,256,4096]{2,1,0:T(8,128)(2,1)S(1)} %bitcast.62, f32[3,8,4096]{2,1,0:T(8,128)S(1)} %pad_convert_fusion.halo_ref, f32[9,4096]{1,0:T(8,128)S(1)} %reshape.13.taps_ref, bf16[256,4096]{1,0:T(8,128)(2,1)S(1)} %copy-done.5, f32[1,4096]{1,0:T(1,128)S(1)} %bitcast.66, ...), custom_call_target="tpu_custom_call" | custom-call | flops 1048576 | bytes 256 | tf_op jit(solution)/shard_map/gated_rows/pallas_call | solution.py:162
  81.6 61.8 %collective-permute-done.8 = bf16[128,4096]{1,0:T(8,128)(2,1)} collective-permute-done((bf16[128,4096]{1,0:T(8,128)(2,1)S(1)}, bf16[128,4096]{1,0:T(8,128)(2,1)}, u32[]{:S(2)}, u32[]{:S(2)}) %collective-permute-start.8) | collective-permute-done | bytes 1048608 | tf_op jit(solution)/shard_map/ppermute | solution.py:20
  143.6 2.9 constant_dynamic-update-slice_fusion.5
  146.6 19.9 %collective-permute-done.9 = bf16[128,4096]{1,0:T(8,128)(2,1)} collective-permute-done((bf16[128,4096]{1,0:T(8,128)(2,1)}, bf16[128,4096]{1,0:T(8,128)(2,1)}, u32[]{:S(2)}, u32[]{:S(2)}) %collective-permute-start.9) | collective-permute-done | bytes 1048608 | tf_op jit(solution)/shard_map/ppermute | solution.py:20
  166.5 3.5 %collective-permute-start.14 = (bf16[128,4096]{1,0:T(8,128)(2,1)S(1)}, bf16[128,4096]{1,0:T(8,128)(2,1)S(1)}, u32[]{:S(2)}, u32[]{:S(2)}) collective-permute-start(bf16[128,4096]{1,0:T(8,128)(2,1)S(1)} %copy-done.11), channel_id=1, source_target_pairs={{0,16},{2,18},{4,20},{6,22},{8,24},{10,26},{12,28},{14,30},{16,0},... | collective-permute-start | bytes 3145736 | tf_op jit(solution)/shard_map/ppermute | solution.py:20
  170.1 3.1 constant_dynamic-update-slice_fusion.4
  178.6 4.0 %constant_dynamic-update-slice_fusion.2 = bf16[4096,1024]{1,0:T(8,128)(2,1)} fusion(bf16[4096,1024]{1,0:T(8,128)(2,1)} %constant_dynamic-update-slice_fusion.3, bf16[4096,384]{1,0:T(8,128)(2,1)} %collective-permute-done.10), kind=kLoop, calls=%fused_computation.49 | loop fusion | bytes 6291456
  185.9 5.7 %convolution_convert_fusion.5 = bf16[256,1024]{1,0:T(8,128)(2,1)S(1)} fusion(bf16[256,4096]{1,0:T(8,128)(2,1)S(1)} %pad_maximum_fusion.1, bf16[4096,1024]{1,0:T(8,128)(2,1)} %constant_dynamic-update-slice_fusion), kind=kOutput, calls=%fused_computation.10 | convolution fusion | flops 2147745792 | bytes 11010048 | tf_op jit(solution)/shard_map/dot_general | solution.py:330
  195.5 7.0 %convolution_convert_fusion = bf16[512,1024]{1,0:T(8,128)(2,1)S(1)} fusion(bf16[512,4096]{1,0:T(8,128)(2,1)S(1)} %pad_maximum_fusion, bf16[4096,1024]{1,0:T(8,128)(2,1)} %constant_dynamic-update-slice_fusion), kind=kOutput, calls=%fused_computation.5 | convolution fusion | flops 4295491584 | bytes 13631488 | tf_op jit(solution)/shard_map/dot_general | solution.py:330
  202.5 13.7 %collective-permute-done.14 = bf16[128,4096]{1,0:T(8,128)(2,1)S(1)} collective-permute-done((bf16[128,4096]{1,0:T(8,128)(2,1)S(1)}, bf16[128,4096]{1,0:T(8,128)(2,1)S(1)}, u32[]{:S(2)}, u32[]{:S(2)}) %collective-permute-start.14) | collective-permute-done | bytes 1048608 | tf_op jit(solution)/shard_map/ppermute | solution.py:20
  216.6 4.5 %convolution_convert_fusion.1 = bf16[512,1024]{1,0:T(8,128)(2,1)S(1)} fusion(bf16[512,4096]{1,0:T(8,128)(2,1)S(1)} %pad_maximum_fusion, bf16[4096,1024]{1,0:T(8,128)(2,1)S(1)} %constant_dynamic-update-slice_fusion.4), kind=kOutput, calls=%fused_computation.6 | convolution fusion | flops 4295491584 | bytes 13631488 | tf_op jit(solution)/shard_map/dot_general | solution.py:330
  222.4 19.0 %collective-permute-done.15 = bf16[128,4096]{1,0:T(8,128)(2,1)S(1)} collective-permute-done((bf16[128,4096]{1,0:T(8,128)(2,1)S(1)}, bf16[128,4096]{1,0:T(8,128)(2,1)S(1)}, u32[]{:S(2)}, u32[]{:S(2)}) %collective-permute-start.15) | collective-permute-done | bytes 1048608 | tf_op jit(solution)/shard_map/ppermute | solution.py:20
  253.6 3.7 %collective-permute-start.20 = (bf16[256,1024]{1,0:T(8,128)(2,1)S(1)}, bf16[256,1024]{1,0:T(8,128)(2,1)S(1)}, u32[]{:S(2)}, u32[]{:S(2)}) collective-permute-start(bf16[256,1024]{1,0:T(8,128)(2,1)S(1)} %slice.164), channel_id=1, source_target_pairs={{0,4},{2,6},{4,0},{6,2},{8,12},{10,14},{12,8},{14,10},{17,21},{19,... | collective-permute-start | bytes 1572872 | tf_op jit(solution)/shard_map/ppermute | solution.py:344
  258.5 6.6 %collective-permute-done.21 = bf16[128,1024]{1,0:T(8,128)(2,1)S(1)} collective-permute-done((bf16[128,1024]{1,0:T(8,128)(2,1)S(1)}, bf16[128,1024]{1,0:T(8,128)(2,1)S(1)}, u32[]{:S(2)}, u32[]{:S(2)}) %collective-permute-start.21) | collective-permute-done | bytes 262176 | tf_op jit(solution)/shard_map/ppermute | solution.py:20
  265.2 3.3 %collective-permute-start.24 = (bf16[128,2048]{1,0:T(8,128)(2,1)S(1)}, bf16[128,2048]{1,0:T(8,128)(2,1)S(1)}, u32[]{:S(2)}, u32[]{:S(2)}) collective-permute-start(bf16[128,2048]{1,0:T(8,128)(2,1)S(1)} %pad_maximum_fusion.3), channel_id=1, source_target_pairs={{0,1},{2,3},{4,5},{6,7},{8,9},{10,11},{12,13},{14,15},{17,16},{19,... | collective-permute-start | bytes 1572872 | tf_op jit(solution)/shard_map/ppermute | solution.py:344
  269.0 2.8 collective-permute-start.22
  271.8 15.3 %collective-permute-done.19 = bf16[128,1024]{1,0:T(8,128)(2,1)S(1)} collective-permute-done((bf16[128,1024]{1,0:T(8,128)(2,1)S(1)}, bf16[128,1024]{1,0:T(8,128)(2,1)S(1)}, u32[]{:S(2)}, u32[]{:S(2)}) %collective-permute-start.19) | collective-permute-done | bytes 262176 | tf_op jit(solution)/shard_map/ppermute | solution.py:20
  287.2 6.7 %collective-permute-done.22 = bf16[128,1024]{1,0:T(8,128)(2,1)S(1)} collective-permute-done((bf16[128,1024]{1,0:T(8,128)(2,1)S(1)}, bf16[128,1024]{1,0:T(8,128)(2,1)S(1)}, u32[]{:S(2)}, u32[]{:S(2)}) %collective-permute-start.22) | collective-permute-done | bytes 262176 | tf_op jit(solution)/shard_map/ppermute | solution.py:20
  296.5 4.3 %collective-permute-start.26 = (bf16[256,1024]{1,0:T(8,128)(2,1)S(1)}, bf16[256,1024]{1,0:T(8,128)(2,1)S(1)}, u32[]{:S(2)}, u32[]{:S(2)}) collective-permute-start(bf16[256,1024]{1,0:T(8,128)(2,1)S(1)} %slice.179), channel_id=1, source_target_pairs={{0,4},{2,6},{4,0},{6,2},{8,12},{10,14},{12,8},{14,10},{17,21},{19,... | collective-permute-start | bytes 1572872 | tf_op jit(solution)/shard_map/ppermute | solution.py:344
  300.9 6.0 %collective-permute-done.25 = bf16[128,2048]{1,0:T(8,128)(2,1)S(1)} collective-permute-done((bf16[128,2048]{1,0:T(8,128)(2,1)S(1)}, bf16[128,2048]{1,0:T(8,128)(2,1)S(1)}, u32[]{:S(2)}, u32[]{:S(2)}) %collective-permute-start.25) | collective-permute-done | bytes 524320 | tf_op jit(solution)/shard_map/ppermute | solution.py:344
  307.1 5.2 %collective-permute-done.26 = bf16[256,1024]{1,0:T(8,128)(2,1)S(1)} collective-permute-done((bf16[256,1024]{1,0:T(8,128)(2,1)S(1)}, bf16[256,1024]{1,0:T(8,128)(2,1)S(1)}, u32[]{:S(2)}, u32[]{:S(2)}) %collective-permute-start.26) | collective-permute-done | bytes 524320 | tf_op jit(solution)/shard_map/ppermute | solution.py:344
  312.5 5.9 %output_rows.1 = (bf16[256,4096]{1,0:T(8,128)(2,1)}, bf16[528,256]{1,0:T(8,128)(2,1)S(1)}) custom-call(s32[8]{0:T(128)S(1)} %iota_xor_fusion.order_ref, bf16[8,256,512]{2,1,0:T(8,128)(2,1)S(1)} %fusion.1.added_ref, bf16[256,4096]{1,0:T(8,128)(2,1)S(1)} %copy-done.3, f32[1,4096]{1,0:T(1,128)S(1)} %bitcast.67, bf16[512,4096]{1,0:T(8,128)(2,1)S(1)} %copy-done.2), custom_call_target="tpu_custom_call" | custom-call | flops 1073741824 | bytes 10485760 | tf_op jit(solution)/shard_map/output_rows/pallas_call | solution.py:253
  318.4 7.1 %collective-permute-done.27.second_ref = bf16[528,256]{1,0:T(8,128)(2,1)S(1)} collective-permute-done((bf16[528,256]{1,0:T(8,128)(2,1)S(1)}, bf16[528,256]{1,0:T(8,128)(2,1)S(1)}, u32[]{:S(2)}, u32[]{:S(2)}) %collective-permute-start.27) | collective-permute-done | bytes 270368 | tf_op jit(solution)/shard_map/ppermute | solution.py:20
  (111 shorter events, 52.8 us)
Async XLA Ops:
  0.6 60.4 %collective-permute-start.6 = (bf16[4096,512]{1,0:T(8,128)(2,1)}, bf16[4096,512]{1,0:T(8,128)(2,1)}, u32[]{:S(2)}, u32[]{:S(2)}) collective-permute-start(bf16[4096,512]{1,0:T(8,128)(2,1)} %param.16), channel_id=1, source_target_pairs={{0,2},{2,0},{4,6},{6,4},{8,10},{10,8},{12,14},{14,12},{16,18},{18,... | collective-permute-start | bytes 12582920 | tf_op jit(solution)/shard_map/ppermute | solution.py:20
  2.1 8.4 %collective-permute-start = (bf16[2,3,4096]{2,0,1:T(2,128)(2,1)S(1)}, bf16[2,3,4096]{2,0,1:T(2,128)(2,1)S(1)}, u32[]{:S(2)}, u32[]{:S(2)}) collective-permute-start(bf16[2,3,4096]{2,0,1:T(2,128)(2,1)S(1)} %slice.119), channel_id=1, source_target_pairs={{0,2},{2,4},{4,6},{6,8},{8,10},{10,12},{12,14},{14,16},{16,18},{18... | collective-permute-start | bytes 147464 | tf_op jit(solution)/shard_map/ppermute | solution.py:26
  5.4 33.0 %collective-permute-start.3 = (bf16[4096,128]{1,0:T(8,128)(2,1)S(1)}, bf16[4096,128]{1,0:T(8,128)(2,1)S(1)}, u32[]{:S(2)}, u32[]{:S(2)}) collective-permute-start(bf16[4096,128]{1,0:T(8,128)(2,1)S(1)} %slice.120), channel_id=1, source_target_pairs={{0,8},{2,10},{4,12},{6,14},{8,0},{10,2},{12,4},{14,6},{16,24},{18,... | collective-permute-start | bytes 3145736 | tf_op jit(solution)/shard_map/ppermute | solution.py:20
  25.5 2.1 collective-permute-start.1
  28.6 8.8 %collective-permute-start.2 = (f32[16,32,128]{2,1,0:T(8,128)S(1)}, f32[16,32,128]{2,1,0:T(8,128)}, u32[]{:S(2)}, u32[]{:S(2)}) collective-permute-start(f32[16,32,128]{2,1,0:T(8,128)S(1)} %multiply_add_fusion.2), channel_id=1, source_target_pairs={{0,4},{2,6},{4,0},{6,2},{8,12},{10,14},{12,8},{14,10},{16,20},{18,... | collective-permute-start | bytes 786440 | tf_op jit(solution)/shard_map/ppermute | solution.py:20
  38.5 7.8 %collective-permute-start.4 = (f32[16,32,128]{2,1,0:T(8,128)S(1)}, f32[16,32,128]{2,1,0:T(8,128)S(1)}, u32[]{:S(2)}, u32[]{:S(2)}) collective-permute-start(f32[16,32,128]{2,1,0:T(8,128)S(1)} %multiply_add_fusion.1), channel_id=1, source_target_pairs={{0,8},{2,10},{4,12},{6,14},{8,0},{10,2},{12,4},{14,6},{16,24},{18,... | collective-permute-start | bytes 786440 | tf_op jit(solution)/shard_map/ppermute | solution.py:20
  42.8 18.2 %copy-start.6 = (f32[4096]{0:T(1024)S(1)}, f32[4096]{0:T(1024)}, u32[]{:S(2)}) copy-start(f32[4096]{0:T(1024)} %param.15) | copy-start | bytes 49156
  46.4 13.4 %collective-permute-start.5 = (f32[16,32,128]{2,1,0:T(8,128)S(1)}, f32[16,32,128]{2,1,0:T(8,128)S(1)}, u32[]{:S(2)}, u32[]{:S(2)}) collective-permute-start(f32[16,32,128]{2,1,0:T(8,128)S(1)} %multiply_add_fusion), channel_id=1, source_target_pairs={{0,16},{2,18},{4,20},{6,22},{8,24},{10,26},{12,28},{14,30},{16,0},... | collective-permute-start | bytes 786440 | tf_op jit(solution)/shard_map/ppermute | solution.py:20
  49.1 97.5 %collective-permute-start.10 = (bf16[4096,384]{1,0:T(8,128)(2,1)}, bf16[4096,384]{1,0:T(8,128)(2,1)}, u32[]{:S(2)}, u32[]{:S(2)}) collective-permute-start(bf16[4096,384]{1,0:T(8,128)(2,1)} %slice.121), channel_id=1, source_target_pairs={{0,8},{2,10},{4,12},{6,14},{8,0},{10,2},{12,4},{14,6},{16,24},{18,... | collective-permute-start | bytes 9437192 | tf_op jit(solution)/shard_map/ppermute | solution.py:20
  80.0 63.3 %collective-permute-start.8 = (bf16[128,4096]{1,0:T(8,128)(2,1)S(1)}, bf16[128,4096]{1,0:T(8,128)(2,1)}, u32[]{:S(2)}, u32[]{:S(2)}) collective-permute-start(bf16[128,4096]{1,0:T(8,128)(2,1)S(1)} %get-tuple-element.39), channel_id=1, source_target_pairs={{0,16},{2,18},{4,20},{6,22},{8,24},{10,26},{12,28},{14,30},{16,0},... | collective-permute-start | bytes 3145736 | tf_op jit(solution)/shard_map/ppermute | solution.py:20
  80.1 93.2 %collective-permute-start.7 = (bf16[256,4096]{1,0:T(8,128)(2,1)S(1)}, bf16[256,4096]{1,0:T(8,128)(2,1)}, u32[]{:S(2)}, u32[]{:S(2)}) collective-permute-start(bf16[256,4096]{1,0:T(8,128)(2,1)S(1)} %gated_rows.1), channel_id=1, source_target_pairs={{0,4},{2,6},{4,0},{6,2},{8,12},{10,14},{12,8},{14,10},{16,20},{18,... | collective-permute-start | bytes 6291464 | tf_op jit(solution)/shard_map/ppermute | solution.py:20
  143.4 23.1 %collective-permute-start.9 = (bf16[128,4096]{1,0:T(8,128)(2,1)}, bf16[128,4096]{1,0:T(8,128)(2,1)}, u32[]{:S(2)}, u32[]{:S(2)}) collective-permute-start(bf16[128,4096]{1,0:T(8,128)(2,1)} %collective-permute-done.8), channel_id=1, source_target_pairs={{0,4},{2,6},{4,0},{6,2},{8,12},{10,14},{12,8},{14,10},{16,20},{18,... | collective-permute-start | bytes 3145736 | tf_op jit(solution)/shard_map/ppermute | solution.py:20
  143.6 22.9 %copy-start.11 = (bf16[128,4096]{1,0:T(8,128)(2,1)S(1)}, bf16[128,4096]{1,0:T(8,128)(2,1)}, u32[]{:S(2)}) copy-start(bf16[128,4096]{1,0:T(8,128)(2,1)} %get-tuple-element.38) | copy-start | bytes 3145732
  166.5 17.2 %collective-permute-start.12 = (bf16[4096,384]{1,0:T(8,128)(2,1)}, bf16[4096,384]{1,0:T(8,128)(2,1)S(1)}, u32[]{:S(2)}, u32[]{:S(2)}) collective-permute-start(bf16[4096,384]{1,0:T(8,128)(2,1)} %collective-permute-done.10), channel_id=1, source_target_pairs={{0,2},{2,0},{4,6},{6,4},{8,10},{10,8},{12,14},{14,12},{16,18},{18,... | collective-permute-start | bytes 9437192 | tf_op jit(solution)/shard_map/ppermute | solution.py:20
  166.5 49.7 %collective-permute-start.14 = (bf16[128,4096]{1,0:T(8,128)(2,1)S(1)}, bf16[128,4096]{1,0:T(8,128)(2,1)S(1)}, u32[]{:S(2)}, u32[]{:S(2)}) collective-permute-start(bf16[128,4096]{1,0:T(8,128)(2,1)S(1)} %copy-done.11), channel_id=1, source_target_pairs={{0,16},{2,18},{4,20},{6,22},{8,24},{10,26},{12,28},{14,30},{16,0},... | collective-permute-start | bytes 3145736 | tf_op jit(solution)/shard_map/ppermute | solution.py:20
  175.4 7.2 %collective-permute-start.11 = (bf16[4096,128]{1,0:T(8,128)(2,1)S(1)}, bf16[4096,128]{1,0:T(8,128)(2,1)S(1)}, u32[]{:S(2)}, u32[]{:S(2)}) collective-permute-start(bf16[4096,128]{1,0:T(8,128)(2,1)S(1)} %copy-done.10), channel_id=1, source_target_pairs={{0,2},{2,0},{4,6},{6,4},{8,10},{10,8},{12,14},{14,12},{16,18},{18,... | collective-permute-start | bytes 3145736 | tf_op jit(solution)/shard_map/ppermute | solution.py:20
  193.9 28.5 %collective-permute-start.16 = (bf16[256,1024]{1,0:T(8,128)(2,1)S(1)}, bf16[256,1024]{1,0:T(8,128)(2,1)S(1)}, u32[]{:S(2)}, u32[]{:S(2)}) collective-permute-start(bf16[256,1024]{1,0:T(8,128)(2,1)S(1)} %get-tuple-element.41), channel_id=1, source_target_pairs={{0,1},{1,0},{2,3},{3,2},{4,5},{5,4},{6,7},{7,6},{8,9},{9,8},{10,11... | collective-permute-start | bytes 1572872 | tf_op jit(solution)/shard_map/ppermute | solution.py:20
  216.2 25.2 %collective-permute-start.15 = (bf16[128,4096]{1,0:T(8,128)(2,1)S(1)}, bf16[128,4096]{1,0:T(8,128)(2,1)S(1)}, u32[]{:S(2)}, u32[]{:S(2)}) collective-permute-start(bf16[128,4096]{1,0:T(8,128)(2,1)S(1)} %collective-permute-done.14), channel_id=1, source_target_pairs={{0,4},{2,6},{4,0},{6,2},{8,12},{10,14},{12,8},{14,10},{16,20},{18,... | collective-permute-start | bytes 3145736 | tf_op jit(solution)/shard_map/ppermute | solution.py:20
  221.1 32.1 %collective-permute-start.13 = (bf16[512,1024]{1,0:T(8,128)(2,1)S(1)}, bf16[512,1024]{1,0:T(8,128)(2,1)S(1)}, u32[]{:S(2)}, u32[]{:S(2)}) collective-permute-start(bf16[512,1024]{1,0:T(8,128)(2,1)S(1)} %convolution_convert_fusion.1), channel_id=1, source_target_pairs={{1,0},{3,2},{5,4},{7,6},{9,8},{11,10},{13,12},{15,14},{16,17},{18,... | collective-permute-start | bytes 3145736 | tf_op jit(solution)/shard_map/ppermute | solution.py:344
  241.6 16.9 %collective-permute-start.17 = (bf16[128,1024]{1,0:T(8,128)(2,1)S(1)}, bf16[128,1024]{1,0:T(8,128)(2,1)S(1)}, u32[]{:S(2)}, u32[]{:S(2)}) collective-permute-start(bf16[128,1024]{1,0:T(8,128)(2,1)S(1)} %get-tuple-element.51), channel_id=1, source_target_pairs={{0,16},{2,18},{4,20},{6,22},{8,24},{10,26},{12,28},{14,30},{16,0},... | collective-permute-start | bytes 786440 | tf_op jit(solution)/shard_map/ppermute | solution.py:20
  241.7 23.4 %collective-permute-start.21 = (bf16[128,1024]{1,0:T(8,128)(2,1)S(1)}, bf16[128,1024]{1,0:T(8,128)(2,1)S(1)}, u32[]{:S(2)}, u32[]{:S(2)}) collective-permute-start(bf16[128,1024]{1,0:T(8,128)(2,1)S(1)} %get-tuple-element.50), channel_id=1, source_target_pairs={{0,20},{2,22},{4,16},{6,18},{8,28},{10,30},{12,24},{14,26},{16,4},... | collective-permute-start | bytes 786440 | tf_op jit(solution)/shard_map/ppermute | solution.py:20
  250.3 18.3 %collective-permute-start.18 = (bf16[256,1024]{1,0:T(8,128)(2,1)S(1)}, bf16[256,1024]{1,0:T(8,128)(2,1)S(1)}, u32[]{:S(2)}, u32[]{:S(2)}) collective-permute-start(bf16[256,1024]{1,0:T(8,128)(2,1)S(1)} %get-tuple-element.62), channel_id=1, source_target_pairs={{0,1},{1,0},{2,3},{3,2},{4,5},{5,4},{6,7},{7,6},{8,9},{9,8},{10,11... | collective-permute-start | bytes 1572872 | tf_op jit(solution)/shard_map/ppermute | solution.py:20
  251.9 44.2 %collective-permute-start.23 = (bf16[512,1024]{1,0:T(8,128)(2,1)S(1)}, bf16[512,1024]{1,0:T(8,128)(2,1)S(1)}, u32[]{:S(2)}, u32[]{:S(2)}) collective-permute-start(bf16[512,1024]{1,0:T(8,128)(2,1)S(1)} %convolution_convert_fusion), channel_id=1, source_target_pairs={{1,0},{3,2},{5,4},{7,6},{9,8},{11,10},{13,12},{15,14},{16,17},{18,... | collective-permute-start | bytes 3145736 | tf_op jit(solution)/shard_map/ppermute | solution.py:344
  253.6 42.2 %collective-permute-start.20 = (bf16[256,1024]{1,0:T(8,128)(2,1)S(1)}, bf16[256,1024]{1,0:T(8,128)(2,1)S(1)}, u32[]{:S(2)}, u32[]{:S(2)}) collective-permute-start(bf16[256,1024]{1,0:T(8,128)(2,1)S(1)} %slice.164), channel_id=1, source_target_pairs={{0,4},{2,6},{4,0},{6,2},{8,12},{10,14},{12,8},{14,10},{17,21},{19,... | collective-permute-start | bytes 1572872 | tf_op jit(solution)/shard_map/ppermute | solution.py:344
  265.2 30.7 %collective-permute-start.24 = (bf16[128,2048]{1,0:T(8,128)(2,1)S(1)}, bf16[128,2048]{1,0:T(8,128)(2,1)S(1)}, u32[]{:S(2)}, u32[]{:S(2)}) collective-permute-start(bf16[128,2048]{1,0:T(8,128)(2,1)S(1)} %pad_maximum_fusion.3), channel_id=1, source_target_pairs={{0,1},{2,3},{4,5},{6,7},{8,9},{10,11},{12,13},{14,15},{17,16},{19,... | collective-permute-start | bytes 1572872 | tf_op jit(solution)/shard_map/ppermute | solution.py:344
  268.9 18.3 %collective-permute-start.19 = (bf16[128,1024]{1,0:T(8,128)(2,1)S(1)}, bf16[128,1024]{1,0:T(8,128)(2,1)S(1)}, u32[]{:S(2)}, u32[]{:S(2)}) collective-permute-start(bf16[128,1024]{1,0:T(8,128)(2,1)S(1)} %get-tuple-element.53), channel_id=1, source_target_pairs={{0,16},{2,18},{4,20},{6,22},{8,24},{10,26},{12,28},{14,30},{16,0},... | collective-permute-start | bytes 786440 | tf_op jit(solution)/shard_map/ppermute | solution.py:20
  269.0 24.9 %collective-permute-start.22 = (bf16[128,1024]{1,0:T(8,128)(2,1)S(1)}, bf16[128,1024]{1,0:T(8,128)(2,1)S(1)}, u32[]{:S(2)}, u32[]{:S(2)}) collective-permute-start(bf16[128,1024]{1,0:T(8,128)(2,1)S(1)} %get-tuple-element.52), channel_id=1, source_target_pairs={{0,20},{2,22},{4,16},{6,18},{8,28},{10,30},{12,24},{14,26},{16,4},... | collective-permute-start | bytes 786440 | tf_op jit(solution)/shard_map/ppermute | solution.py:20
  293.9 13.0 %collective-permute-start.25 = (bf16[128,2048]{1,0:T(8,128)(2,1)S(1)}, bf16[128,2048]{1,0:T(8,128)(2,1)S(1)}, u32[]{:S(2)}, u32[]{:S(2)}) collective-permute-start(bf16[128,2048]{1,0:T(8,128)(2,1)S(1)} %pad_maximum_fusion.4), channel_id=1, source_target_pairs={{0,1},{2,3},{4,5},{6,7},{8,9},{10,11},{12,13},{14,15},{17,16},{19,... | collective-permute-start | bytes 1572872 | tf_op jit(solution)/shard_map/ppermute | solution.py:344
  296.1 16.4 %copy-start.3 = (bf16[256,4096]{1,0:T(8,128)(2,1)S(1)}, bf16[256,4096]{1,0:T(8,128)(2,1)}, u32[]{:S(2)}) copy-start(bf16[256,4096]{1,0:T(8,128)(2,1)} %residual_ref.1) | copy-start | bytes 6291460
  296.5 16.0 %copy-start.2 = (bf16[512,4096]{1,0:T(8,128)(2,1)S(1)}, bf16[512,4096]{1,0:T(8,128)(2,1)}, u32[]{:S(2)}) copy-start(bf16[512,4096]{1,0:T(8,128)(2,1)} %table_ref.1) | copy-start | bytes 12582916
  296.5 15.7 %collective-permute-start.26 = (bf16[256,1024]{1,0:T(8,128)(2,1)S(1)}, bf16[256,1024]{1,0:T(8,128)(2,1)S(1)}, u32[]{:S(2)}, u32[]{:S(2)}) collective-permute-start(bf16[256,1024]{1,0:T(8,128)(2,1)S(1)} %slice.179), channel_id=1, source_target_pairs={{0,4},{2,6},{4,0},{6,2},{8,12},{10,14},{12,8},{14,10},{17,21},{19,... | collective-permute-start | bytes 1572872 | tf_op jit(solution)/shard_map/ppermute | solution.py:344
  318.4 7.1 %collective-permute-start.27 = (bf16[528,256]{1,0:T(8,128)(2,1)S(1)}, bf16[528,256]{1,0:T(8,128)(2,1)S(1)}, u32[]{:S(2)}, u32[]{:S(2)}) collective-permute-start(bf16[528,256]{1,0:T(8,128)(2,1)S(1)} %get-tuple-element.37.first_ref), channel_id=1, source_target_pairs={{0,1},{1,0},{2,3},{3,2},{4,5},{5,4},{6,7},{7,6},{8,9},{9,8},{10,11... | collective-permute-start | bytes 811016 | tf_op jit(solution)/shard_map/ppermute | solution.py:20
  (11 other events, 60.6 us)
